TPU v7x, 128 devices: a whole 4x4x4 slice. The times are simulated.
128 devices in a mesh: row: 16 (over x, y), col: 8 (over z, core).
Axes of the slice: x: 4, y: 4, z: 4, core: 2. Of those that a mesh axis runs over, the one named last changes fastest.
Arguments:
- density: bfloat16 [64, 64, 128, 128], P('row', 'col'), as said below
- basis: bfloat16 [384, 4, 256, 1024], P(('row', 'col')), may hold values from -6 to 6
- weights: float32 [384, 256], P(('row', 'col')), may hold values from 0.01 to 0.1
- batch_start: int32 [384], replicated, may hold values from 0 to 56
- batch_count: int32 [128], replicated, may hold values from 1 to 3, as said below
Outputs:
- potential: float32 [64, 64, 128, 128], P('row', 'col')
- energy: float32 [], replicated
Inputs may be any that keep to these rules, and one draw needn't show every extreme that they name: Device d holds batch slots d * 3 to d * 3 + 2 and works on the first batch_count[d] of them; some device has 3. Batch k's significant shell blocks are the 8 consecutive blocks starting at batch_start[k]; the basis arrays list their functions in that order. density is symmetric: block (i, j) is the transpose of block (j, i).
All inputs are finite; a program needn't handle non-finite values.
Results may differ from a plain program's by a relative error of at most 0.0021.
Values may be sent and summed in bfloat16 or wider, within the bound.
No kernel may reach another device: no remote copies, remote signals or barrier semaphores. Data moves between devices by JAX's collectives and lax.ppermute only.
A program may use at most 128 MiB of HBM per device.

v0:
```python
import jax
import jax.numpy as jnp
from jax import lax
from jax.sharding import PartitionSpec as P

CX_CONST = 0.7385587663820224
MU_CONST = 0.2195149727645171
KAPPA_CONST = 0.804


def exchange_energy(density_value, gradient_square):
    square = density_value * density_value + 1.0
    scaled = square ** (2.0 / 3.0)
    reduced = gradient_square / square ** (4.0 / 3.0)
    factor = 1.0 + MU_CONST * reduced / (1.0 + MU_CONST * reduced / KAPPA_CONST)
    return -CX_CONST * scaled * factor


def batch_terms(phi_all, quad_weight, sub_matrix):
    values = phi_all[0]
    product = jnp.dot(values, sub_matrix, preferred_element_type=jnp.float32)
    density_value = jnp.sum(values * product, axis=1)
    gradient = 2.0 * jnp.sum(phi_all[1:4] * product[None], axis=2)
    gradient_square = jnp.sum(gradient * gradient, axis=0)
    energy_point, pullback = jax.vjp(exchange_energy, density_value, gradient_square)
    weighted_rho, weighted_sigma = pullback(quad_weight)
    along = jnp.sum(gradient[:, :, None] * phi_all[1:4], axis=0)
    kernel = (0.5 * weighted_rho[:, None] * values + 2.0 * weighted_sigma[:, None] * along).astype(
        jnp.bfloat16
    )
    half = jnp.dot(values.T, kernel, preferred_element_type=jnp.float32)
    return (half + half.T, jnp.sum(quad_weight * energy_point))


def owner_index(
    starts, row_id, col_id, row_count, col_count, row_turns, col_turns, span, local_rows, local_cols
):
    row_pos = jnp.mod(row_id - starts, row_count)[:, :, None] + jnp.arange(row_turns) * row_count
    col_pos = jnp.mod(col_id - starts, col_count)[:, :, None] + jnp.arange(col_turns) * col_count
    rows_local = jnp.minimum((starts[:, :, None] + row_pos) // row_count, local_rows - 1)
    cols_local = jnp.minimum((starts[:, :, None] + col_pos) // col_count, local_cols - 1)
    usable = (row_pos < span)[:, :, :, None] & (col_pos < span)[:, :, None, :]
    return (rows_local, cols_local, usable)


def move_blocks(outgoing):
    arrived = lax.all_to_all(outgoing, ("row", "col"), split_axis=0, concat_axis=0, tiled=True)
    return arrived


def move_partials(outgoing):
    arrived = lax.all_to_all(outgoing, ("row", "col"), split_axis=0, concat_axis=0, tiled=True)
    return arrived


def shards(density, basis, weights, batch_start, batch_count):
    row_count = lax.axis_size("row")
    col_count = lax.axis_size("col")
    devices = row_count * col_count
    row_id = lax.axis_index("row")
    col_id = lax.axis_index("col")
    slots = basis.shape[0]
    block = density.shape[2]
    nblocks = density.shape[0] * row_count
    span = basis.shape[3] // block
    width = span * block
    row_turns = (span + row_count - 1) // row_count
    col_turns = (span + col_count - 1) // col_count
    starts = batch_start.reshape(devices, slots)
    live = jnp.arange(slots)[None, :] < batch_count[:, None]
    rows_local, cols_local, usable = owner_index(
        starts,
        row_id,
        col_id,
        row_count,
        col_count,
        row_turns,
        col_turns,
        span,
        density.shape[0],
        density.shape[1],
    )
    usable = usable & live[:, :, None, None]
    picked = density[rows_local[:, :, :, None], cols_local[:, :, None, :]]
    outgoing = jnp.where(usable[..., None, None], picked, jnp.zeros((), density.dtype))
    incoming = move_blocks(outgoing)
    incoming = incoming.reshape(row_count, col_count, slots, row_turns, col_turns, block, block)
    self_index = row_id * col_count + col_id
    own_starts = starts[self_index]
    own_count = batch_count[self_index]
    offsets = jnp.arange(span)
    energy = jnp.zeros((), jnp.float32)
    returns = []

    def work(operands):
        return batch_terms(operands[0], operands[1], operands[2])

    def skip(operands):
        return (jnp.zeros((width, width), jnp.float32), jnp.zeros((), jnp.float32))

    for slot_index in range(slots):
        anchor = own_starts[slot_index]
        source_rows = jnp.mod(anchor + offsets, row_count)
        source_cols = jnp.mod(anchor + offsets, col_count)
        grid = incoming[
            source_rows[:, None],
            source_cols[None, :],
            slot_index,
            (offsets // row_count)[:, None],
            (offsets // col_count)[None, :],
        ]
        sub_matrix = grid.transpose(0, 2, 1, 3).reshape(width, width)
        result, part_energy = lax.cond(
            slot_index < own_count, work, skip, (basis[slot_index], weights[slot_index], sub_matrix)
        )
        energy = energy + part_energy
        pieces = result.reshape(span, block, span, block).transpose(0, 2, 1, 3)
        row_pos = (
            jnp.mod(jnp.arange(row_count) - anchor, row_count)[:, None]
            + jnp.arange(row_turns) * row_count
        )
        col_pos = (
            jnp.mod(jnp.arange(col_count) - anchor, col_count)[:, None]
            + jnp.arange(col_turns) * col_count
        )
        fits = (row_pos < span)[:, None, :, None] & (col_pos < span)[None, :, None, :]
        taken = pieces[
            jnp.minimum(row_pos, span - 1)[:, None, :, None],
            jnp.minimum(col_pos, span - 1)[None, :, None, :],
        ]
        returns.append(jnp.where(fits[..., None, None], taken, 0.0))
    partial_blocks = jnp.stack(returns, axis=2).reshape(
        devices, slots, row_turns, col_turns, block, block
    )
    arrived = move_partials(partial_blocks)
    contributions = jnp.where(usable[..., None, None], arrived, 0.0)
    potential = (
        jnp.zeros(density.shape, jnp.float32)
        .at[rows_local[:, :, :, None], cols_local[:, :, None, :]]
        .add(contributions)
    )
    total = lax.psum(energy, ("row", "col"))
    return (potential, total / (nblocks * block))


def solution(mesh):
    in_specs = (
        P("row", "col", None, None),
        P(("row", "col"), None, None, None),
        P(("row", "col"), None),
        P(),
        P(),
    )
    out_specs = (P("row", "col", None, None), P())
    return jax.shard_map(shards, mesh=mesh, in_specs=in_specs, out_specs=out_specs, check_vma=False)
```

profile of v0, /device:TPU:18, one launch (start us, length us, event | category | flops | bytes accessed | tf_op | source)
XLA Modules:
  0.0 891.2 jit_solution(9160527982449723045)
XLA Ops:
  0.6 1.0 reshape.1173
  1.6 0.9 broadcast_in_dim_reshape.4
  2.5 0.2 compare_select_fusion.1
  2.9 0.1 copy.41
  3.0 0.2 reshape.1189
  3.2 16.3 %gather_fusion = bf16[384,128,128]{2,1,0:T(8,128)(2,1)} fusion(bf16[4,8,128,128]{3,2,1,0:T(8,128)(2,1)S(1)} %copy-done, s32[384]{0:T(512)S(1)} %reshape.1189), kind=kCustom, calls=%fused_computation | custom fusion | bytes 25168896 | tf_op jit(solution)/shard_map/gather | solution.py:84
  19.6 10.6 %select_bitcast_fusion = bf16[128,3,1,1,128,128]{5,4,3,2,1,0:T(8,128)(2,1)} fusion(bf16[128,3,1,1,128,128]{5,4,1,0,3,2:T(8,128)(2,1)} %bitcast.191, pred[128,3]{1,0:T(8,128)(4,1)S(1)} %fusion.71), kind=kLoop, calls=%fused_computation.121 | loop fusion | flops 6291456 | bytes 25166208 | tf_op jit(solution)/shard_map/jit(_where)/select_n | solution.py:85
  30.3 10.7 %all-to-all-start = ((bf16[128,3,1,1,128,128]{5,4,3,2,1,0:T(8,128)(2,1)}), bf16[128,3,1,1,128,128]{5,4,3,2,1,0:T(8,128)(2,1)}, u32[]{:S(2)}, u32[]{:S(2)}) async-start(bf16[128,3,1,1,128,128]{5,4,3,2,1,0:T(8,128)(2,1)} %select_bitcast_fusion), calls=%async_computation | async-start | bytes 25165824 | tf_op jit(solution)/shard_map/all_to_all | solution.py:47
  41.0 0.6 dynamic_slice.7
  41.6 0.6 fusion.109
  42.2 0.6 fusion.107
  42.9 0.6 compare_select_fusion.10
  43.5 1.2 fusion.99
  44.7 0.6 compare_select_fusion.6
  45.3 0.6 compare_select_fusion.2
  46.8 0.6 compare_select_fusion.3
  47.6 0.6 broadcast_compare_fusion.3
  48.4 0.6 broadcast_compare_fusion
  49.9 0.6 compare_select_fusion.7
  50.7 0.6 broadcast_compare_fusion.4
  51.4 0.1 and.498
  51.5 0.6 broadcast_compare_fusion.1
  52.9 0.6 compare_select_fusion.11
  53.7 0.6 broadcast_compare_fusion.5
  54.5 0.6 broadcast_compare_fusion.2
  55.3 148.9 %all-to-all-done = bf16[128,3,1,1,128,128]{5,4,3,2,1,0:T(8,128)(2,1)} async-done(((bf16[128,3,1,1,128,128]{5,4,3,2,1,0:T(8,128)(2,1)}), bf16[128,3,1,1,128,128]{5,4,3,2,1,0:T(8,128)(2,1)}, u32[]{:S(2)}, u32[]{:S(2)}) %all-to-all-start) | async-done | bytes 12582944 | tf_op jit(solution)/shard_map/all_to_all | solution.py:47
  204.2 5.6 gather_fusion.5
  209.8 2.7 conditional.5
  209.8 2.5 broadcast.1977
  212.5 3.2 copy.56
  215.7 2.7 copy.78
  218.4 5.6 gather_fusion.3
  224.0 2.5 conditional.4
  224.0 2.5 broadcast.1965
  226.5 3.2 copy.55
  229.7 2.7 copy.79
  232.4 5.6 gather_fusion.1
  238.0 21.2 %conditional.3 = (f32[1024,1024]{1,0:T(8,128)}, f32[]{:T(128)}) conditional(s32[]{:T(128)} %bitcast.26, () %tuple.32, (bf16[3,4,256,1024]{3,2,1,0:T(8,128)(2,1)}, bf16[8,128,8,128]{3,1,2,0:T(8,128)(2,1)S(1)}, f32[3,256]{1,0:T(4,128)S(1)}) %tuple.82), branch_computations={%region_0.1_spmd, %region_1.7_spmd} | conditional | flops 1081355520 | bytes 66086960 | solution.py:113
  238.2 1.4 copy.43
  239.6 2.4 multiply_reduce_fusion
  242.0 0.4 fusion
  242.4 0.7 multiply_multiply_fusion
  243.1 0.3 fusion.1
  243.5 2.9 fusion.8
  246.4 5.3 copy.35
  251.7 6.8 bitcast_add_fusion
  259.1 3.2 copy.54
  262.3 2.7 copy.80
  265.1 6.5 gather_fusion.6
  271.6 7.2 bitcast_select_fusion.1
  278.8 6.5 gather_fusion.4
  285.3 7.2 bitcast_select_fusion.2
  292.5 6.5 gather_fusion.2
  299.0 7.7 bitcast_select_fusion.3
  306.7 7.9 pad_maximum_fusion
  314.5 8.5 copy.49
  323.1 49.5 %all-to-all-start.1 = ((f32[128,3,1,1,128,128]{5,4,3,2,1,0:T(8,128)}), f32[128,3,1,1,128,128]{5,4,3,2,1,0:T(8,128)}, u32[]{:S(2)}, u32[]{:S(2)}) async-start(f32[128,3,1,1,128,128]{5,4,3,2,1,0:T(8,128)} %copy.49), calls=%async_computation.1 | async-start | bytes 50331648 | tf_op jit(solution)/shard_map/all_to_all | solution.py:52
  372.6 0.1 copy.40
  372.7 0.2 reshape.1239
  372.9 444.9 %psum.7 = f32[]{:T(128)} all-reduce(f32[]{:T(128)S(6)} %add.631), channel_id=1, replica_groups=mesh['row'=16,'col'=8] {'row','col'}, use_global_device_ids=true, to_apply=%region_22.23 | all-reduce | flops 1 | bytes 8 | tf_op jit(solution)/shard_map/psum | solution.py:142
  818.5 17.1 %bitcast_select_fusion = f32[128,3,1,1,128,128]{5,4,1,0,3,2:T(8,128)} fusion(f32[128,3,1,1,128,128]{5,4,3,2,1,0:T(8,128)} %all-to-all-done.1, pred[128,3]{1,0:T(8,128)(4,1)S(1)} %fusion.71), kind=kLoop, calls=%fused_computation.120 | loop fusion | flops 6291456 | bytes 50332032 | tf_op jit(solution)/shard_map/jit(_where)/select_n | solution.py:136
  835.6 0.2 broadcast_in_dim.94
  835.8 52.5 %scatter_fusion = f32[4,8,128,128]{3,2,1,0:T(8,128)S(1)} fusion(f32[4,8,128,128]{3,2,1,0:T(8,128)S(1)} %broadcast_in_dim.94, s32[384]{0:T(512)S(1)} %reshape.1239, f32[384,128,128]{2,1,0:T(8,128)} %bitcast.190), kind=kCustom, calls=%fused_computation.7 | custom fusion | flops 6291456 | bytes 75500544 | tf_op jit(solution)/shard_map/scatter-add | solution.py:140
  888.3 1.3 copy-done.2
  (57 shorter events, 2.0 us)
Async XLA Ops:
  0.6 2.6 copy-start
  3.2 16.3 %copy-start.8 = (s32[128]{0:T(128)S(1)}, s32[128]{0:T(128)}, u32[]{:S(2)}) copy-start(s32[128]{0:T(128)} %param.15) | copy-start | bytes 1540
  30.3 174.0 %all-to-all-start = ((bf16[128,3,1,1,128,128]{5,4,3,2,1,0:T(8,128)(2,1)}), bf16[128,3,1,1,128,128]{5,4,3,2,1,0:T(8,128)(2,1)}, u32[]{:S(2)}, u32[]{:S(2)}) async-start(bf16[128,3,1,1,128,128]{5,4,3,2,1,0:T(8,128)(2,1)} %select_bitcast_fusion), calls=%async_computation | async-start | bytes 25165824 | tf_op jit(solution)/shard_map/all_to_all | solution.py:47
  41.0 168.8 %copy-start.7 = (f32[3,256]{1,0:T(4,128)S(1)}, f32[3,256]{1,0:T(4,128)}, u32[]{:S(2)}) copy-start(f32[3,256]{1,0:T(4,128)} %param.13) | copy-start | bytes 9220
  238.2 3.8 copy-start.6
  299.0 7.7 copy-start.3
  323.1 495.4 %all-to-all-start.1 = ((f32[128,3,1,1,128,128]{5,4,3,2,1,0:T(8,128)}), f32[128,3,1,1,128,128]{5,4,3,2,1,0:T(8,128)}, u32[]{:S(2)}, u32[]{:S(2)}) async-start(f32[128,3,1,1,128,128]{5,4,3,2,1,0:T(8,128)} %copy.49), calls=%async_computation.1 | async-start | bytes 50331648 | tf_op jit(solution)/shard_map/all_to_all | solution.py:52
  835.8 53.8 %copy-start.1 = (bf16[4,8,128,128]{3,2,1,0:T(8,128)(2,1)S(1)}, bf16[4,8,128,128]{3,2,1,0:T(8,128)(2,1)}, u32[]{:S(2)}) copy-start(bf16[4,8,128,128]{3,2,1,0:T(8,128)(2,1)} %param.11) | copy-start | bytes 3145732
  888.3 1.3 copy-start.2
where the time goes:
time: 906 us; the launch traced here: 891 us
  blocking collectives  445 us (49%)
  waiting for transfers between devices  149 us (16%)
  other arithmetic  128 us (14%)
  local copies, waits for them, and re-layouts  97.4 us (11%)
  starting transfers between devices  60.2 us (7%)
    psum x1, blocking collectives, shards(): total = lax.psum(energy, ('row', 'col'))  445 us
    all_to_all x1, waiting for transfers between devices, move_blocks(): lax.all_to_all(outgoing, ('row', 'col'), split_axis=0, concat_axis=0, til...  149 us
    scatter-add x1, other arithmetic, shards(): potential = jnp.zeros(density.shape, jnp.float32).at[rows_local[:, :, :,...  52.5 us
    all_to_all x1, starting transfers between devices, move_partials(): lax.all_to_all(outgoing, ('row', 'col'), split_axis=0, concat_axis=0, til...  49.5 us
    select_n x3, other arithmetic, shards(): returns.append(jnp.where(fits[..., None, None], taken, 0.0))  22.1 us
    gather x3, local copies, waits for them, and re-layouts, shards(): pieces[jnp.minimum(row_pos, span - 1)[:, None, :, None], jnp.minimum(col_...  19.5 us
  transfers between devices with their start and end apart: 2, of which 1 were waited for; matrix products, arithmetic and copies ran while one was open for 1% of the time, Pallas kernels for 0%

commit v1 on v0

v1 whole, which is shorter than its diff:
```python
import functools

import jax
import jax.numpy as jnp
import numpy as np
from jax import lax
from jax.experimental import pallas as pl
from jax.experimental.pallas import tpu as pltpu
from jax.sharding import Mesh, PartitionSpec as P

CX = 0.7385587663820224
MU = 0.2195149727645171
KAPPA = 0.804
BF = 128
KB = 8
NBLK = 64
G = 256
SLOTS = 3
KF = 1024
N_ROW = 16
N_COL = 8
HALF = 64
MIB = 1024 * 1024
ROW = ("h", "xl", "y")
COL = ("z", "c")
ALL = ROW + COL
GROUP = ("xl", "y", "z", "c")
ANY = pl.BlockSpec(memory_space=pl.ANY)


def half_band_kernel(where, density, out, sems):
    copies = [
        pltpu.make_async_copy(density.at[a, where[a]], out.at[a], sems.at[a])
        for a in range(NBLK // N_ROW)
    ]
    for copy in copies:
        copy.start()
    for copy in copies:
        copy.wait()


def half_band(density, row_id, col_id):
    turns = jnp.arange(NBLK // N_ROW, dtype=jnp.int32)
    shift = jnp.mod(col_id - row_id, N_COL)
    where = jnp.minimum((row_id + N_ROW * turns + shift) // N_COL, NBLK // N_COL - 1)
    return pl.pallas_call(
        half_band_kernel,
        out_shape=jax.ShapeDtypeStruct((NBLK // N_ROW, BF, BF), jnp.bfloat16),
        grid_spec=pltpu.PrefetchScalarGridSpec(
            num_scalar_prefetch=1,
            grid=(),
            in_specs=[ANY],
            out_specs=ANY,
            scratch_shapes=[pltpu.SemaphoreType.DMA((NBLK // N_ROW,))],
        ),
        name="half_band",
    )(where.astype(jnp.int32), density)


def batch_kernel(
    scal, weights, basis, band, out, energy, phis, upper, mat, pair, stage, sem_b, sem_u, sem_o
):
    count = scal[SLOTS]

    def basis_copy(slot):
        return pltpu.make_async_copy(basis.at[slot], phis.at[slot], sem_b.at[slot])

    def row_copy(slot, o):
        i = scal[slot] + o
        return pltpu.make_async_copy(
            band.at[lax.rem(i, N_ROW), :, i // N_ROW], upper.at[slot, o], sem_u.at[slot, o]
        )

    def out_copy(slot):
        return pltpu.make_async_copy(stage.at[slot], out.at[:, slot], sem_o.at[slot])

    def fetch(slot, carry):
        basis_copy(slot).start()
        for o in range(KB):
            row_copy(slot, o).start()
        return carry

    lax.fori_loop(0, count, fetch, 0)

    def work(slot, total):
        start = scal[slot]
        for o in range(KB):
            row_copy(slot, o).wait()
        for o1 in range(KB):
            for o2 in range(o1, KB):
                block = upper[slot, o1, lax.rem(start + o2, KB)]
                mat[o1 * BF : (o1 + 1) * BF, o2 * BF : (o2 + 1) * BF] = block
                if o2 == o1 + 1 and o1 % 2 == 0:
                    mat[o2 * BF : (o2 + 1) * BF, o1 * BF : (o1 + 1) * BF] = block.T
        basis_copy(slot).wait()
        sums = [jnp.zeros((G, 1), jnp.float32) for _ in range(4)]
        for t in range(4):
            lo, hi = 256 * t, 256 * (t + 1)
            product = jnp.dot(
                phis[slot, 0, :, :hi], mat[:hi, lo:hi], preferred_element_type=jnp.float32
            )
            if hi < KF:
                product += lax.dot_general(
                    phis[slot, 0, :, hi:],
                    mat[lo:hi, hi:],
                    (((1,), (1,)), ((), ())),
                    preferred_element_type=jnp.float32,
                )
            for k in range(4):
                sums[k] += jnp.sum(
                    phis[slot, k, :, lo:hi].astype(jnp.float32) * product, axis=1, keepdims=True
                )
        rho = sums[0]
        grads = [2.0 * x for x in sums[1:]]
        sigma = grads[0] * grads[0] + grads[1] * grads[1] + grads[2] * grads[2]
        quad = weights[slot]
        square = rho * rho + 1.0
        logs = jnp.log(square)
        cube = jnp.exp(logs * (1.0 / 3.0))
        scaled = cube * cube
        reduced = sigma / (scaled * scaled)
        denom = 1.0 + MU * reduced / KAPPA
        factor = 1.0 + MU * reduced / denom
        slope = MU / denom / denom
        point = -CX * scaled * factor
        by_rho = (-CX * 2.0) * rho / cube * ((2.0 / 3.0) * factor - (4.0 / 3.0) * slope * reduced)
        by_sigma = -CX * slope / scaled
        wr = 0.5 * quad * by_rho
        ws = 2.0 * quad * by_sigma
        total = total + jnp.sum(quad * point)
        coeffs = [wr] + [ws * x for x in grads]
        for t in range(4):
            lo, hi = 256 * t, 256 * (t + 1)
            mixed = coeffs[0] * phis[slot, 0, :, lo:hi].astype(jnp.float32)
            for k in range(1, 4):
                mixed += coeffs[k] * phis[slot, k, :, lo:hi].astype(jnp.float32)
            pair[:G, lo:hi] = mixed.astype(jnp.bfloat16)
        pair[G:, :] = phis[slot, 0]
        for t in range(4):
            lo, hi = 256 * t, 256 * (t + 1)
            left = jnp.concatenate([pair[G:, lo:hi], pair[:G, lo:hi]], axis=0)
            rows = lax.dot_general(
                left, pair[...], (((0,), (0,)), ((), ())), preferred_element_type=jnp.float32
            ).astype(jnp.bfloat16)
            for k in range(2):
                a = lax.rem(start + 2 * t + k, KB)
                for o2 in range(KB):
                    b = lax.rem(start + o2, KB)
                    stage[slot, a * KB + b] = rows[
                        k * BF : (k + 1) * BF, o2 * BF : (o2 + 1) * BF
                    ]
        out_copy(slot).start()
        return total

    total = lax.fori_loop(0, count, work, jnp.float32(0.0))
    energy[...] = jnp.full(energy.shape, total, jnp.float32)

    def drain(slot, carry):
        out_copy(slot).wait()
        return carry

    lax.fori_loop(0, count, drain, 0)


def batches(scal, weights, basis, band):
    return pl.pallas_call(
        batch_kernel,
        out_shape=(
            jax.ShapeDtypeStruct((HALF, SLOTS, BF, BF), jnp.bfloat16),
            jax.ShapeDtypeStruct((1, BF), jnp.float32),
        ),
        grid_spec=pltpu.PrefetchScalarGridSpec(
            num_scalar_prefetch=1,
            grid=(),
            in_specs=[pl.BlockSpec(memory_space=pltpu.VMEM), ANY, ANY],
            out_specs=[ANY, pl.BlockSpec(memory_space=pltpu.VMEM)],
            scratch_shapes=[
                pltpu.VMEM((SLOTS, 4, G, KF), jnp.bfloat16),
                pltpu.VMEM((SLOTS, KB, KB, BF, BF), jnp.bfloat16),
                pltpu.VMEM((KF, KF), jnp.bfloat16),
                pltpu.VMEM((2 * G, KF), jnp.bfloat16),
                pltpu.VMEM((SLOTS, HALF, BF, BF), jnp.bfloat16),
                pltpu.SemaphoreType.DMA((SLOTS,)),
                pltpu.SemaphoreType.DMA((SLOTS, KB)),
                pltpu.SemaphoreType.DMA((SLOTS,)),
            ],
        ),
        compiler_params=pltpu.CompilerParams(vmem_limit_bytes=44 * MIB),
        name="batches",
    )(scal, weights, basis, band)


CHUNK = 8


def collect_kernel(scal, arrived, acc):
    step = pl.program_id(0)
    a, b, h = scal[HALF * (SLOTS + 1)], scal[HALF * (SLOTS + 1) + 1], scal[HALF * (SLOTS + 1) + 2]

    @pl.when(step == 0)
    def _():
        acc[...] = jnp.zeros(acc.shape, acc.dtype)

    def source(k, carry):
        peer = step * CHUNK + k

        def one(slot, inner):
            start = scal[peer * SLOTS + slot]
            i = start + lax.rem(a - start + NBLK, KB)
            j = start + lax.rem(b - start + NBLK, KB)
            below = jnp.where(j < i, 1, 0)
            turn = i // KB
            other = jnp.where(lax.rem(turn, 2) == h, 0, 1)
            acc[other, below, turn // 2] += arrived[k, slot].astype(jnp.float32)
            return inner

        lax.fori_loop(0, scal[HALF * SLOTS + peer], one, 0)
        return carry

    lax.fori_loop(0, CHUNK, source, 0)


def collect(scal, arrived):
    shape = (2, 2, NBLK // N_ROW, BF, BF)
    return pl.pallas_call(
        collect_kernel,
        out_shape=jax.ShapeDtypeStruct(shape, jnp.float32),
        grid_spec=pltpu.PrefetchScalarGridSpec(
            num_scalar_prefetch=1,
            grid=(HALF // CHUNK,),
            in_specs=[pl.BlockSpec((CHUNK, SLOTS, BF, BF), lambda s, _: (s, 0, 0, 0))],
            out_specs=pl.BlockSpec(shape, lambda s, _: (0, 0, 0, 0, 0)),
        ),
        compiler_params=pltpu.CompilerParams(vmem_limit_bytes=16 * MIB),
        name="collect",
    )(scal, arrived)


def place_kernel(scal, mine, theirs, out):
    turn = pl.program_id(0)
    row_id, shift = scal[0], scal[1]
    out[...] = jnp.zeros(out.shape, out.dtype)
    at = (row_id + N_ROW * turn + shift) // N_COL

    @pl.when(at < NBLK // N_COL)
    def _():
        out[0, at] = mine[0, 0] + theirs[0, 0]

    @pl.when((at > 0) & (shift > 0))
    def _():
        out[0, at - 1] = mine[1, 0] + theirs[1, 0]


def place(scal, mine, theirs):
    block = pl.BlockSpec((2, 1, BF, BF), lambda t, _: (0, t, 0, 0))
    return pl.pallas_call(
        place_kernel,
        out_shape=jax.ShapeDtypeStruct((NBLK // N_ROW, NBLK // N_COL, BF, BF), jnp.float32),
        grid_spec=pltpu.PrefetchScalarGridSpec(
            num_scalar_prefetch=1,
            grid=(NBLK // N_ROW,),
            in_specs=[block, block],
            out_specs=pl.BlockSpec((1, NBLK // N_COL, BF, BF), lambda t, _: (t, 0, 0, 0)),
        ),
        name="place",
    )(scal, mine, theirs)


def shards(density, basis, weights, batch_start, batch_count):
    row_id = lax.axis_index(ROW).astype(jnp.int32)
    col_id = lax.axis_index(COL).astype(jnp.int32)
    half_id = lax.axis_index("h").astype(jnp.int32)
    self_index = row_id * N_COL + col_id
    shift = jnp.mod(col_id - row_id, N_COL)

    band = lax.all_gather(half_band(density, row_id, col_id), ALL, axis=0, tiled=True)
    band = band.reshape(N_ROW, N_COL, NBLK // N_ROW, BF, BF)

    own_starts = lax.dynamic_slice(batch_start, (self_index * SLOTS,), (SLOTS,))
    own_count = lax.dynamic_slice(batch_count, (self_index,), (1,))
    scal = jnp.concatenate([own_starts, own_count])
    outgoing, energy = batches(scal, weights.reshape(SLOTS, G, 1), basis, band)

    energies = lax.all_gather(energy, ALL, axis=0, tiled=True)
    arrived = lax.all_to_all(outgoing, GROUP, split_axis=0, concat_axis=0, tiled=True)

    half_starts = lax.dynamic_slice(batch_start, (half_id * HALF * SLOTS,), (HALF * SLOTS,))
    half_counts = lax.dynamic_slice(batch_count, (half_id * HALF,), (HALF,))
    ids = jnp.stack([jnp.mod(row_id, KB), col_id, half_id])
    acc = collect(jnp.concatenate([half_starts, half_counts, ids]), arrived)
    theirs = lax.ppermute(acc[1], "h", [(0, 1), (1, 0)])
    potential = place(jnp.stack([row_id, shift]), acc[0], theirs)
    return potential, jnp.sum(energies[:, 0]) / (NBLK * BF)


def solution(mesh):
    fine = Mesh(np.asarray(mesh.devices).reshape(2, 2, 4, 4, 2), ALL)
    in_specs = (P(ROW, COL), P(ALL), P(ALL), P(), P())
    out_specs = (P(ROW, COL), P())
    return jax.shard_map(shards, mesh=fine, in_specs=in_specs, out_specs=out_specs, check_vma=False)
```

time: 906 us -> 266 us (0.29); the launches traced: 891 us -> 262 us
  blocking collectives: 445 us -> 40.8 us
  other arithmetic: 128 us -> 2.51 us
  local copies, waits for them, and re-layouts: 97.4 us -> 7.45 us
  starting transfers between devices: 60.2 us -> 16 us
  Pallas kernels: 0 us -> 24.4 us
  between operations: 5.21 us -> 15.9 us
    psum x1 -> x0, blocking collectives: 445 us -> none  [shards(): total = lax.psum(energy, ('row', 'col'))]
    all_gather x0 -> x1, waiting for transfers between devices: none -> 79 us  [shards(): lax.all_gather(half_band(density, row_id, col_id), ALL, axis=0, tiled=True)]
    all_to_all x2 -> x1, waiting for transfers between devices: 149 us -> 75.6 us  [shards(): lax.all_to_all(outgoing, GROUP, split_axis=0, concat_axis=0, tiled=True)]
    select_n x12 -> x0, other arithmetic: 53.7 us -> none  [the longest x3 22.1 us: shards(): returns.append(jnp.where(fits[..., None, None], taken, 0.0))]
    gather x7 -> x0, local copies, waits for them, and re-layouts: 52.6 us -> none  [the longest x3 19.5 us: shards(): pieces[jnp.minimum(row_pos, span - 1)[:, None, :, None], jnp.minimum(col_...]
    scatter-add x1 -> x0, other arithmetic: 52.5 us -> none  [shards(): potential = jnp.zeros(density.shape, jnp.float32).at[rows_local[:, :, :,...]
    all_to_all x2 -> x1, starting transfers between devices: 60.2 us -> 15.3 us  [shards(): lax.all_to_all(outgoing, GROUP, split_axis=0, concat_axis=0, tiled=True)]
    all_gather x0 -> x1, blocking collectives: none -> 40.8 us  [shards(): energies = lax.all_gather(energy, ALL, axis=0, tiled=True)]
  transfers between devices with their start and end apart: 2 -> 3, of which waited for: 1 -> 2; matrix products, arithmetic and copies ran while one was open for 1% -> 2% of each run, Pallas kernels for 0% -> 0%
where the time goes in v1:
time: 266 us; the launch traced here: 262 us
  waiting for transfers between devices  155 us (58%)
  blocking collectives  40.8 us (15%)
  Pallas kernels  24.4 us (9%)
  starting transfers between devices  16 us (6%)
  between operations  15.9 us (6%)
  local copies, waits for them, and re-layouts  7.45 us (3%)
    all_gather x1, waiting for transfers between devices, shards(): lax.all_gather(half_band(density, row_id, col_id), ALL, axis=0, tiled=True)  79 us
    all_to_all x1, waiting for transfers between devices, shards(): lax.all_to_all(outgoing, GROUP, split_axis=0, concat_axis=0, tiled=True)  75.6 us
    all_gather x1, blocking collectives, shards(): energies = lax.all_gather(energy, ALL, axis=0, tiled=True)  40.8 us
    all_to_all x1, starting transfers between devices, shards(): lax.all_to_all(outgoing, GROUP, split_axis=0, concat_axis=0, tiled=True)  15.3 us
    pallas_call x1, Pallas kernels, collect(): pl.pallas_call(collect_kernel, out_shape=jax.ShapeDtypeStruct(shape, jnp....  7.67 us
    pallas_call x1, Pallas kernels, batches(): pl.pallas_call(batch_kernel, out_shape=(jax.ShapeDtypeStruct((HALF, SLOTS...  6.63 us
    pallas_call x1, Pallas kernels, half_band(): pl.pallas_call(half_band_kernel, out_shape=jax.ShapeDtypeStruct((NBLK //...  5.77 us
  transfers between devices with their start and end apart: 3, of which 2 were waited for; matrix products, arithmetic and copies ran while one was open for 2% of the time, Pallas kernels for 0%

profile of v1, /device:TPU:18, one launch (start us, length us, event | category | flops | bytes accessed | tf_op | source)
XLA Modules:
  0.0 261.7 jit_solution(13479056877970097084)
XLA Ops:
  7.2 0.0 all-gather.3.cloned.1.call-start
  7.2 0.6 fusion.where
  7.8 5.8 %half_band.1 = bf16[4,128,128]{2,1,0:T(8,128)(2,1)} custom-call(s32[4]{0:T(128)} %fusion.where, bf16[4,8,128,128]{3,2,1,0:T(8,128)(2,1)} %density.1), custom_call_target="tpu_custom_call" | custom-call | tf_op jit(solution)/shard_map/half_band/pallas_call | solution.py:46
  13.6 0.0 all-gather.3.cloned.1.call-update
  13.6 0.9 copy.8.weights
  14.5 0.8 dynamic_slice.14
  15.3 1.3 dynamic_slice.15
  16.6 0.7 pad_add_fusion.1.scal
  17.3 79.0 %all-gather.3.cloned.1.call-done = bf16[512,128,128]{2,1,0:T(8,128)(2,1)} async-done(((bf16[4,128,128]{2,1,0:T(8,128)(2,1)}), bf16[512,128,128]{2,1,0:T(8,128)(2,1)}) %all-gather.3.cloned.1.call-update) | async-done | bytes 16777232 | tf_op jit(solution)/shard_map/all_gather | solution.py:276
  96.3 6.6 %batches.1 = (bf16[64,3,128,128]{3,2,1,0:T(8,128)(2,1)S(1)}, f32[1,128]{1,0:T(1,128)S(1)}) custom-call(s32[4]{0:T(128)S(1)} %pad_add_fusion.1.scal, f32[3,256,1]{2,1,0:T(8,128)S(1)} %copy.8.weights, bf16[3,4,256,1024]{3,2,1,0:T(8,128)(2,1)} %basis.1, bf16[16,8,4,128,128]{4,3,2,1,0:T(8,128)(2,1)} %bitcast.14), custom_call_target="tpu_custom_call" | custom-call | tf_op jit(solution)/shard_map/batches/pallas_call | solution.py:166
  102.9 0.0 copy-start
  102.9 2.6 %copy-done = bf16[64,3,128,128]{3,2,1,0:T(8,128)(2,1)} copy-done((bf16[64,3,128,128]{3,2,1,0:T(8,128)(2,1)}, bf16[64,3,128,128]{3,2,1,0:T(8,128)(2,1)S(1)}, u32[]{:S(2)}) %copy-start) | copy-done | bytes 6291480
  105.6 0.0 copy-start.2
  105.6 0.0 copy-start.3
  105.6 15.3 %all-to-all-start = ((bf16[64,3,128,128]{3,2,1,0:T(8,128)(2,1)}), bf16[64,3,128,128]{3,2,1,0:T(8,128)(2,1)}, u32[]{:S(2)}, u32[]{:S(2)}) async-start(bf16[64,3,128,128]{3,2,1,0:T(8,128)(2,1)} %copy-done), calls=%async_computation | async-start | bytes 12582912 | tf_op jit(solution)/shard_map/all_to_all | solution.py:285
  120.9 0.0 copy-done.2
  120.9 0.1 dynamic_slice.12
  121.0 0.0 copy-done.3
  121.0 0.1 dynamic_slice.13
  121.1 0.1 concatenate.6.scal
  121.2 75.6 %all-to-all-done.arrived = bf16[64,3,128,128]{3,2,1,0:T(8,128)(2,1)} async-done(((bf16[64,3,128,128]{3,2,1,0:T(8,128)(2,1)}), bf16[64,3,128,128]{3,2,1,0:T(8,128)(2,1)}, u32[]{:S(2)}, u32[]{:S(2)}) %all-to-all-start) | async-done | bytes 6291488 | tf_op jit(solution)/shard_map/all_to_all | solution.py:285
  196.8 7.7 %collect.1 = f32[2,2,4,128,128]{4,3,2,1,0:T(8,128)S(1)} custom-call(s32[259]{0:T(512)S(1)} %concatenate.6.scal, bf16[64,3,128,128]{3,2,1,0:T(8,128)(2,1)} %all-to-all-done.arrived), custom_call_target="tpu_custom_call" | custom-call | tf_op jit(solution)/shard_map/collect/pallas_call | solution.py:225
  204.5 0.9 slice_bitcast_fusion
  205.3 0.6 collective-permute-start
  205.9 0.6 pad_add_fusion.scal
  206.6 40.8 %all-gather = f32[128,1,128]{2,1,0:T(1,128)S(1)} all-gather(f32[1,1,128]{2,1,0:T(1,128)S(1)} %bitcast.13), channel_id=1, replica_groups=mesh['h'=2,'xl'=2,'y'=4,'z'=4,'c'=2] {'h','xl','y','z','c'}, dimensions={0}, use_global_device_ids=true | all-gather | bytes 66048 | tf_op jit(solution)/shard_map/all_gather | solution.py:284
  247.3 0.6 slice_reduce_fusion
  248.6 0.0 collective-permute-done.theirs
  248.6 0.0 copy-start.1
  248.6 0.8 copy-done.1
  249.4 4.3 %place.1 = f32[4,8,128,128]{3,2,1,0:T(8,128)} custom-call(s32[2]{0:T(128)} %pad_add_fusion.scal, f32[2,4,128,128]{3,2,1,0:T(8,128)} %get-tuple-element.7.mine, f32[2,4,128,128]{3,2,1,0:T(8,128)} %copy-done.1), custom_call_target="tpu_custom_call" | custom-call | tf_op jit(solution)/shard_map/place/pallas_call | solution.py:256
Async XLA Ops:
  7.2 89.1 %all-gather.3.cloned.1.call-start = ((), (), s32[]{:S(2)}) async-start(), calls=%async_computation.1 | async-start | bytes 16908288 | tf_op jit(solution)/shard_map/all_gather | solution.py:276
  102.9 2.6 %copy-start = (bf16[64,3,128,128]{3,2,1,0:T(8,128)(2,1)}, bf16[64,3,128,128]{3,2,1,0:T(8,128)(2,1)S(1)}, u32[]{:S(2)}) copy-start(bf16[64,3,128,128]{3,2,1,0:T(8,128)(2,1)S(1)} %get-tuple-element.4) | copy-start | bytes 18874372
  105.6 15.4 %copy-start.2 = (s32[384]{0:T(512)S(1)}, s32[384]{0:T(512)}, u32[]{:S(2)}) copy-start(s32[384]{0:T(512)} %param.8) | copy-start | bytes 4612
  105.6 15.4 %copy-start.3 = (s32[128]{0:T(128)S(1)}, s32[128]{0:T(128)}, u32[]{:S(2)}) copy-start(s32[128]{0:T(128)} %param.9) | copy-start | bytes 1540
  105.6 91.2 %all-to-all-start = ((bf16[64,3,128,128]{3,2,1,0:T(8,128)(2,1)}), bf16[64,3,128,128]{3,2,1,0:T(8,128)(2,1)}, u32[]{:S(2)}, u32[]{:S(2)}) async-start(bf16[64,3,128,128]{3,2,1,0:T(8,128)(2,1)} %copy-done), calls=%async_computation | async-start | bytes 12582912 | tf_op jit(solution)/shard_map/all_to_all | solution.py:285
  205.3 43.3 %collective-permute-start = (f32[2,4,128,128]{3,2,1,0:T(8,128)S(1)}, f32[2,4,128,128]{3,2,1,0:T(8,128)S(1)}, u32[]{:S(2)}, u32[]{:S(2)}) collective-permute-start(f32[2,4,128,128]{3,2,1,0:T(8,128)S(1)} %get-tuple-element.6), channel_id=1, source_target_pairs={{0,64},{64,0},{1,65},{65,1},{2,66},{66,2},{3,67},{67,3},{4,68},{68... | collective-permute-start | bytes 1572872 | tf_op jit(solution)/shard_map/ppermute | solution.py:291
  248.6 0.8 copy-start.1
Sparse Core Ops, SparseCore 0:
  13.7 82.5 all-gather.2

commit v2 on v1

v2 whole, which is shorter than its diff:
```python
import jax
import jax.numpy as jnp
import numpy as np
from jax import lax
from jax.experimental import pallas as pl
from jax.experimental.pallas import tpu as pltpu
from jax.sharding import Mesh, PartitionSpec as P

CX = 0.7385587663820224
MU = 0.2195149727645171
KAPPA = 0.804
BF = 128
KB = 8
NBLK = 64
G = 256
SLOTS = 3
KF = 1024
N_ROW = 16
N_COL = 8
TURNS = NBLK // N_ROW
PEERS = 64
MIB = 1024 * 1024
HB = BF // 2
EXT = SLOTS * HB
ROWS = EXT + 16
BAND = 2 * TURNS * HB
ROW = ("h", "xl", "y")
COL = ("z", "c")
ALL = ROW + COL
GROUP = ("xl", "y", "z", "c")
VMEM = pl.BlockSpec(memory_space=pltpu.VMEM)
HBM = pl.BlockSpec(memory_space=pltpu.HBM)
ANY = pl.BlockSpec(memory_space=pl.ANY)
F32 = jnp.float32
BF16 = jnp.bfloat16


def lanes(shape):
    return lax.broadcasted_iota(jnp.int32, shape, 0), lax.broadcasted_iota(jnp.int32, shape, 1)


def pack_symmetric(full):
    r, c = lanes((HB, BF))
    top, bottom = full[:HB], full[HB:]
    packed = jnp.where((c >= HB) | (r <= c), top, pltpu.roll(bottom, HB, 1))
    row = jnp.sum(jnp.where(c - HB == r, bottom, 0.0), axis=0, keepdims=True)
    return packed, row


def unpack_symmetric(packed, row):
    r, c = lanes((HB, BF))
    flip = jnp.concatenate([packed, packed], axis=0).T
    top = jnp.where((c >= HB) | (r <= c), packed, flip[:HB])
    corner = jnp.where(c - HB < r, pltpu.roll(packed, HB, 1), flip[:HB])
    corner = jnp.where(c - HB == r, row, corner)
    return jnp.concatenate([top, jnp.where(c < HB, flip[HB:], corner)], axis=0)


def pick_row(rows, index):
    r, _ = lanes(rows.shape)
    return jnp.sum(jnp.where(r == index, rows, 0.0), axis=0, keepdims=True)


def entry(scal, peer, slot):
    a, b, h = scal[PEERS * (SLOTS + 1)], scal[PEERS * (SLOTS + 1) + 1], scal[PEERS * (SLOTS + 1) + 2]
    start = scal[peer * SLOTS + slot]
    i = start + lax.rem(a - start + NBLK, KB)
    j = start + lax.rem(b - start + NBLK, KB)
    turn = i // KB
    other = jnp.where(lax.rem(turn, 2) == h, 0, 1)
    below = jnp.where(j < i, TURNS, 0)
    return other, turn // 2, pl.multiple_of((below + turn // 2) * HB, HB)


def share_kernel(scal, density, out):
    row_id, shift = scal[0], scal[1]
    row, _ = lanes((16, BF))
    out[BAND:, :] = jnp.zeros((16, BF), BF16)
    for t in range(TURNS):
        at = (row_id + N_ROW * t + shift) // N_COL
        low = TURNS * HB + t * HB

        @pl.when(shift > 0)
        def _():
            out[t * HB : (t + 1) * HB, :] = density[t, jnp.minimum(at, N_COL - 1), :HB, :]
            flip = density[t, jnp.maximum(at - 1, 0)].astype(F32).T
            out[low : low + HB, :] = flip[HB:].astype(BF16)

        @pl.when(shift == 0)
        def _():
            packed, line = pack_symmetric(density[t, at].astype(F32))
            out[t * HB : (t + 1) * HB, :] = packed.astype(BF16)
            out[low : low + HB, :] = jnp.zeros((HB, BF), BF16)
            old = out[BAND:, :].astype(F32)
            out[BAND:, :] = jnp.where(row == t, line, old).astype(BF16)


def share(scal, density):
    return pl.pallas_call(
        share_kernel,
        out_shape=jax.ShapeDtypeStruct((BAND + 16, BF), BF16),
        grid_spec=pltpu.PrefetchScalarGridSpec(
            num_scalar_prefetch=1, grid=(), in_specs=[VMEM], out_specs=VMEM
        ),
        name="share",
    )(scal, density)


CHUNK = 8


def pack_kernel(scal, mine, theirs, out, table, lines, buf, sems):
    table[0] = mine[:BAND, :]
    table[1] = theirs[:BAND, :]
    lines[0] = mine[BAND:, :].astype(F32)
    lines[1] = theirs[BAND:, :].astype(F32)
    row, _ = lanes((16, BF))

    def send(chunk):
        span = pl.ds(pl.multiple_of(chunk * CHUNK, CHUNK), CHUNK)
        return pltpu.make_async_copy(buf.at[span], out.at[span], sems.at[chunk])

    def one_chunk(chunk, carry):
        def one_peer(k, inner):
            peer = chunk * CHUNK + k

            def one(slot, ext):
                other, turn, at = entry(scal, peer, slot)
                buf[peer, pl.ds(pl.multiple_of(slot * HB, HB), HB), :] = table[
                    other, pl.ds(at, HB), :
                ]
                return jnp.where(row == slot, lines[other, pl.ds(turn, 1), :], ext)

            ext = lax.fori_loop(0, scal[PEERS * SLOTS + peer], one, jnp.zeros((16, BF), F32))
            buf[peer, EXT:, :] = ext.astype(BF16)
            return inner

        lax.fori_loop(0, CHUNK, one_peer, 0)
        send(chunk).start()
        return carry

    lax.fori_loop(0, PEERS // CHUNK, one_chunk, 0)

    def drain(chunk, carry):
        send(chunk).wait()
        return carry

    lax.fori_loop(0, PEERS // CHUNK, drain, 0)


def pack(scal, mine, theirs):
    return pl.pallas_call(
        pack_kernel,
        out_shape=jax.ShapeDtypeStruct((PEERS, ROWS, BF), BF16),
        grid_spec=pltpu.PrefetchScalarGridSpec(
            num_scalar_prefetch=1,
            grid=(),
            in_specs=[VMEM, VMEM],
            out_specs=HBM,
            scratch_shapes=[
                pltpu.VMEM((2, BAND, BF), BF16),
                pltpu.VMEM((2, 16, BF), F32),
                pltpu.VMEM((PEERS, ROWS, BF), BF16),
                pltpu.SemaphoreType.DMA((PEERS // CHUNK,)),
            ],
        ),
        compiler_params=pltpu.CompilerParams(vmem_limit_bytes=16 * MIB),
        name="pack",
    )(scal, mine, theirs)


def batch_kernel(
    scal, weights, basis, window, out,
    phis, win, win_ext, mat, pair, stage, stage_ext, lines, sem_b, sem_w, sem_o, sem_e,
):
    count = scal[SLOTS]
    row, lane = lanes((16, BF))

    def span(slot):
        return pl.ds(pl.multiple_of(slot * HB, HB), HB)

    def basis_copy(slot):
        return pltpu.make_async_copy(basis.at[slot], phis.at[slot], sem_b.at[slot])

    def window_copy(slot):
        return pltpu.make_async_copy(window.at[:, span(slot)], win.at[slot], sem_w.at[slot])

    def out_copy(slot):
        return pltpu.make_async_copy(stage.at[slot], out.at[:, span(slot)], sem_o.at[slot])

    ext_in = pltpu.make_async_copy(window.at[:, pl.ds(EXT, 16)], win_ext, sem_e.at[0])
    ext_out = pltpu.make_async_copy(stage_ext, out.at[:, pl.ds(EXT, 16)], sem_e.at[1])

    def fetch(slot, carry):
        window_copy(slot).start()
        basis_copy(slot).start()
        return carry

    ext_in.start()
    lax.fori_loop(0, count, fetch, 0)
    lines[...] = jnp.zeros(lines.shape, F32)
    ext_in.wait()

    def work(slot, total):
        start = scal[slot]
        cls = [lax.rem(start + o, KB) for o in range(KB)]
        window_copy(slot).wait()
        for o1 in range(KB):
            r1 = o1 * BF
            for o2 in range(o1 + 1, KB):
                top = win[slot, cls[o1] * KB + cls[o2]]
                bottom = win[slot, cls[o2] * KB + cls[o1]]
                mat[r1 : r1 + HB, o2 * BF : (o2 + 1) * BF] = top
                mat[r1 + HB : r1 + BF, o2 * BF : (o2 + 1) * BF] = bottom
                if o2 == o1 + 1 and o1 % 2 == 0:
                    mat[o2 * BF : (o2 + 1) * BF, r1 : r1 + BF] = jnp.concatenate(
                        [top, bottom], axis=0
                    ).T
            line = pick_row(win_ext[cls[o1] * (KB + 1)].astype(F32), slot)
            block = unpack_symmetric(win[slot, cls[o1] * (KB + 1)].astype(F32), line)
            mat[r1 : r1 + BF, r1 : r1 + BF] = block.astype(BF16)
        basis_copy(slot).wait()
        sums = [jnp.zeros((G, 1), F32) for _ in range(4)]
        for t in range(4):
            lo, hi = 256 * t, 256 * (t + 1)
            product = jnp.dot(phis[slot, 0, :, :hi], mat[:hi, lo:hi], preferred_element_type=F32)
            if hi < KF:
                product += lax.dot_general(
                    phis[slot, 0, :, hi:],
                    mat[lo:hi, hi:],
                    (((1,), (1,)), ((), ())),
                    preferred_element_type=F32,
                )
            for k in range(4):
                sums[k] += jnp.sum(
                    phis[slot, k, :, lo:hi].astype(F32) * product, axis=1, keepdims=True
                )
        rho = sums[0]
        grads = [2.0 * x for x in sums[1:]]
        sigma = grads[0] * grads[0] + grads[1] * grads[1] + grads[2] * grads[2]
        quad = weights[slot]
        square = rho * rho + 1.0
        logs = jnp.log(square)
        cube = jnp.exp(logs * (1.0 / 3.0))
        scaled = cube * cube
        reduced = sigma / (scaled * scaled)
        denom = 1.0 + MU * reduced / KAPPA
        factor = 1.0 + MU * reduced / denom
        slope = MU / denom / denom
        point = -CX * scaled * factor
        by_rho = (-CX * 2.0) * rho / cube * ((2.0 / 3.0) * factor - (4.0 / 3.0) * slope * reduced)
        by_sigma = -CX * slope / scaled
        wr = 0.5 * quad * by_rho
        ws = 2.0 * quad * by_sigma
        total = total + jnp.sum(quad * point)
        coeffs = [wr] + [ws * x for x in grads]
        for t in range(4):
            lo, hi = 256 * t, 256 * (t + 1)
            mixed = coeffs[0] * phis[slot, 0, :, lo:hi].astype(F32)
            for k in range(1, 4):
                mixed += coeffs[k] * phis[slot, k, :, lo:hi].astype(F32)
            pair[:G, lo:hi] = mixed.astype(BF16)
        pair[G:, :] = phis[slot, 0]
        for t in range(4):
            lo, hi = 256 * t, 256 * (t + 1)
            left = jnp.concatenate([pair[G:, lo:hi], pair[:G, lo:hi]], axis=0)
            rows = lax.dot_general(
                left, pair[:, lo:], (((0,), (0,)), ((), ())), preferred_element_type=F32
            )
            for k in range(2):
                o1 = 2 * t + k
                for o2 in range(o1, KB):
                    c0 = o2 * BF - lo
                    block = rows[k * BF : (k + 1) * BF, c0 : c0 + BF]
                    if o2 == o1:
                        packed, line = pack_symmetric(block)
                        stage[slot, cls[o1] * (KB + 1)] = packed.astype(BF16)
                        lines[cls[o1]] = jnp.where(row == slot, line, lines[cls[o1]])
                    else:
                        stage[slot, cls[o1] * KB + cls[o2]] = block[:HB].astype(BF16)
                        stage[slot, cls[o2] * KB + cls[o1]] = block[HB:].astype(BF16)
        out_copy(slot).start()
        return total

    total = jnp.full((16, BF), lax.fori_loop(0, count, work, jnp.float32(0.0)), F32)
    first = total.astype(BF16).astype(F32)
    second = (total - first).astype(BF16).astype(F32)
    third = total - first - second
    spread = jnp.where(lane == 0, first, jnp.where(lane == 1, second, third))
    energy = jnp.where((row == 0) & (lane < 3), spread, 0.0)
    for peer in range(PEERS):
        if peer % (KB + 1) == 0:
            stage_ext[peer] = (lines[peer // (KB + 1)] + energy).astype(BF16)
        else:
            stage_ext[peer] = energy.astype(BF16)
    ext_out.start()

    def drain(slot, carry):
        out_copy(slot).wait()
        return carry

    lax.fori_loop(0, count, drain, 0)
    ext_out.wait()


def batches(scal, weights, basis, window):
    return pl.pallas_call(
        batch_kernel,
        out_shape=jax.ShapeDtypeStruct((PEERS, ROWS, BF), BF16),
        grid_spec=pltpu.PrefetchScalarGridSpec(
            num_scalar_prefetch=1,
            grid=(),
            in_specs=[VMEM, ANY, ANY],
            out_specs=HBM,
            scratch_shapes=[
                pltpu.VMEM((SLOTS, 4, G, KF), BF16),
                pltpu.VMEM((SLOTS, PEERS, HB, BF), BF16),
                pltpu.VMEM((PEERS, 16, BF), BF16),
                pltpu.VMEM((KF, KF), BF16),
                pltpu.VMEM((2 * G, KF), BF16),
                pltpu.VMEM((SLOTS, PEERS, HB, BF), BF16),
                pltpu.VMEM((PEERS, 16, BF), BF16),
                pltpu.VMEM((KB, 16, BF), F32),
                pltpu.SemaphoreType.DMA((SLOTS,)),
                pltpu.SemaphoreType.DMA((SLOTS,)),
                pltpu.SemaphoreType.DMA((SLOTS,)),
                pltpu.SemaphoreType.DMA((2,)),
            ],
        ),
        compiler_params=pltpu.CompilerParams(vmem_limit_bytes=40 * MIB),
        name="batches",
    )(scal, weights, basis, window)


def collect_kernel(scal, arrived, mine, other_out, acc, lines, energy):
    step = pl.program_id(0)
    row, lane = lanes((16, BF))
    on_diagonal = scal[PEERS * (SLOTS + 1)] == scal[PEERS * (SLOTS + 1) + 1]

    @pl.when(step == 0)
    def _():
        acc[...] = jnp.zeros(acc.shape, F32)
        lines[...] = jnp.zeros(lines.shape, F32)
        energy[...] = jnp.zeros(energy.shape, F32)

    def source(k, carry):
        peer = step * CHUNK + k
        ext = arrived[k, EXT:, :].astype(F32)
        energy[...] += jnp.where((row == 0) & (lane < 3), ext, 0.0)

        def one(slot, inner):
            other, turn, at = entry(scal, peer, slot)
            part = arrived[k, pl.ds(pl.multiple_of(slot * HB, HB), HB), :]
            acc[other, pl.ds(at, HB), :] += part.astype(F32)

            @pl.when(on_diagonal)
            def _():
                line = jnp.where((row == slot) & (lane >= HB), ext, 0.0)
                lines[other, pl.ds(turn, 1), :] += jnp.sum(line, axis=0, keepdims=True)

            return inner

        lax.fori_loop(0, scal[PEERS * SLOTS + peer], one, 0)
        return carry

    lax.fori_loop(0, CHUNK, source, 0)

    @pl.when(step == PEERS // CHUNK - 1)
    def _():
        total = jnp.sum(jnp.sum(energy[...], axis=0, keepdims=True), axis=1, keepdims=True)
        eight, _ = lanes((8, BF))
        mine[:BAND, :] = acc[0]
        other_out[:BAND, :] = acc[1]
        mine[BAND:, :] = jnp.where(eight == TURNS, total, lines[0])
        other_out[BAND:, :] = jnp.where(eight == TURNS, total, lines[1])


def collect(scal, arrived):
    shape = (BAND + 8, BF)
    return pl.pallas_call(
        collect_kernel,
        out_shape=[jax.ShapeDtypeStruct(shape, F32)] * 2,
        grid_spec=pltpu.PrefetchScalarGridSpec(
            num_scalar_prefetch=1,
            grid=(PEERS // CHUNK,),
            in_specs=[pl.BlockSpec((CHUNK, ROWS, BF), lambda s, _: (s, 0, 0))],
            out_specs=[pl.BlockSpec(shape, lambda s, _: (0, 0))] * 2,
            scratch_shapes=[
                pltpu.VMEM((2, BAND, BF), F32),
                pltpu.VMEM((2, 8, BF), F32),
                pltpu.VMEM((16, BF), F32),
            ],
        ),
        compiler_params=pltpu.CompilerParams(vmem_limit_bytes=16 * MIB),
        name="collect",
    )(scal, arrived)


def merge_kernel(mine, theirs, upper, lower, rest):
    upper[...] = mine[: TURNS * HB, :] + theirs[: TURNS * HB, :]
    lower[...] = mine[TURNS * HB : BAND, :] + theirs[TURNS * HB : BAND, :]
    rest[...] = mine[BAND:, :] + theirs[BAND:, :]


def merge(mine, theirs):
    half = jax.ShapeDtypeStruct((TURNS * HB, BF), F32)
    return pl.pallas_call(
        merge_kernel,
        out_shape=[half, half, jax.ShapeDtypeStruct((8, BF), F32)],
        in_specs=[VMEM, VMEM],
        out_specs=[VMEM, VMEM, VMEM],
        name="merge",
    )(mine, theirs)


def place_kernel(scal, upper, lower, rest, got_upper, got_lower, out):
    t = pl.program_id(0)
    row_id, shift = scal[0], scal[1]
    out[...] = jnp.zeros(out.shape, F32)
    at = (row_id + N_ROW * t + shift) // N_COL

    def part(ref, turn):
        return ref[pl.ds(pl.multiple_of(turn * HB, HB), HB), :]

    @pl.when((shift > 0) & (at < N_COL))
    def _():
        turn = t + jnp.where(row_id + shift >= N_ROW, 1, 0)
        out[0, at, :HB, :] = part(upper, t)
        out[0, at, HB:, :] = part(got_lower, jnp.minimum(turn, TURNS - 1))

    @pl.when((shift > 0) & (at > 0))
    def _():
        turn = t - jnp.where(row_id + shift < N_COL, 1, 0)
        both = jnp.concatenate([part(got_upper, jnp.maximum(turn, 0)), part(lower, t)], axis=0)
        out[0, at - 1] = both.T

    @pl.when(shift == 0)
    def _():
        out[0, at] = unpack_symmetric(part(upper, t), rest[pl.ds(t, 1), :])


def place(scal, upper, lower, rest, got_upper, got_lower):
    return pl.pallas_call(
        place_kernel,
        out_shape=jax.ShapeDtypeStruct((TURNS, N_COL, BF, BF), F32),
        grid_spec=pltpu.PrefetchScalarGridSpec(
            num_scalar_prefetch=1,
            grid=(TURNS,),
            in_specs=[VMEM] * 5,
            out_specs=pl.BlockSpec((1, N_COL, BF, BF), lambda t, _: (t, 0, 0, 0)),
        ),
        name="place",
    )(scal, upper, lower, rest, got_upper, got_lower)


def mirror_pairs():
    pairs = []
    for row in range(N_ROW):
        for col in range(N_COL):
            shift = (col - row) % N_COL
            pairs.append((row * N_COL + col, (row + shift) % N_ROW * N_COL + row % N_COL))
    return pairs


def shards(density, basis, weights, batch_start, batch_count):
    row_id = lax.axis_index(ROW).astype(jnp.int32)
    col_id = lax.axis_index(COL).astype(jnp.int32)
    half_id = lax.axis_index("h").astype(jnp.int32)
    self_index = row_id * N_COL + col_id
    where = jnp.stack([row_id, jnp.mod(col_id - row_id, N_COL)])
    half_starts = lax.dynamic_slice(batch_start, (half_id * PEERS * SLOTS,), (PEERS * SLOTS,))
    half_counts = lax.dynamic_slice(batch_count, (half_id * PEERS,), (PEERS,))
    ids = jnp.stack([jnp.mod(row_id, KB), col_id, half_id])
    plan = jnp.concatenate([half_starts, half_counts, ids])
    own_starts = lax.dynamic_slice(batch_start, (self_index * SLOTS,), (SLOTS,))
    own_count = lax.dynamic_slice(batch_count, (self_index,), (1,))
    scal = jnp.concatenate([own_starts, own_count])
    swap = [(0, 1), (1, 0)]

    held = share(where, density)
    packed = pack(plan, held, lax.ppermute(held, "h", swap))
    window = lax.all_to_all(packed, GROUP, split_axis=0, concat_axis=0, tiled=True)

    outgoing = batches(scal, weights.reshape(SLOTS, G, 1), basis, window)
    arrived = lax.all_to_all(outgoing, GROUP, split_axis=0, concat_axis=0, tiled=True)

    mine, other = collect(plan, arrived)
    upper, lower, rest = merge(mine, lax.ppermute(other, "h", swap))
    there = mirror_pairs()
    got_upper = lax.ppermute(upper, ALL, there)
    got_lower = lax.ppermute(lower, ALL, [(d, s) for s, d in there])
    potential = place(where, upper, lower, rest, got_upper, got_lower)
    return potential, rest[TURNS, 0] / (NBLK * BF)


def solution(mesh):
    fine = Mesh(np.asarray(mesh.devices).reshape(2, 2, 4, 4, 2), ALL)
    in_specs = (P(ROW, COL), P(ALL), P(ALL), P(), P())
    out_specs = (P(ROW, COL), P())
    return jax.shard_map(shards, mesh=fine, in_specs=in_specs, out_specs=out_specs, check_vma=False)
```

time: 266 us -> 177 us (0.67); the launches traced: 262 us -> 176 us
  waiting for transfers between devices: 155 us -> 56.9 us
  blocking collectives: 40.8 us -> 56.2 us
  between operations: 15.9 us -> 2.54 us
  starting transfers between devices: 16 us -> 25 us
  local copies, waits for them, and re-layouts: 7.45 us -> 11.8 us
    all_gather x1 -> x0, waiting for transfers between devices: 79 us -> none  [shards(): lax.all_gather(half_band(density, row_id, col_id), ALL, axis=0, tiled=True)]
    all_to_all x0 -> x1, blocking collectives: none -> 56.2 us  [shards(): lax.all_to_all(outgoing, GROUP, split_axis=0, concat_axis=0, tiled=True)]
    all_gather x1 -> x0, blocking collectives: 40.8 us -> none  [shards(): energies = lax.all_gather(energy, ALL, axis=0, tiled=True)]
    all_to_all x1, waiting for transfers between devices: 75.6 us -> 39 us  [shards(): lax.all_to_all(packed, GROUP, split_axis=0, concat_axis=0, tiled=True)]
    ppermute x1 -> x4, waiting for transfers between devices: 0.01 us -> 17.9 us  [the longest x1 7.46 us: shards(): upper, lower, rest = merge(mine, lax.ppermute(other, 'h', swap))]
    ppermute x1 -> x4, starting transfers between devices: 0.61 us -> 15.1 us  [the longest x1 5.47 us: shards(): got_lower = lax.ppermute(lower, ALL, [(d, s) for s, d in there])]
    all_to_all x1, starting transfers between devices: 15.3 us -> 9.96 us  [shards(): lax.all_to_all(packed, GROUP, split_axis=0, concat_axis=0, tiled=True)]
    unnamed x8 -> x18, local copies, waits for them, and re-layouts: 3.42 us -> 6.74 us
  transfers between devices with their start and end apart: 3 -> 5, of which waited for: 2 -> 4; matrix products, arithmetic and copies ran while one was open for 2% -> 3% of each run, Pallas kernels for 0% -> 0%
where the time goes in v2:
time: 177 us; the launch traced here: 176 us
  waiting for transfers between devices  56.9 us (32%)
  blocking collectives  56.2 us (32%)
  starting transfers between devices  25 us (14%)
  Pallas kernels  22.3 us (13%)
  local copies, waits for them, and re-layouts  11.8 us (7%)
  between operations  2.54 us (1%)
    all_to_all x1, blocking collectives, shards(): lax.all_to_all(outgoing, GROUP, split_axis=0, concat_axis=0, tiled=True)  56.2 us
    all_to_all x1, waiting for transfers between devices, shards(): lax.all_to_all(packed, GROUP, split_axis=0, concat_axis=0, tiled=True)  39 us
    all_to_all x1, starting transfers between devices, shards(): lax.all_to_all(packed, GROUP, split_axis=0, concat_axis=0, tiled=True)  9.96 us
    ppermute x1, waiting for transfers between devices, shards(): upper, lower, rest = merge(mine, lax.ppermute(other, 'h', swap))  7.46 us
    ppermute x1, waiting for transfers between devices, shards(): got_lower = lax.ppermute(lower, ALL, [(d, s) for s, d in there])  7.06 us
    unnamed x18, local copies, waits for them, and re-layouts  6.74 us
    ppermute x1, starting transfers between devices, shards(): got_lower = lax.ppermute(lower, ALL, [(d, s) for s, d in there])  5.47 us
    pallas_call x1, Pallas kernels, pack(): pl.pallas_call(pack_kernel, out_shape=jax.ShapeDtypeStruct((PEERS, ROWS,...  4.95 us
  transfers between devices with their start and end apart: 5, of which 4 were waited for; matrix products, arithmetic and copies ran while one was open for 3% of the time, Pallas kernels for 0%

profile of v2, /device:TPU:18, one launch (start us, length us, event | category | flops | bytes accessed | tf_op | source)
XLA Modules:
  0.0 176.1 jit_solution(8149654602930031684)
XLA Ops:
  0.7 0.7 pad_add_fusion.scal
  1.3 3.0 %share.1.mine = bf16[528,128]{1,0:T(8,128)(2,1)} custom-call(s32[2]{0:T(128)} %pad_add_fusion.scal, bf16[4,8,128,128]{3,2,1,0:T(8,128)(2,1)} %density.1), custom_call_target="tpu_custom_call" | custom-call | tf_op jit(solution)/shard_map/share/pallas_call | solution.py:99
  4.3 2.1 %collective-permute-start = (bf16[528,128]{1,0:T(8,128)(2,1)}, bf16[528,128]{1,0:T(8,128)(2,1)S(1)}, u32[]{:S(2)}, u32[]{:S(2)}) collective-permute-start(bf16[528,128]{1,0:T(8,128)(2,1)} %share.1.mine), channel_id=1, source_target_pairs={{0,64},{64,0},{1,65},{65,1},{2,66},{66,2},{3,67},{67,3},{4,68},{68... | collective-permute-start | bytes 405512 | tf_op jit(solution)/shard_map/ppermute | solution.py:481
  6.4 0.8 dynamic_slice.12
  7.2 0.7 dynamic_slice.13
  7.9 0.1 concatenate.6.scal
  8.0 3.3 %collective-permute-done.theirs = bf16[528,128]{1,0:T(8,128)(2,1)S(1)} collective-permute-done((bf16[528,128]{1,0:T(8,128)(2,1)}, bf16[528,128]{1,0:T(8,128)(2,1)S(1)}, u32[]{:S(2)}, u32[]{:S(2)}) %collective-permute-start) | collective-permute-done | bytes 135200 | tf_op jit(solution)/shard_map/ppermute | solution.py:481
  11.3 0.0 copy-start.2
  11.3 0.9 copy-done.2
  12.2 5.0 %pack.1 = bf16[64,208,128]{2,1,0:T(8,128)(2,1)} custom-call(s32[259]{0:T(512)S(1)} %concatenate.6.scal, bf16[528,128]{1,0:T(8,128)(2,1)S(1)} %copy-done.2, bf16[528,128]{1,0:T(8,128)(2,1)S(1)} %collective-permute-done.theirs), custom_call_target="tpu_custom_call" | custom-call | tf_op jit(solution)/shard_map/pack/pallas_call | solution.py:152
  17.2 0.0 copy-start.8
  17.2 0.0 copy-start.7
  17.2 10.0 %all-to-all-start = ((bf16[64,208,128]{2,1,0:T(8,128)(2,1)}), bf16[64,208,128]{2,1,0:T(8,128)(2,1)S(1)}, u32[]{:S(2)}, u32[]{:S(2)}) async-start(bf16[64,208,128]{2,1,0:T(8,128)(2,1)} %pack.1), calls=%async_computation | async-start | bytes 6815744 | tf_op jit(solution)/shard_map/all_to_all | solution.py:482
  27.2 0.8 dynamic_slice.14
  27.9 0.0 copy-done.8
  27.9 0.6 dynamic_slice.15
  28.5 0.0 copy-done.7
  28.5 0.9 copy.7.weights
  29.5 0.7 pad_add_fusion.1.scal
  30.2 39.0 %all-to-all-done.window = bf16[64,208,128]{2,1,0:T(8,128)(2,1)S(1)} async-done(((bf16[64,208,128]{2,1,0:T(8,128)(2,1)}), bf16[64,208,128]{2,1,0:T(8,128)(2,1)S(1)}, u32[]{:S(2)}, u32[]{:S(2)}) %all-to-all-start) | async-done | bytes 3407904 | tf_op jit(solution)/shard_map/all_to_all | solution.py:482
  69.2 0.0 copy-start
  69.2 2.8 %copy-done = bf16[3,4,256,1024]{3,2,1,0:T(8,128)(2,1)S(1)} copy-done((bf16[3,4,256,1024]{3,2,1,0:T(8,128)(2,1)S(1)}, bf16[3,4,256,1024]{3,2,1,0:T(8,128)(2,1)}, u32[]{:S(2)}) %copy-start) | copy-done | bytes 6291480
  72.0 0.0 copy-start.1
  72.0 1.0 copy-done.1
  73.0 4.0 %batches.1 = bf16[64,208,128]{2,1,0:T(8,128)(2,1)S(1)} custom-call(s32[4]{0:T(128)S(1)} %pad_add_fusion.1.scal, f32[3,256,1]{2,1,0:T(8,128)S(1)} %copy-done.1, bf16[3,4,256,1024]{3,2,1,0:T(8,128)(2,1)S(1)} %copy-done, bf16[64,208,128]{2,1,0:T(8,128)(2,1)S(1)} %all-to-all-done.window), custom_call_target="tpu_custom_call" | custom-call | tf_op jit(solution)/shard_map/batches/pallas_call | solution.py:307
  77.0 56.2 %all_to_all.10.arrived = bf16[64,208,128]{2,1,0:T(8,128)(2,1)S(1)} all-to-all(bf16[64,208,128]{2,1,0:T(8,128)(2,1)S(1)} %batches.1), channel_id=1, replica_groups=mesh['h'=2,'xl'=2,'y'=4,'z'=4,'c'=2] {'xl','y','z','c'}, dimensions={0} | all-to-all | bytes 6815744 | tf_op jit(solution)/shard_map/all_to_all | solution.py:485
  133.2 4.8 %collect.1 = (f32[520,128]{1,0:T(8,128)S(1)}, f32[520,128]{1,0:T(8,128)S(1)}) custom-call(s32[259]{0:T(512)S(1)} %concatenate.6.scal, bf16[64,208,128]{2,1,0:T(8,128)(2,1)S(1)} %all_to_all.10.arrived), custom_call_target="tpu_custom_call" | custom-call | tf_op jit(solution)/shard_map/collect/pallas_call | solution.py:380
  138.0 0.0 copy-start.3
  138.0 0.7 copy-done.3
  138.7 2.6 %collective-permute-start.1 = (f32[520,128]{1,0:T(8,128)S(1)}, f32[520,128]{1,0:T(8,128)S(1)}, u32[]{:S(2)}, u32[]{:S(2)}) collective-permute-start(f32[520,128]{1,0:T(8,128)S(1)} %get-tuple-element.8), channel_id=1, source_target_pairs={{0,64},{64,0},{1,65},{65,1},{2,66},{66,2},{3,67},{67,3},{4,68},{68... | collective-permute-start | bytes 798728 | tf_op jit(solution)/shard_map/ppermute | solution.py:488
  141.3 7.5 %collective-permute-done.1.theirs = f32[520,128]{1,0:T(8,128)S(1)} collective-permute-done((f32[520,128]{1,0:T(8,128)S(1)}, f32[520,128]{1,0:T(8,128)S(1)}, u32[]{:S(2)}, u32[]{:S(2)}) %collective-permute-start.1) | collective-permute-done | bytes 266272 | tf_op jit(solution)/shard_map/ppermute | solution.py:488
  148.8 0.0 copy-start.4
  148.8 0.7 copy-done.4
  149.4 1.7 merge.1
  151.2 4.9 %collective-permute-start.2 = (f32[256,128]{1,0:T(8,128)}, f32[256,128]{1,0:T(8,128)S(1)}, u32[]{:S(2)}, u32[]{:S(2)}) collective-permute-start(f32[256,128]{1,0:T(8,128)} %get-tuple-element.9.upper), channel_id=1, source_target_pairs={{0,0},{1,8},{2,16},{3,24},{4,32},{5,40},{6,48},{7,56},{8,65},{9,9}... | collective-permute-start | bytes 393224 | tf_op jit(solution)/shard_map/ppermute | solution.py:490
  156.1 5.5 %collective-permute-start.3 = (f32[256,128]{1,0:T(8,128)}, f32[256,128]{1,0:T(8,128)S(1)}, u32[]{:S(2)}, u32[]{:S(2)}) collective-permute-start(f32[256,128]{1,0:T(8,128)} %get-tuple-element.10.lower), channel_id=1, source_target_pairs={{0,0},{8,1},{16,2},{24,3},{32,4},{40,5},{48,6},{56,7},{65,8},{9,9}... | collective-permute-start | bytes 393224 | tf_op jit(solution)/shard_map/ppermute | solution.py:491
  161.6 1.2 slice.3
  163.4 0.0 collective-permute-done.2.got_upper
  163.4 0.0 copy-start.5
  163.4 7.1 %collective-permute-done.3.got_lower = f32[256,128]{1,0:T(8,128)S(1)} collective-permute-done((f32[256,128]{1,0:T(8,128)}, f32[256,128]{1,0:T(8,128)S(1)}, u32[]{:S(2)}, u32[]{:S(2)}) %collective-permute-start.3) | collective-permute-done | bytes 131104 | tf_op jit(solution)/shard_map/ppermute | solution.py:491
  170.5 0.0 copy-done.5
  170.5 0.0 copy-start.6
  170.5 0.6 copy-done.6
  171.1 3.8 %place.1 = f32[4,8,128,128]{3,2,1,0:T(8,128)} custom-call(s32[2]{0:T(128)} %pad_add_fusion.scal, f32[256,128]{1,0:T(8,128)} %get-tuple-element.9.upper, f32[256,128]{1,0:T(8,128)} %get-tuple-element.10.lower, f32[8,128]{1,0:T(8,128)} %get-tuple-element.11.rest, f32[256,128]{1,0:T(8,128)} %copy-done.5, f32[256,128]{1,0:T(8,128)} %copy-done.6), custom_call_target="tpu_custom_call" | custom-call | tf_op jit(solution)/shard_map/place/pallas_call | solution.py:443
Async XLA Ops:
  4.3 7.0 %collective-permute-start = (bf16[528,128]{1,0:T(8,128)(2,1)}, bf16[528,128]{1,0:T(8,128)(2,1)S(1)}, u32[]{:S(2)}, u32[]{:S(2)}) collective-permute-start(bf16[528,128]{1,0:T(8,128)(2,1)} %share.1.mine), channel_id=1, source_target_pairs={{0,64},{64,0},{1,65},{65,1},{2,66},{66,2},{3,67},{67,3},{4,68},{68... | collective-permute-start | bytes 405512 | tf_op jit(solution)/shard_map/ppermute | solution.py:481
  11.3 0.9 copy-start.2
  17.2 10.8 %copy-start.8 = (s32[128]{0:T(128)S(1)}, s32[128]{0:T(128)}, u32[]{:S(2)}) copy-start(s32[128]{0:T(128)} %param.9) | copy-start | bytes 1540
  17.2 11.3 %copy-start.7 = (f32[3,256]{1,0:T(4,128)S(1)}, f32[3,256]{1,0:T(4,128)}, u32[]{:S(2)}) copy-start(f32[3,256]{1,0:T(4,128)} %param.7) | copy-start | bytes 9220
  17.2 52.0 %all-to-all-start = ((bf16[64,208,128]{2,1,0:T(8,128)(2,1)}), bf16[64,208,128]{2,1,0:T(8,128)(2,1)S(1)}, u32[]{:S(2)}, u32[]{:S(2)}) async-start(bf16[64,208,128]{2,1,0:T(8,128)(2,1)} %pack.1), calls=%async_computation | async-start | bytes 6815744 | tf_op jit(solution)/shard_map/all_to_all | solution.py:482
  69.2 2.8 %copy-start = (bf16[3,4,256,1024]{3,2,1,0:T(8,128)(2,1)S(1)}, bf16[3,4,256,1024]{3,2,1,0:T(8,128)(2,1)}, u32[]{:S(2)}) copy-start(bf16[3,4,256,1024]{3,2,1,0:T(8,128)(2,1)} %basis.1) | copy-start | bytes 18874372
  72.0 1.0 copy-start.1
  138.0 0.7 copy-start.3
  138.7 10.1 %collective-permute-start.1 = (f32[520,128]{1,0:T(8,128)S(1)}, f32[520,128]{1,0:T(8,128)S(1)}, u32[]{:S(2)}, u32[]{:S(2)}) collective-permute-start(f32[520,128]{1,0:T(8,128)S(1)} %get-tuple-element.8), channel_id=1, source_target_pairs={{0,64},{64,0},{1,65},{65,1},{2,66},{66,2},{3,67},{67,3},{4,68},{68... | collective-permute-start | bytes 798728 | tf_op jit(solution)/shard_map/ppermute | solution.py:488
  148.8 0.7 copy-start.4
  151.2 12.2 %collective-permute-start.2 = (f32[256,128]{1,0:T(8,128)}, f32[256,128]{1,0:T(8,128)S(1)}, u32[]{:S(2)}, u32[]{:S(2)}) collective-permute-start(f32[256,128]{1,0:T(8,128)} %get-tuple-element.9.upper), channel_id=1, source_target_pairs={{0,0},{1,8},{2,16},{3,24},{4,32},{5,40},{6,48},{7,56},{8,65},{9,9}... | collective-permute-start | bytes 393224 | tf_op jit(solution)/shard_map/ppermute | solution.py:490
  156.1 14.4 %collective-permute-start.3 = (f32[256,128]{1,0:T(8,128)}, f32[256,128]{1,0:T(8,128)S(1)}, u32[]{:S(2)}, u32[]{:S(2)}) collective-permute-start(f32[256,128]{1,0:T(8,128)} %get-tuple-element.10.lower), channel_id=1, source_target_pairs={{0,0},{8,1},{16,2},{24,3},{32,4},{40,5},{48,6},{56,7},{65,8},{9,9}... | collective-permute-start | bytes 393224 | tf_op jit(solution)/shard_map/ppermute | solution.py:491
  163.4 7.1 %copy-start.5 = (f32[256,128]{1,0:T(8,128)}, f32[256,128]{1,0:T(8,128)S(1)}, u32[]{:S(2)}) copy-start(f32[256,128]{1,0:T(8,128)S(1)} %collective-permute-done.2.got_upper) | copy-start | bytes 393220
  170.5 0.6 copy-start.6

commit v3 on v2

v3 whole, which is shorter than its diff:
```python
import functools

import jax
import jax.numpy as jnp
import numpy as np
from jax import lax
from jax.experimental import pallas as pl
from jax.experimental.pallas import tpu as pltpu
from jax.sharding import Mesh, PartitionSpec as P

CX = 0.7385587663820224
MU = 0.2195149727645171
KAPPA = 0.804
BF = 128
KB = 8
NBLK = 64
G = 256
SLOTS = 3
KF = 1024
N_ROW = 16
N_COL = 8
TURNS = NBLK // N_ROW
PEERS = 64
MIB = 1024 * 1024
HB = BF // 2
EXT = SLOTS * HB
ROWS = EXT + 16
BAND = 2 * TURNS * HB
ROW = ("h", "xl", "y")
COL = ("z", "c")
ALL = ROW + COL
GROUP = ("xl", "y", "z", "c")
VMEM = pl.BlockSpec(memory_space=pltpu.VMEM)
HBM = pl.BlockSpec(memory_space=pltpu.HBM)
F32 = jnp.float32
BF16 = jnp.bfloat16


def lanes(shape):
    return lax.broadcasted_iota(jnp.int32, shape, 0), lax.broadcasted_iota(jnp.int32, shape, 1)


def pack_symmetric(full):
    r, c = lanes((HB, BF))
    top, bottom = full[:HB], full[HB:]
    packed = jnp.where((c >= HB) | (r <= c), top, pltpu.roll(bottom, HB, 1))
    row = jnp.sum(jnp.where(c - HB == r, bottom, 0.0), axis=0, keepdims=True)
    return packed, row


def unpack_symmetric(packed, row):
    r, c = lanes((HB, BF))
    flip = jnp.concatenate([packed, packed], axis=0).T
    top = jnp.where((c >= HB) | (r <= c), packed, flip[:HB])
    corner = jnp.where(c - HB < r, pltpu.roll(packed, HB, 1), flip[:HB])
    corner = jnp.where(c - HB == r, row, corner)
    return jnp.concatenate([top, jnp.where(c < HB, flip[HB:], corner)], axis=0)


def pick_row(rows, index):
    r, _ = lanes(rows.shape)
    return jnp.sum(jnp.where(r == index, rows, 0.0), axis=0, keepdims=True)


def position():
    h = lax.axis_index("h")
    row_id = (h * 2 + lax.axis_index("xl")) * 4 + lax.axis_index("y")
    return row_id, lax.axis_index("z") * 2 + lax.axis_index("c"), h


def entry(starts, peer, slot, where):
    row_id, col_id, h = where
    start = starts[(h * PEERS + peer) * SLOTS + slot]
    i = start + ((row_id - start) & (KB - 1))
    j = start + ((col_id - start) & (KB - 1))
    other = ((i >> 3) & 1) ^ h
    turn = i >> 4
    below = jnp.where(j < i, TURNS, 0)
    return other, turn, pl.multiple_of((below + turn) * HB, HB)


def scalars(count, in_specs, out_specs, scratch_shapes=()):
    return pltpu.PrefetchScalarGridSpec(
        num_scalar_prefetch=count,
        grid=(),
        in_specs=in_specs,
        out_specs=out_specs,
        scratch_shapes=list(scratch_shapes),
    )


def limit(mib):
    return pltpu.CompilerParams(vmem_limit_bytes=mib * MIB)


def share_kernel(density, out, copy, ups, lows, sems):
    row_id, col_id, _ = position()
    shift = (col_id - row_id) & (N_COL - 1)
    row, _ = lanes((16, BF))
    loads = []
    for t in range(TURNS):
        at = (row_id + N_ROW * t + shift) >> 3
        up = density.at[t, jnp.minimum(at, N_COL - 1)]
        low = density.at[t, jnp.maximum(at - 1, 0)]
        loads.append(pltpu.make_async_copy(up, ups.at[t], sems.at[t]))
        loads.append(pltpu.make_async_copy(low, lows.at[t], sems.at[TURNS + t]))
    for load in loads:
        load.start()
    for load in loads:
        load.wait()

    @pl.when(shift > 0)
    def _():
        for t in range(TURNS):
            low = TURNS * HB + t * HB
            out[t * HB : (t + 1) * HB, :] = ups[t, :HB, :]
            out[low : low + HB, :] = lows[t].astype(F32).T[HB:].astype(BF16)
        out[BAND:, :] = jnp.zeros((16, BF), BF16)

    @pl.when(shift == 0)
    def _():
        ext = jnp.zeros((16, BF), F32)
        for t in range(TURNS):
            packed, line = pack_symmetric(ups[t].astype(F32))
            out[t * HB : (t + 1) * HB, :] = packed.astype(BF16)
            ext = jnp.where(row == t, line, ext)
        out[TURNS * HB : BAND, :] = jnp.zeros((TURNS * HB, BF), BF16)
        out[BAND:, :] = ext.astype(BF16)

    copy[...] = out[...]


def share(density):
    held = jax.ShapeDtypeStruct((BAND + 16, BF), BF16)
    return pl.pallas_call(
        share_kernel,
        out_shape=[held, held],
        in_specs=[HBM],
        out_specs=[VMEM, VMEM],
        scratch_shapes=[
            pltpu.VMEM((TURNS, BF, BF), BF16),
            pltpu.VMEM((TURNS, BF, BF), BF16),
            pltpu.SemaphoreType.DMA((2 * TURNS,)),
        ],
        compiler_params=limit(4),
        name="share",
    )(density)


CHUNK = 8


def pack_kernel(starts, counts, mine, theirs, out, table, lines, buf, sems):
    where = position()
    on_diagonal = ((where[1] - where[0]) & (KB - 1)) == 0
    table[0] = mine[:BAND, :]
    table[1] = theirs[:BAND, :]
    lines[0] = mine[BAND:, :].astype(F32)
    lines[1] = theirs[BAND:, :].astype(F32)
    row, _ = lanes((16, BF))

    def send(chunk):
        span = pl.ds(pl.multiple_of(chunk * CHUNK, CHUNK), CHUNK)
        return pltpu.make_async_copy(buf.at[span], out.at[span], sems.at[chunk])

    def one_chunk(chunk, carry):
        for k in range(CHUNK):
            peer = chunk * CHUNK + k
            count = counts[where[2] * PEERS + peer]

            def one(slot):
                other, _, at = entry(starts, peer, slot, where)
                buf[peer, slot * HB : (slot + 1) * HB, :] = table[other, pl.ds(at, HB), :]

            one(0)
            for slot in range(1, SLOTS):
                pl.when(slot < count)(lambda slot=slot: one(slot))

            @pl.when(on_diagonal)
            def _():
                ext = jnp.zeros((16, BF), F32)
                for slot in range(SLOTS):
                    other, turn, _ = entry(starts, peer, slot, where)
                    ext = jnp.where(row == slot, lines[other, pl.ds(turn, 1), :], ext)
                buf[peer, EXT:, :] = ext.astype(BF16)

        send(chunk).start()
        return carry

    lax.fori_loop(0, PEERS // CHUNK, one_chunk, 0)

    def drain(chunk, carry):
        send(chunk).wait()
        return carry

    lax.fori_loop(0, PEERS // CHUNK, drain, 0)


def pack(starts, counts, mine, theirs):
    return pl.pallas_call(
        pack_kernel,
        out_shape=jax.ShapeDtypeStruct((PEERS, ROWS, BF), BF16),
        grid_spec=scalars(
            2,
            [VMEM, VMEM],
            HBM,
            [
                pltpu.VMEM((2, BAND, BF), BF16),
                pltpu.VMEM((2, 16, BF), F32),
                pltpu.VMEM((PEERS, ROWS, BF), BF16),
                pltpu.SemaphoreType.DMA((PEERS // CHUNK,)),
            ],
        ),
        compiler_params=limit(8),
        name="pack",
    )(starts, counts, mine, theirs)


def batch_kernel(
    starts, counts, weights, basis, window, out, quads, phis, mat, pair, lines, sem_w, sem_b
):
    row_id, col_id, _ = position()
    me = row_id * N_COL + col_id
    count = counts[me]
    row, lane = lanes((16, BF))
    weights_copy = pltpu.make_async_copy(weights, quads, sem_w)

    def basis_copy(slot):
        return pltpu.make_async_copy(basis.at[slot], phis.at[slot], sem_b.at[slot])

    def fetch(slot, carry):
        basis_copy(slot).start()
        return carry

    weights_copy.start()
    lax.fori_loop(0, count, fetch, 0)
    lines[...] = jnp.zeros(lines.shape, F32)
    weights_copy.wait()

    def work(slot, total):
        start = starts[me * SLOTS + slot]
        cls = [(start + o) & (KB - 1) for o in range(KB)]
        span = pl.ds(pl.multiple_of(slot * HB, HB), HB)
        for o1 in range(KB):
            r1 = o1 * BF
            for o2 in range(o1 + 1, KB):
                top = window[cls[o1] * KB + cls[o2], span, :]
                bottom = window[cls[o2] * KB + cls[o1], span, :]
                mat[r1 : r1 + HB, o2 * BF : (o2 + 1) * BF] = top
                mat[r1 + HB : r1 + BF, o2 * BF : (o2 + 1) * BF] = bottom
                if o2 == o1 + 1 and o1 % 2 == 0:
                    mat[o2 * BF : (o2 + 1) * BF, r1 : r1 + BF] = jnp.concatenate(
                        [top, bottom], axis=0
                    ).T
            diagonal = cls[o1] * (KB + 1)
            line = pick_row(window[diagonal, EXT:, :].astype(F32), slot)
            block = unpack_symmetric(window[diagonal, span, :].astype(F32), line)
            mat[r1 : r1 + BF, r1 : r1 + BF] = block.astype(BF16)
        basis_copy(slot).wait()
        sums = [jnp.zeros((G, 1), F32) for _ in range(4)]
        for t in range(4):
            lo, hi = 256 * t, 256 * (t + 1)
            product = jnp.dot(phis[slot, 0, :, :hi], mat[:hi, lo:hi], preferred_element_type=F32)
            if hi < KF:
                product += lax.dot_general(
                    phis[slot, 0, :, hi:],
                    mat[lo:hi, hi:],
                    (((1,), (1,)), ((), ())),
                    preferred_element_type=F32,
                )
            for k in range(4):
                sums[k] += jnp.sum(
                    phis[slot, k, :, lo:hi].astype(F32) * product, axis=1, keepdims=True
                )
        rho = sums[0]
        grads = [2.0 * x for x in sums[1:]]
        sigma = grads[0] * grads[0] + grads[1] * grads[1] + grads[2] * grads[2]
        quad = quads[slot]
        square = rho * rho + 1.0
        logs = jnp.log(square)
        cube = jnp.exp(logs * (1.0 / 3.0))
        scaled = cube * cube
        reduced = sigma / (scaled * scaled)
        denom = 1.0 + MU * reduced / KAPPA
        factor = 1.0 + MU * reduced / denom
        slope = MU / denom / denom
        point = -CX * scaled * factor
        by_rho = (-CX * 2.0) * rho / cube * ((2.0 / 3.0) * factor - (4.0 / 3.0) * slope * reduced)
        by_sigma = -CX * slope / scaled
        wr = 0.5 * quad * by_rho
        ws = 2.0 * quad * by_sigma
        total = total + jnp.sum(quad * point)
        coeffs = [wr] + [ws * x for x in grads]
        for t in range(4):
            lo, hi = 256 * t, 256 * (t + 1)
            mixed = coeffs[0] * phis[slot, 0, :, lo:hi].astype(F32)
            for k in range(1, 4):
                mixed += coeffs[k] * phis[slot, k, :, lo:hi].astype(F32)
            pair[:G, lo:hi] = mixed.astype(BF16)
        pair[G:, :] = phis[slot, 0]
        for t in range(4):
            lo, hi = 256 * t, 256 * (t + 1)
            left = jnp.concatenate([pair[G:, lo:hi], pair[:G, lo:hi]], axis=0)
            rows = lax.dot_general(
                left, pair[:, lo:], (((0,), (0,)), ((), ())), preferred_element_type=F32
            )
            for k in range(2):
                o1 = 2 * t + k
                for o2 in range(o1, KB):
                    c0 = o2 * BF - lo
                    block = rows[k * BF : (k + 1) * BF, c0 : c0 + BF]
                    if o2 == o1:
                        packed, line = pack_symmetric(block)
                        out[cls[o1] * (KB + 1), span, :] = packed.astype(BF16)
                        lines[cls[o1]] = jnp.where(row == slot, line, lines[cls[o1]])
                    else:
                        out[cls[o1] * KB + cls[o2], span, :] = block[:HB].astype(BF16)
                        out[cls[o2] * KB + cls[o1], span, :] = block[HB:].astype(BF16)
        return total

    total = jnp.full((16, BF), lax.fori_loop(0, count, work, jnp.float32(0.0)), F32)
    first = total.astype(BF16).astype(F32)
    second = (total - first).astype(BF16).astype(F32)
    third = total - first - second
    spread = jnp.where(lane == 0, first, jnp.where(lane == 1, second, third))
    energy = jnp.where((row == 0) & (lane < 3), spread, 0.0)
    for peer in range(PEERS):
        if peer % (KB + 1) == 0:
            out[peer, EXT:, :] = (lines[peer // (KB + 1)] + energy).astype(BF16)
        else:
            out[peer, EXT:, :] = energy.astype(BF16)


def batches(starts, counts, weights, basis, window):
    return pl.pallas_call(
        batch_kernel,
        out_shape=jax.ShapeDtypeStruct((PEERS, ROWS, BF), BF16),
        grid_spec=scalars(
            2,
            [HBM, HBM, VMEM],
            VMEM,
            [
                pltpu.VMEM((SLOTS, G, 1), F32),
                pltpu.VMEM((SLOTS, 4, G, KF), BF16),
                pltpu.VMEM((KF, KF), BF16),
                pltpu.VMEM((2 * G, KF), BF16),
                pltpu.VMEM((KB, 16, BF), F32),
                pltpu.SemaphoreType.DMA,
                pltpu.SemaphoreType.DMA((SLOTS,)),
            ],
        ),
        compiler_params=limit(32),
        name="batches",
    )(starts, counts, weights, basis, window)


def collect_kernel(which, starts, counts, arrived, out, energy):
    where = position()
    on_diagonal = ((where[1] - where[0]) & (KB - 1)) == 0
    row, lane = lanes((16, BF))
    eight, _ = lanes((8, BF))
    out[...] = jnp.zeros(out.shape, F32)
    energy[...] = jnp.zeros(energy.shape, F32)

    def one_chunk(chunk, carry):
        for k in range(CHUNK):
            peer = chunk * CHUNK + k
            count = counts[where[2] * PEERS + peer]
            if which:
                energy[...] += arrived[peer, EXT:, :].astype(F32)

            def one(slot, live):
                other, turn, at = entry(starts, peer, slot, where)
                wanted = other == which

                @pl.when(wanted if live is None else wanted & live)
                def _():
                    part = arrived[peer, slot * HB : (slot + 1) * HB, :]
                    out[pl.ds(at, HB), :] += part.astype(F32)

                    @pl.when(on_diagonal)
                    def _():
                        ext = arrived[peer, EXT:, :].astype(F32)
                        line = jnp.where((row == slot) & (lane >= HB), ext, 0.0)
                        line = jnp.sum(line, axis=0, keepdims=True)
                        out[BAND:, :] += jnp.where(eight == turn, line, 0.0)

            one(0, None)
            for slot in range(1, SLOTS):
                one(slot, slot < count)
        return carry

    lax.fori_loop(0, PEERS // CHUNK, one_chunk, 0)
    if which:
        total = jnp.where((row == 0) & (lane < 3), energy[...], 0.0)
        total = jnp.sum(jnp.sum(total, axis=0, keepdims=True), axis=1, keepdims=True)
        out[BAND:, :] = jnp.where(eight == TURNS, total, out[BAND:, :])


def collect(which, starts, counts, arrived):
    return pl.pallas_call(
        functools.partial(collect_kernel, which),
        out_shape=jax.ShapeDtypeStruct((BAND + 8, BF), F32),
        grid_spec=scalars(2, [VMEM], VMEM, [pltpu.VMEM((16, BF), F32)]),
        compiler_params=limit(8),
        cost_estimate=pl.CostEstimate(flops=10**6, bytes_accessed=4 * MIB, transcendentals=0),
        name=("collect_own", "collect_other")[which],
    )(starts, counts, arrived)


def merge_kernel(mine, sent, theirs, upper, lower, rest):
    eight, _ = lanes((8, BF))
    upper[...] = mine[: TURNS * HB, :] + theirs[: TURNS * HB, :]
    lower[...] = mine[TURNS * HB : BAND, :] + theirs[TURNS * HB : BAND, :]
    half = jnp.where(eight == TURNS, sent[BAND:, :], mine[BAND:, :])
    rest[...] = half + theirs[BAND:, :]


def merge(mine, sent, theirs):
    half = jax.ShapeDtypeStruct((TURNS * HB, BF), F32)
    return pl.pallas_call(
        merge_kernel,
        out_shape=[half, half, jax.ShapeDtypeStruct((8, BF), F32)],
        in_specs=[VMEM] * 3,
        out_specs=[VMEM] * 3,
        compiler_params=limit(4),
        name="merge",
    )(mine, sent, theirs)


def place_kernel(upper, lower, rest, got_upper, got_lower, blank, out, blocks, sems):
    del blank
    row_id, col_id, _ = position()
    shift = (col_id - row_id) & (N_COL - 1)

    def part(ref, turn):
        return ref[pl.ds(pl.multiple_of(turn * HB, HB), HB), :]

    def write(t, low, at):
        slot = TURNS * low + t
        return pltpu.make_async_copy(blocks.at[slot], out.at[t, at], sems.at[slot])

    for finish in (False, True):
        for t in range(TURNS):
            at = (row_id + N_ROW * t + shift) >> 3

            @pl.when((shift > 0) & (at < N_COL))
            def _():
                if finish:
                    write(t, 0, at).wait()
                else:
                    turn = t + jnp.where(row_id + shift >= N_ROW, 1, 0)
                    blocks[t, :HB, :] = part(upper, t)
                    blocks[t, HB:, :] = part(got_lower, jnp.minimum(turn, TURNS - 1))
                    write(t, 0, at).start()

            @pl.when((shift > 0) & (at > 0))
            def _():
                if finish:
                    write(t, 1, at - 1).wait()
                else:
                    turn = t - jnp.where(row_id + shift < N_COL, 1, 0)
                    top = part(got_upper, jnp.maximum(turn, 0))
                    blocks[TURNS + t] = jnp.concatenate([top, part(lower, t)], axis=0).T
                    write(t, 1, at - 1).start()

            @pl.when(shift == 0)
            def _():
                if finish:
                    write(t, 0, at).wait()
                else:
                    blocks[t] = unpack_symmetric(part(upper, t), rest[t : t + 1, :])
                    write(t, 0, at).start()


def place(upper, lower, rest, got_upper, got_lower, blank):
    return pl.pallas_call(
        place_kernel,
        out_shape=jax.ShapeDtypeStruct((TURNS, N_COL, BF, BF), F32),
        in_specs=[VMEM] * 5 + [HBM],
        out_specs=HBM,
        scratch_shapes=[
            pltpu.VMEM((2 * TURNS, BF, BF), F32),
            pltpu.SemaphoreType.DMA((2 * TURNS,)),
        ],
        input_output_aliases={5: 0},
        compiler_params=limit(4),
        name="place",
    )(upper, lower, rest, got_upper, got_lower, blank)


def mirror_pairs():
    pairs = []
    for row in range(N_ROW):
        for col in range(N_COL):
            shift = (col - row) % N_COL
            pairs.append((row * N_COL + col, (row + shift) % N_ROW * N_COL + row % N_COL))
    return pairs


def shards(density, basis, weights, batch_start, batch_count):
    swap = [(0, 1), (1, 0)]
    there = mirror_pairs()
    held, sent = share(density)
    theirs = lax.ppermute(sent, "h", swap)
    packed = pack(batch_start, batch_count, held, theirs)
    window = lax.all_to_all(packed, GROUP, split_axis=0, concat_axis=0, tiled=True)

    outgoing = batches(batch_start, batch_count, weights.reshape(SLOTS, G, 1), basis, window)
    arrived = lax.all_to_all(outgoing, GROUP, split_axis=0, concat_axis=0, tiled=True)

    other = collect(1, batch_start, batch_count, arrived)
    theirs = lax.ppermute(other, "h", swap)
    mine = collect(0, batch_start, batch_count, arrived)
    upper, lower, rest = merge(mine, other, theirs)
    got_upper = lax.ppermute(upper, ALL, there)
    got_lower = lax.ppermute(lower, ALL, [(d, s) for s, d in there])
    blank = jnp.zeros(density.shape, F32)
    potential = place(upper, lower, rest, got_upper, got_lower, blank)
    return potential, rest[TURNS, 0] / (NBLK * BF)


def solution(mesh):
    fine = Mesh(np.asarray(mesh.devices).reshape(2, 2, 4, 4, 2), ALL)
    in_specs = (P(ROW, COL), P(ALL), P(ALL), P(), P())
    out_specs = (P(ROW, COL), P())
    return jax.shard_map(shards, mesh=fine, in_specs=in_specs, out_specs=out_specs, check_vma=False)
```

time: 177 us -> 167 us (0.944)
  Pallas kernels: 22.3 us -> 15.7 us
  local copies, waits for them, and re-layouts: 11.8 us -> 9.37 us
    dynamic_slice x4 -> x0, local copies, waits for them, and re-layouts: 2.82 us -> none  [the longest x1 0.76 us: shards(): own_starts = lax.dynamic_slice(batch_start, (self_index * SLOTS,), (SLOTS,))]
    pallas_call x1, Pallas kernels: 3.84 us -> 1.13 us  [place(): pl.pallas_call(place_kernel, out_shape=jax.ShapeDtypeStruct((TURNS, N_COL...]
    all_to_all x1, waiting for transfers between devices: 39 us -> 41.1 us  [shards(): lax.all_to_all(packed, GROUP, split_axis=0, concat_axis=0, tiled=True)]
    pallas_call x1, Pallas kernels: 4.95 us -> 3.16 us  [pack(): pl.pallas_call(pack_kernel, out_shape=jax.ShapeDtypeStruct((PEERS, ROWS,...]
    unnamed x18 -> x16, local copies, waits for them, and re-layouts: 6.74 us -> 6.35 us
    pallas_call x2 -> x3, Pallas kernels: 7.73 us -> 7.49 us  [the longest x2 6.98 us: collect(): pl.pallas_call(functools.partial(collect_kernel, which), out_shape=jax.Sh...]
  transfers between devices with their start and end apart: 5 -> 5, of which waited for: 4 -> 5; matrix products, arithmetic and copies ran while one was open for 3% -> 1% of each run, Pallas kernels for 0% -> 2%
where the time goes in v3:
time: 167 us; the launch traced here: 165 us
  waiting for transfers between devices  57.3 us (34%)
  blocking collectives  55.3 us (33%)
  starting transfers between devices  24.8 us (15%)
  Pallas kernels  15.7 us (9%)
  local copies, waits for them, and re-layouts  9.37 us (6%)
  between operations  2.52 us (2%)
    all_to_all x1, blocking collectives, shards(): lax.all_to_all(outgoing, GROUP, split_axis=0, concat_axis=0, tiled=True)  55.3 us
    all_to_all x1, waiting for transfers between devices, shards(): lax.all_to_all(packed, GROUP, split_axis=0, concat_axis=0, tiled=True)  41.1 us
    all_to_all x1, starting transfers between devices, shards(): lax.all_to_all(packed, GROUP, split_axis=0, concat_axis=0, tiled=True)  10.8 us
    pallas_call x2, Pallas kernels, collect(): pl.pallas_call(functools.partial(collect_kernel, which), out_shape=jax.Sh...  6.98 us
    ppermute x1, starting transfers between devices, shards(): got_lower = lax.ppermute(lower, ALL, [(d, s) for s, d in there])  6.67 us
    unnamed x16, local copies, waits for them, and re-layouts  6.35 us
    ppermute x1, waiting for transfers between devices, shards(): got_lower = lax.ppermute(lower, ALL, [(d, s) for s, d in there])  6.27 us
    ppermute x1, waiting for transfers between devices, shards(): theirs = lax.ppermute(other, 'h', swap)  5.21 us
  transfers between devices with their start and end apart: 5, of which 5 were waited for; matrix products, arithmetic and copies ran while one was open for 1% of the time, Pallas kernels for 2%

profile of v3, /device:TPU:18, one launch (start us, length us, event | category | flops | bytes accessed | tf_op | source)
XLA Modules:
  0.0 165.0 jit_solution(13561254630772395401)
XLA Ops:
  0.6 0.0 copy-start.2
  0.6 1.2 copy-done.2
  1.9 0.5 share.1
  2.4 2.2 %collective-permute-start = (bf16[528,128]{1,0:T(8,128)(2,1)S(1)}, bf16[528,128]{1,0:T(8,128)(2,1)S(1)}, u32[]{:S(2)}, u32[]{:S(2)}) collective-permute-start(bf16[528,128]{1,0:T(8,128)(2,1)S(1)} %get-tuple-element.8), channel_id=1, source_target_pairs={{0,64},{64,0},{1,65},{65,1},{2,66},{66,2},{3,67},{67,3},{4,68},{68... | collective-permute-start | bytes 405512 | tf_op jit(solution)/shard_map/ppermute | solution.py:505
  4.6 4.7 %collective-permute-done.theirs = bf16[528,128]{1,0:T(8,128)(2,1)S(1)} collective-permute-done((bf16[528,128]{1,0:T(8,128)(2,1)S(1)}, bf16[528,128]{1,0:T(8,128)(2,1)S(1)}, u32[]{:S(2)}, u32[]{:S(2)}) %collective-permute-start) | collective-permute-done | bytes 135200 | tf_op jit(solution)/shard_map/ppermute | solution.py:505
  9.3 0.0 copy-start.3
  9.3 0.7 copy-done.3
  10.0 0.0 copy-start.5
  10.0 0.7 copy-done.5
  10.6 3.2 %pack.1 = bf16[64,208,128]{2,1,0:T(8,128)(2,1)} custom-call(s32[384]{0:T(512)S(1)} %copy-done.3, s32[128]{0:T(128)S(1)} %copy-done.5, bf16[528,128]{1,0:T(8,128)(2,1)S(1)} %get-tuple-element.7.mine, bf16[528,128]{1,0:T(8,128)(2,1)S(1)} %collective-permute-done.theirs), custom_call_target="tpu_custom_call" | custom-call | tf_op jit(solution)/shard_map/pack/pallas_call | solution.py:200
  13.8 0.0 copy-start.7
  13.8 0.0 copy-start.4
  13.8 0.0 copy-start.6
  13.8 10.8 %all-to-all-start = ((bf16[64,208,128]{2,1,0:T(8,128)(2,1)}), bf16[64,208,128]{2,1,0:T(8,128)(2,1)S(1)}, u32[]{:S(2)}, u32[]{:S(2)}) async-start(bf16[64,208,128]{2,1,0:T(8,128)(2,1)} %pack.1), calls=%async_computation | async-start | bytes 6815744 | tf_op jit(solution)/shard_map/all_to_all | solution.py:507
  24.7 0.0 copy-done.7
  24.7 0.9 copy.8.weights
  25.6 41.1 %all-to-all-done.window = bf16[64,208,128]{2,1,0:T(8,128)(2,1)S(1)} async-done(((bf16[64,208,128]{2,1,0:T(8,128)(2,1)}), bf16[64,208,128]{2,1,0:T(8,128)(2,1)S(1)}, u32[]{:S(2)}, u32[]{:S(2)}) %all-to-all-start) | async-done | bytes 3407904 | tf_op jit(solution)/shard_map/all_to_all | solution.py:507
  66.7 0.0 copy-done.4
  66.7 0.0 copy-done.6
  66.7 0.0 copy-start
  66.7 2.8 %copy-done = bf16[3,4,256,1024]{3,2,1,0:T(8,128)(2,1)S(1)} copy-done((bf16[3,4,256,1024]{3,2,1,0:T(8,128)(2,1)S(1)}, bf16[3,4,256,1024]{3,2,1,0:T(8,128)(2,1)}, u32[]{:S(2)}) %copy-start) | copy-done | bytes 6291480
  69.5 0.0 copy-start.1
  69.5 1.0 copy-done.1
  70.5 3.8 %batches.1 = bf16[64,208,128]{2,1,0:T(8,128)(2,1)S(1)} custom-call(s32[384]{0:T(512)S(1)} %copy-done.4, s32[128]{0:T(128)S(1)} %copy-done.6, f32[3,256,1]{2,1,0:T(8,128)S(1)} %copy-done.1, bf16[3,4,256,1024]{3,2,1,0:T(8,128)(2,1)S(1)} %copy-done, bf16[64,208,128]{2,1,0:T(8,128)(2,1)S(1)} %all-to-all-done.window), custom_call_target="tpu_custom_call" | custom-call | tf_op jit(solution)/shard_map/batches/pallas_call | solution.py:335
  74.3 55.3 %all_to_all.10.arrived = bf16[64,208,128]{2,1,0:T(8,128)(2,1)S(1)} all-to-all(bf16[64,208,128]{2,1,0:T(8,128)(2,1)S(1)} %batches.1), channel_id=1, replica_groups=mesh['h'=2,'xl'=2,'y'=4,'z'=4,'c'=2] {'xl','y','z','c'}, dimensions={0} | all-to-all | bytes 6815744 | tf_op jit(solution)/shard_map/all_to_all | solution.py:510
  129.6 3.5 %collect_other.1.sent = f32[520,128]{1,0:T(8,128)S(1)} custom-call(s32[384]{0:T(512)S(1)} %copy-done.4, s32[128]{0:T(128)S(1)} %copy-done.6, bf16[64,208,128]{2,1,0:T(8,128)(2,1)S(1)} %all_to_all.10.arrived), custom_call_target="tpu_custom_call" | custom-call | flops 1000000 | bytes 4194304 | tf_op jit(solution)/shard_map/collect_other/pallas_call | solution.py:401
  133.1 1.4 collective-permute-start.1
  134.6 3.4 %collect_own.1.mine = f32[520,128]{1,0:T(8,128)S(1)} custom-call(s32[384]{0:T(512)S(1)} %copy-done.4, s32[128]{0:T(128)S(1)} %copy-done.6, bf16[64,208,128]{2,1,0:T(8,128)(2,1)S(1)} %all_to_all.10.arrived), custom_call_target="tpu_custom_call" | custom-call | flops 1000000 | bytes 4194304 | tf_op jit(solution)/shard_map/collect_own/pallas_call | solution.py:401
  138.0 5.2 %collective-permute-done.1.theirs = f32[520,128]{1,0:T(8,128)S(1)} collective-permute-done((f32[520,128]{1,0:T(8,128)S(1)}, f32[520,128]{1,0:T(8,128)S(1)}, u32[]{:S(2)}, u32[]{:S(2)}) %collective-permute-start.1) | collective-permute-done | bytes 266272 | tf_op jit(solution)/shard_map/ppermute | solution.py:513
  143.3 3.7 %collective-permute-start.2 = (f32[256,128]{1,0:T(8,128)S(1)}, f32[256,128]{1,0:T(8,128)S(1)}, u32[]{:S(2)}, u32[]{:S(2)}) collective-permute-start(f32[256,128]{1,0:T(8,128)S(1)} %get-tuple-element.9.upper), channel_id=1, source_target_pairs={{0,0},{1,8},{2,16},{3,24},{4,32},{5,40},{6,48},{7,56},{8,65},{9,9}... | collective-permute-start | bytes 393224 | tf_op jit(solution)/shard_map/ppermute | solution.py:516
  147.0 6.7 %collective-permute-start.3 = (f32[256,128]{1,0:T(8,128)S(1)}, f32[256,128]{1,0:T(8,128)S(1)}, u32[]{:S(2)}, u32[]{:S(2)}) collective-permute-start(f32[256,128]{1,0:T(8,128)S(1)} %get-tuple-element.10.lower), channel_id=1, source_target_pairs={{0,0},{8,1},{16,2},{24,3},{32,4},{40,5},{48,6},{56,7},{65,8},{9,9}... | collective-permute-start | bytes 393224 | tf_op jit(solution)/shard_map/ppermute | solution.py:517
  153.6 0.5 slice.3
  154.8 0.1 collective-permute-done.2.got_upper
  154.9 6.3 %collective-permute-done.3.got_lower = f32[256,128]{1,0:T(8,128)S(1)} collective-permute-done((f32[256,128]{1,0:T(8,128)S(1)}, f32[256,128]{1,0:T(8,128)S(1)}, u32[]{:S(2)}, u32[]{:S(2)}) %collective-permute-start.3) | collective-permute-done | bytes 131104 | tf_op jit(solution)/shard_map/ppermute | solution.py:517
  161.1 1.6 broadcast_in_dim.3.blank
  162.7 1.1 place.1
  (1 shorter events, 0.0 us)
Async XLA Ops:
  0.6 1.2 copy-start.2
  2.4 6.9 %collective-permute-start = (bf16[528,128]{1,0:T(8,128)(2,1)S(1)}, bf16[528,128]{1,0:T(8,128)(2,1)S(1)}, u32[]{:S(2)}, u32[]{:S(2)}) collective-permute-start(bf16[528,128]{1,0:T(8,128)(2,1)S(1)} %get-tuple-element.8), channel_id=1, source_target_pairs={{0,64},{64,0},{1,65},{65,1},{2,66},{66,2},{3,67},{67,3},{4,68},{68... | collective-permute-start | bytes 405512 | tf_op jit(solution)/shard_map/ppermute | solution.py:505
  9.3 0.7 copy-start.3
  10.0 0.7 copy-start.5
  13.8 10.9 %copy-start.7 = (f32[3,256]{1,0:T(4,128)S(1)}, f32[3,256]{1,0:T(4,128)}, u32[]{:S(2)}) copy-start(f32[3,256]{1,0:T(4,128)} %param.7) | copy-start | bytes 9220
  13.8 52.9 %copy-start.4 = (s32[384]{0:T(512)S(1)}, s32[384]{0:T(512)}, u32[]{:S(2)}) copy-start(s32[384]{0:T(512)} %starts.7) | copy-start | bytes 4612
  13.8 52.9 %copy-start.6 = (s32[128]{0:T(128)S(1)}, s32[128]{0:T(128)}, u32[]{:S(2)}) copy-start(s32[128]{0:T(128)} %counts.7) | copy-start | bytes 1540
  13.8 52.8 %all-to-all-start = ((bf16[64,208,128]{2,1,0:T(8,128)(2,1)}), bf16[64,208,128]{2,1,0:T(8,128)(2,1)S(1)}, u32[]{:S(2)}, u32[]{:S(2)}) async-start(bf16[64,208,128]{2,1,0:T(8,128)(2,1)} %pack.1), calls=%async_computation | async-start | bytes 6815744 | tf_op jit(solution)/shard_map/all_to_all | solution.py:507
  66.7 2.8 %copy-start = (bf16[3,4,256,1024]{3,2,1,0:T(8,128)(2,1)S(1)}, bf16[3,4,256,1024]{3,2,1,0:T(8,128)(2,1)}, u32[]{:S(2)}) copy-start(bf16[3,4,256,1024]{3,2,1,0:T(8,128)(2,1)} %basis.1) | copy-start | bytes 18874372
  69.5 1.0 copy-start.1
  133.1 10.1 %collective-permute-start.1 = (f32[520,128]{1,0:T(8,128)S(1)}, f32[520,128]{1,0:T(8,128)S(1)}, u32[]{:S(2)}, u32[]{:S(2)}) collective-permute-start(f32[520,128]{1,0:T(8,128)S(1)} %collect_other.1.sent), channel_id=1, source_target_pairs={{0,64},{64,0},{1,65},{65,1},{2,66},{66,2},{3,67},{67,3},{4,68},{68... | collective-permute-start | bytes 798728 | tf_op jit(solution)/shard_map/ppermute | solution.py:513
  143.3 11.6 %collective-permute-start.2 = (f32[256,128]{1,0:T(8,128)S(1)}, f32[256,128]{1,0:T(8,128)S(1)}, u32[]{:S(2)}, u32[]{:S(2)}) collective-permute-start(f32[256,128]{1,0:T(8,128)S(1)} %get-tuple-element.9.upper), channel_id=1, source_target_pairs={{0,0},{1,8},{2,16},{3,24},{4,32},{5,40},{6,48},{7,56},{8,65},{9,9}... | collective-permute-start | bytes 393224 | tf_op jit(solution)/shard_map/ppermute | solution.py:516
  147.0 14.2 %collective-permute-start.3 = (f32[256,128]{1,0:T(8,128)S(1)}, f32[256,128]{1,0:T(8,128)S(1)}, u32[]{:S(2)}, u32[]{:S(2)}) collective-permute-start(f32[256,128]{1,0:T(8,128)S(1)} %get-tuple-element.10.lower), channel_id=1, source_target_pairs={{0,0},{8,1},{16,2},{24,3},{32,4},{40,5},{48,6},{56,7},{65,8},{9,9}... | collective-permute-start | bytes 393224 | tf_op jit(solution)/shard_map/ppermute | solution.py:517

commit v4 on v3

--- a/solution.py
+++ b/solution.py
@@ -1,4 +1,5 @@
 import functools
+import math
 
 import jax
 import jax.numpy as jnp
@@ -68,9 +69,13 @@
     return row_id, lax.axis_index("z") * 2 + lax.axis_index("c"), h
 
 
-def entry(starts, peer, slot, where):
+def live(plan, device):
+    return plan[N_ROW * N_COL * SLOTS + device]
+
+
+def entry(plan, peer, slot, where):
     row_id, col_id, h = where
-    start = starts[(h * PEERS + peer) * SLOTS + slot]
+    start = plan[(h * PEERS + peer) * SLOTS + slot]
     i = start + ((row_id - start) & (KB - 1))
     j = start + ((col_id - start) & (KB - 1))
     other = ((i >> 3) & 1) ^ h
@@ -150,7 +155,7 @@
 CHUNK = 8
 
 
-def pack_kernel(starts, counts, mine, theirs, out, table, lines, buf, sems):
+def pack_kernel(plan, mine, theirs, out, table, lines, buf, sems):
     where = position()
     on_diagonal = ((where[1] - where[0]) & (KB - 1)) == 0
     table[0] = mine[:BAND, :]
@@ -166,10 +171,10 @@
     def one_chunk(chunk, carry):
         for k in range(CHUNK):
             peer = chunk * CHUNK + k
-            count = counts[where[2] * PEERS + peer]
+            count = live(plan, where[2] * PEERS + peer)
 
             def one(slot):
-                other, _, at = entry(starts, peer, slot, where)
+                other, _, at = entry(plan, peer, slot, where)
                 buf[peer, slot * HB : (slot + 1) * HB, :] = table[other, pl.ds(at, HB), :]
 
             one(0)
@@ -180,7 +185,7 @@
             def _():
                 ext = jnp.zeros((16, BF), F32)
                 for slot in range(SLOTS):
-                    other, turn, _ = entry(starts, peer, slot, where)
+                    other, turn, _ = entry(plan, peer, slot, where)
                     ext = jnp.where(row == slot, lines[other, pl.ds(turn, 1), :], ext)
                 buf[peer, EXT:, :] = ext.astype(BF16)
 
@@ -196,12 +201,12 @@
     lax.fori_loop(0, PEERS // CHUNK, drain, 0)
 
 
-def pack(starts, counts, mine, theirs):
+def pack(plan, mine, theirs):
     return pl.pallas_call(
         pack_kernel,
         out_shape=jax.ShapeDtypeStruct((PEERS, ROWS, BF), BF16),
         grid_spec=scalars(
-            2,
+            1,
             [VMEM, VMEM],
             HBM,
             [
@@ -213,39 +218,49 @@
         ),
         compiler_params=limit(8),
         name="pack",
-    )(starts, counts, mine, theirs)
+    )(plan, mine, theirs)
 
 
 def batch_kernel(
-    starts, counts, weights, basis, window, out, quads, phis, mat, pair, lines, sem_w, sem_b
+    plan, weights, basis, window, out,
+    quads, phis, win, win_ext, mat, pair, lines, sem_e, sem_w, sem_b,
 ):
     row_id, col_id, _ = position()
     me = row_id * N_COL + col_id
-    count = counts[me]
+    count = live(plan, me)
     row, lane = lanes((16, BF))
-    weights_copy = pltpu.make_async_copy(weights, quads, sem_w)
+    weights_copy = pltpu.make_async_copy(weights, quads, sem_e.at[0])
+    ext_copy = pltpu.make_async_copy(window.at[:, pl.ds(EXT, 16)], win_ext, sem_e.at[1])
+
+    def window_copy(slot):
+        span = pl.ds(pl.multiple_of(slot * HB, HB), HB)
+        return pltpu.make_async_copy(window.at[:, span], win.at[slot], sem_w.at[slot])
 
     def basis_copy(slot):
         return pltpu.make_async_copy(basis.at[slot], phis.at[slot], sem_b.at[slot])
 
     def fetch(slot, carry):
+        window_copy(slot).start()
         basis_copy(slot).start()
         return carry
 
+    ext_copy.start()
     weights_copy.start()
     lax.fori_loop(0, count, fetch, 0)
     lines[...] = jnp.zeros(lines.shape, F32)
+    ext_copy.wait()
     weights_copy.wait()
 
     def work(slot, total):
-        start = starts[me * SLOTS + slot]
+        start = plan[me * SLOTS + slot]
         cls = [(start + o) & (KB - 1) for o in range(KB)]
         span = pl.ds(pl.multiple_of(slot * HB, HB), HB)
+        window_copy(slot).wait()
         for o1 in range(KB):
             r1 = o1 * BF
             for o2 in range(o1 + 1, KB):
-                top = window[cls[o1] * KB + cls[o2], span, :]
-                bottom = window[cls[o2] * KB + cls[o1], span, :]
+                top = win[slot, cls[o1] * KB + cls[o2]]
+                bottom = win[slot, cls[o2] * KB + cls[o1]]
                 mat[r1 : r1 + HB, o2 * BF : (o2 + 1) * BF] = top
                 mat[r1 + HB : r1 + BF, o2 * BF : (o2 + 1) * BF] = bottom
                 if o2 == o1 + 1 and o1 % 2 == 0:
@@ -253,11 +268,11 @@
                         [top, bottom], axis=0
                     ).T
             diagonal = cls[o1] * (KB + 1)
-            line = pick_row(window[diagonal, EXT:, :].astype(F32), slot)
-            block = unpack_symmetric(window[diagonal, span, :].astype(F32), line)
+            line = pick_row(win_ext[diagonal].astype(F32), slot)
+            block = unpack_symmetric(win[slot, diagonal].astype(F32), line)
             mat[r1 : r1 + BF, r1 : r1 + BF] = block.astype(BF16)
         basis_copy(slot).wait()
-        sums = [jnp.zeros((G, 1), F32) for _ in range(4)]
+        sums = [jnp.zeros((G, BF), F32) for _ in range(4)]
         for t in range(4):
             lo, hi = 256 * t, 256 * (t + 1)
             product = jnp.dot(phis[slot, 0, :, :hi], mat[:hi, lo:hi], preferred_element_type=F32)
@@ -269,9 +284,9 @@
                     preferred_element_type=F32,
                 )
             for k in range(4):
-                sums[k] += jnp.sum(
-                    phis[slot, k, :, lo:hi].astype(F32) * product, axis=1, keepdims=True
-                )
+                terms = phis[slot, k, :, lo:hi].astype(F32) * product
+                sums[k] += terms[:, :BF] + terms[:, BF:]
+        sums = [jnp.sum(x, axis=1, keepdims=True) for x in sums]
         rho = sums[0]
         grads = [2.0 * x for x in sums[1:]]
         sigma = grads[0] * grads[0] + grads[1] * grads[1] + grads[2] * grads[2]
@@ -331,59 +346,89 @@
             out[peer, EXT:, :] = energy.astype(BF16)
 
 
-def batches(starts, counts, weights, basis, window):
+def batches(plan, weights, basis, window):
     return pl.pallas_call(
         batch_kernel,
         out_shape=jax.ShapeDtypeStruct((PEERS, ROWS, BF), BF16),
         grid_spec=scalars(
-            2,
-            [HBM, HBM, VMEM],
+            1,
+            [HBM, HBM, HBM],
             VMEM,
             [
                 pltpu.VMEM((SLOTS, G, 1), F32),
                 pltpu.VMEM((SLOTS, 4, G, KF), BF16),
+                pltpu.VMEM((SLOTS, PEERS, HB, BF), BF16),
+                pltpu.VMEM((PEERS, 16, BF), BF16),
                 pltpu.VMEM((KF, KF), BF16),
                 pltpu.VMEM((2 * G, KF), BF16),
                 pltpu.VMEM((KB, 16, BF), F32),
-                pltpu.SemaphoreType.DMA,
+                pltpu.SemaphoreType.DMA((2,)),
+                pltpu.SemaphoreType.DMA((SLOTS,)),
                 pltpu.SemaphoreType.DMA((SLOTS,)),
             ],
         ),
-        compiler_params=limit(32),
+        compiler_params=limit(48),
         name="batches",
-    )(starts, counts, weights, basis, window)
-
-
-def collect_kernel(which, starts, counts, arrived, out, energy):
+    )(plan, weights, basis, window)
+
+
+STEP = math.log(2.0) / 128.0
+FULL = 32767.0
+
+
+def integer(values):
+    return values.astype(jnp.int32).astype(jnp.int16)
+
+
+def encode(values):
+    top = jnp.max(jnp.max(jnp.abs(values), axis=0, keepdims=True), axis=1, keepdims=True)
+    code = jnp.ceil(jnp.log(jnp.maximum(top, 2.0**-110)) * (1.0 / STEP))
+    scaled = values * jnp.exp(math.log(FULL) - code * STEP)
+    return jnp.clip(scaled, -FULL, FULL), code
+
+
+def decode(words, code):
+    return words.astype(F32) * jnp.exp(code.astype(F32) * STEP - math.log(FULL))
+
+
+def collect_kernel(which, plan, arrived, *refs):
     where = position()
     on_diagonal = ((where[1] - where[0]) & (KB - 1)) == 0
     row, lane = lanes((16, BF))
     eight, _ = lanes((8, BF))
-    out[...] = jnp.zeros(out.shape, F32)
-    energy[...] = jnp.zeros(energy.shape, F32)
+    if which:
+        out, acc, energy = refs
+        energy[...] = jnp.zeros(energy.shape, F32)
+    else:
+        acc, blank, zeros, sems = refs
+        zeros[...] = jnp.zeros(zeros.shape, F32)
+        fills = [pltpu.make_async_copy(zeros, blank.at[t], sems.at[t]) for t in range(TURNS)]
+        for fill in fills:
+            fill.start()
+    acc[...] = jnp.zeros(acc.shape, F32)
 
     def one_chunk(chunk, carry):
         for k in range(CHUNK):
             peer = chunk * CHUNK + k
-            count = counts[where[2] * PEERS + peer]
+            count = live(plan, where[2] * PEERS + peer)
             if which:
                 energy[...] += arrived[peer, EXT:, :].astype(F32)
 
-            def one(slot, live):
-                other, turn, at = entry(starts, peer, slot, where)
+            def one(slot, used):
+                other, turn, at = entry(plan, peer, slot, where)
                 wanted = other == which
 
-                @pl.when(wanted if live is None else wanted & live)
+                @pl.when(wanted if used is None else wanted & used)
                 def _():
                     part = arrived[peer, slot * HB : (slot + 1) * HB, :]
-                    out[pl.ds(at, HB), :] += part.astype(F32)
+                    acc[pl.ds(at, HB), :] += part.astype(F32)
 
                     @pl.when(on_diagonal)
                     def _():
                         ext = arrived[peer, EXT:, :].astype(F32)
                         line = jnp.where((row == slot) & (lane >= HB), ext, 0.0)
                         line = jnp.sum(line, axis=0, keepdims=True)
-                        out[BAND:, :] += jnp.where(eight == turn, line, 0.0)
+                        acc[BAND:, :] += jnp.where(eight == turn, line, 0.0)
 
             one(0, None)
             for slot in range(1, SLOTS):
@@ -391,38 +436,83 @@
         return carry
 
     lax.fori_loop(0, PEERS // CHUNK, one_chunk, 0)
+    if not which:
+        for fill in fills:
+            fill.wait()
+        return
+
+    words, code = encode(acc[BAND:, :])
+    ext = jnp.concatenate([words, words], axis=0)
+    ext = jnp.where(row == 7, code, ext)
+    total = jnp.where((row == 0) & (lane < 3), energy[...], 0.0)
+    total = jnp.sum(jnp.sum(total, axis=0, keepdims=True), axis=1, keepdims=True)
+    words, code = encode(total)
+    first = jnp.floor(words + 0.5)
+    ext = jnp.where(row == 4, first, ext)
+    ext = jnp.where(row == 5, (words - first) * FULL, ext)
+    ext = jnp.where(row == 6, code, ext)
+    for k in range(2 * TURNS):
+        words, code = encode(acc[k * HB : (k + 1) * HB, :])
+        out[k * HB : (k + 1) * HB, :] = integer(jnp.floor(words + 0.5))
+        ext = jnp.where(row == 8 + k, code, ext)
+    out[BAND:, :] = integer(jnp.floor(ext + 0.5))
+
+
+def collect(which, plan, arrived):
+    acc = jax.ShapeDtypeStruct((BAND + 8, BF), F32)
     if which:
-        total = jnp.where((row == 0) & (lane < 3), energy[...], 0.0)
-        total = jnp.sum(jnp.sum(total, axis=0, keepdims=True), axis=1, keepdims=True)
-        out[BAND:, :] = jnp.where(eight == TURNS, total, out[BAND:, :])
-
-
-def collect(which, starts, counts, arrived):
+        out_shape = jax.ShapeDtypeStruct((BAND + 16, BF), jnp.int16)
+        out_specs = VMEM
+        scratch = [pltpu.VMEM((BAND + 8, BF), F32), pltpu.VMEM((16, BF), F32)]
+    else:
+        out_shape = [acc, jax.ShapeDtypeStruct((TURNS, N_COL, BF, BF), F32)]
+        out_specs = [VMEM, HBM]
+        scratch = [pltpu.VMEM((N_COL, BF, BF), F32), pltpu.SemaphoreType.DMA((TURNS,))]
     return pl.pallas_call(
         functools.partial(collect_kernel, which),
-        out_shape=jax.ShapeDtypeStruct((BAND + 8, BF), F32),
-        grid_spec=scalars(2, [VMEM], VMEM, [pltpu.VMEM((16, BF), F32)]),
+        out_shape=out_shape,
+        grid_spec=scalars(1, [VMEM], out_specs, scratch),
         compiler_params=limit(8),
         cost_estimate=pl.CostEstimate(flops=10**6, bytes_accessed=4 * MIB, transcendentals=0),
         name=("collect_own", "collect_other")[which],
-    )(starts, counts, arrived)
-
-
-def merge_kernel(mine, sent, theirs, upper, lower, rest):
+    )(plan, arrived)
+
+
+def merge_kernel(mine, sent, theirs, upper, lower, rest, up_words, low_words):
     eight, _ = lanes((8, BF))
-    upper[...] = mine[: TURNS * HB, :] + theirs[: TURNS * HB, :]
-    lower[...] = mine[TURNS * HB : BAND, :] + theirs[TURNS * HB : BAND, :]
-    half = jnp.where(eight == TURNS, sent[BAND:, :], mine[BAND:, :])
-    rest[...] = half + theirs[BAND:, :]
+    row, _ = lanes((16, BF))
+    got = theirs[BAND:, :].astype(F32)
+    own = sent[BAND:, :].astype(F32)
+
+    def line(rows, index):
+        return rows[index : index + 1, :]
+
+    def energy(rows):
+        return decode(line(rows, 4) + line(rows, 5) * (1.0 / FULL), line(rows, 6))
+
+    more = jnp.where(eight < TURNS, decode(got[:8, :], line(got, 7)), 0.0)
+    rest[...] = jnp.where(eight == TURNS, energy(own) + energy(got), mine[BAND:, :] + more)
+    for low, full, words in ((0, upper, up_words), (1, lower, low_words)):
+        codes = jnp.zeros((16, BF), F32)
+        for t in range(TURNS):
+            k = low * TURNS + t
+            span = slice(k * HB, (k + 1) * HB)
+            total = mine[span, :] + decode(theirs[span, :].astype(F32), line(got, 8 + k))
+            full[t * HB : (t + 1) * HB, :] = total
+            scaled, code = encode(total)
+            words[t * HB : (t + 1) * HB, :] = integer(jnp.floor(scaled + 0.5))
+            codes = jnp.where(row == t, code, codes)
+        words[TURNS * HB :, :] = integer(jnp.floor(codes + 0.5))
 
 
 def merge(mine, sent, theirs):
     half = jax.ShapeDtypeStruct((TURNS * HB, BF), F32)
+    words = jax.ShapeDtypeStruct((TURNS * HB + 16, BF), jnp.int16)
     return pl.pallas_call(
         merge_kernel,
-        out_shape=[half, half, jax.ShapeDtypeStruct((8, BF), F32)],
+        out_shape=[half, half, jax.ShapeDtypeStruct((8, BF), F32), words, words],
         in_specs=[VMEM] * 3,
-        out_specs=[VMEM] * 3,
+        out_specs=[VMEM] * 5,
         compiler_params=limit(4),
         name="merge",
     )(mine, sent, theirs)
@@ -435,6 +525,10 @@
 
     def part(ref, turn):
         return ref[pl.ds(pl.multiple_of(turn * HB, HB), HB), :]
+
+    def coded(ref, turn):
+        code = pick_row(ref[TURNS * HB :, :].astype(F32), turn)
+        return decode(part(ref, turn).astype(F32), code)
 
     def write(t, low, at):
         slot = TURNS * low + t
@@ -451,7 +545,7 @@
                 else:
                     turn = t + jnp.where(row_id + shift >= N_ROW, 1, 0)
                     blocks[t, :HB, :] = part(upper, t)
-                    blocks[t, HB:, :] = part(got_lower, jnp.minimum(turn, TURNS - 1))
+                    blocks[t, HB:, :] = coded(got_lower, jnp.minimum(turn, TURNS - 1))
                     write(t, 0, at).start()
 
             @pl.when((shift > 0) & (at > 0))
@@ -460,7 +554,7 @@
                     write(t, 1, at - 1).wait()
                 else:
                     turn = t - jnp.where(row_id + shift < N_COL, 1, 0)
-                    top = part(got_upper, jnp.maximum(turn, 0))
+                    top = coded(got_upper, jnp.maximum(turn, 0))
                     blocks[TURNS + t] = jnp.concatenate([top, part(lower, t)], axis=0).T
                     write(t, 1, at - 1).start()
 
@@ -501,21 +595,21 @@
 def shards(density, basis, weights, batch_start, batch_count):
     swap = [(0, 1), (1, 0)]
     there = mirror_pairs()
+    plan = jnp.concatenate([batch_start, batch_count])
     held, sent = share(density)
     theirs = lax.ppermute(sent, "h", swap)
-    packed = pack(batch_start, batch_count, held, theirs)
+    packed = pack(plan, held, theirs)
     window = lax.all_to_all(packed, GROUP, split_axis=0, concat_axis=0, tiled=True)
 
-    outgoing = batches(batch_start, batch_count, weights.reshape(SLOTS, G, 1), basis, window)
+    outgoing = batches(plan, weights.reshape(SLOTS, G, 1), basis, window)
     arrived = lax.all_to_all(outgoing, GROUP, split_axis=0, concat_axis=0, tiled=True)
 
-    other = collect(1, batch_start, batch_count, arrived)
-    theirs = lax.ppermute(other, "h", swap)
-    mine = collect(0, batch_start, batch_count, arrived)
-    upper, lower, rest = merge(mine, other, theirs)
-    got_upper = lax.ppermute(upper, ALL, there)
-    got_lower = lax.ppermute(lower, ALL, [(d, s) for s, d in there])
-    blank = jnp.zeros(density.shape, F32)
+    sent = collect(1, plan, arrived)
+    theirs = lax.ppermute(sent, "h", swap)
+    mine, blank = collect(0, plan, arrived)
+    upper, lower, rest, up_words, low_words = merge(mine, sent, theirs)
+    got_upper = lax.ppermute(up_words, ALL, there)
+    got_lower = lax.ppermute(low_words, ALL, [(d, s) for s, d in there])
     potential = place(upper, lower, rest, got_upper, got_lower, blank)
     return potential, rest[TURNS, 0] / (NBLK * BF)
 

time: 167 us -> 156 us (0.934); the launches traced: 165 us -> 156 us
  waiting for transfers between devices: 57.3 us -> 51 us
  local copies, waits for them, and re-layouts: 9.37 us -> 3.28 us
  Pallas kernels: 15.7 us -> 17.6 us
    ppermute x3 -> x2, waiting for transfers between devices: 11.5 us -> 5.07 us  [the longest x1 5.06 us: shards(): got_lower = lax.ppermute(low_words, ALL, [(d, s) for s, d in there])]
    unnamed x16 -> x5, local copies, waits for them, and re-layouts: 6.35 us -> 1.92 us
    ppermute x1 -> x2, starting transfers between devices: 2.2 us -> 5.17 us  [shards(): theirs = lax.ppermute(sent, 'h', swap)]
    ppermute x3 -> x2, starting transfers between devices: 11.8 us -> 10.4 us  [the longest x1 5.23 us: shards(): got_lower = lax.ppermute(low_words, ALL, [(d, s) for s, d in there])]
    ppermute x1 -> x2, waiting for transfers between devices: 4.7 us -> 4.15 us  [shards(): theirs = lax.ppermute(sent, 'h', swap)]
  transfers between devices with their start and end apart: 5 -> 5, of which waited for: 5 -> 4; matrix products, arithmetic and copies ran while one was open for 1% -> 1% of each run, Pallas kernels for 2% -> 2%
where the time goes in v4:
time: 156 us
  blocking collectives  55.1 us (35%)
  waiting for transfers between devices  51 us (33%)
  starting transfers between devices  26.4 us (17%)
  Pallas kernels  17.6 us (11%)
  local copies, waits for them, and re-layouts  3.28 us (2%)
  between operations  2.53 us (2%)
    all_to_all x1, blocking collectives, shards(): lax.all_to_all(outgoing, GROUP, split_axis=0, concat_axis=0, tiled=True)  55.1 us
    all_to_all x1, waiting for transfers between devices, shards(): lax.all_to_all(packed, GROUP, split_axis=0, concat_axis=0, tiled=True)  41.7 us
    all_to_all x1, starting transfers between devices, shards(): lax.all_to_all(packed, GROUP, split_axis=0, concat_axis=0, tiled=True)  10.9 us
    pallas_call x2, Pallas kernels, collect(): pl.pallas_call(functools.partial(collect_kernel, which), out_shape=out_sh...  7.16 us
    ppermute x1, starting transfers between devices, shards(): got_lower = lax.ppermute(low_words, ALL, [(d, s) for s, d in there])  5.23 us
    pallas_call x1, Pallas kernels, batches(): pl.pallas_call(batch_kernel, out_shape=jax.ShapeDtypeStruct((PEERS, ROWS,...  5.2 us
    ppermute x2, starting transfers between devices, shards(): theirs = lax.ppermute(sent, 'h', swap)  5.17 us
    ppermute x1, starting transfers between devices, shards(): got_upper = lax.ppermute(up_words, ALL, there)  5.12 us
  transfers between devices with their start and end apart: 5, of which 4 were waited for; matrix products, arithmetic and copies ran while one was open for 1% of the time, Pallas kernels for 2%

profile of v4, /device:TPU:18, one launch (start us, length us, event | category | flops | bytes accessed | tf_op | source)
XLA Modules:
  0.0 155.8 jit_solution(6814566102193181119)
XLA Ops:
  0.6 0.0 copy-start
  0.6 1.2 copy-done
  1.9 0.5 share.1
  2.4 2.2 %collective-permute-start = (bf16[528,128]{1,0:T(8,128)(2,1)S(1)}, bf16[528,128]{1,0:T(8,128)(2,1)S(1)}, u32[]{:S(2)}, u32[]{:S(2)}) collective-permute-start(bf16[528,128]{1,0:T(8,128)(2,1)S(1)} %get-tuple-element.12), channel_id=1, source_target_pairs={{0,64},{64,0},{1,65},{65,1},{2,66},{66,2},{3,67},{67,3},{4,68},{68... | collective-permute-start | bytes 405512 | tf_op jit(solution)/shard_map/ppermute | solution.py:600
  4.6 0.7 constant_dynamic-update-slice_fusion.1
  5.3 0.7 constant_dynamic-update-slice_fusion.plan
  5.9 3.3 %collective-permute-done.theirs = bf16[528,128]{1,0:T(8,128)(2,1)S(1)} collective-permute-done((bf16[528,128]{1,0:T(8,128)(2,1)S(1)}, bf16[528,128]{1,0:T(8,128)(2,1)S(1)}, u32[]{:S(2)}, u32[]{:S(2)}) %collective-permute-start) | collective-permute-done | bytes 135200 | tf_op jit(solution)/shard_map/ppermute | solution.py:600
  9.3 3.2 %pack.1 = bf16[64,208,128]{2,1,0:T(8,128)(2,1)} custom-call(s32[512]{0:T(512)S(1)} %constant_dynamic-update-slice_fusion.plan, bf16[528,128]{1,0:T(8,128)(2,1)S(1)} %get-tuple-element.11.mine, bf16[528,128]{1,0:T(8,128)(2,1)S(1)} %collective-permute-done.theirs), custom_call_target="tpu_custom_call" | custom-call | tf_op jit(solution)/shard_map/pack/pallas_call | solution.py:205
  12.5 0.0 copy-start.1
  12.5 10.9 %all-to-all-start = ((bf16[64,208,128]{2,1,0:T(8,128)(2,1)}), bf16[64,208,128]{2,1,0:T(8,128)(2,1)}, u32[]{:S(2)}, u32[]{:S(2)}) async-start(bf16[64,208,128]{2,1,0:T(8,128)(2,1)} %pack.1), calls=%async_computation | async-start | bytes 6815744 | tf_op jit(solution)/shard_map/all_to_all | solution.py:602
  23.4 0.0 copy-done.1
  23.4 0.2 copy.8.weights
  23.6 41.7 %all-to-all-done.window = bf16[64,208,128]{2,1,0:T(8,128)(2,1)} async-done(((bf16[64,208,128]{2,1,0:T(8,128)(2,1)}), bf16[64,208,128]{2,1,0:T(8,128)(2,1)}, u32[]{:S(2)}, u32[]{:S(2)}) %all-to-all-start) | async-done | bytes 3407904 | tf_op jit(solution)/shard_map/all_to_all | solution.py:602
  65.3 5.2 %batches.1 = bf16[64,208,128]{2,1,0:T(8,128)(2,1)S(1)} custom-call(s32[512]{0:T(512)S(1)} %constant_dynamic-update-slice_fusion.plan, f32[3,256,1]{2,1,0:T(8,128)S(1)} %copy.8.weights, bf16[3,4,256,1024]{3,2,1,0:T(8,128)(2,1)} %basis.1, bf16[64,208,128]{2,1,0:T(8,128)(2,1)} %all-to-all-done.window), custom_call_target="tpu_custom_call" | custom-call | tf_op jit(solution)/shard_map/batches/pallas_call | solution.py:350
  70.5 55.1 %all_to_all.10.arrived = bf16[64,208,128]{2,1,0:T(8,128)(2,1)S(1)} all-to-all(bf16[64,208,128]{2,1,0:T(8,128)(2,1)S(1)} %batches.1), channel_id=1, replica_groups=mesh['h'=2,'xl'=2,'y'=4,'z'=4,'c'=2] {'xl','y','z','c'}, dimensions={0} | all-to-all | bytes 6815744 | tf_op jit(solution)/shard_map/all_to_all | solution.py:605
  125.6 3.6 %collect_other.1.sent = s16[528,128]{1,0:T(8,128)(2,1)S(1)} custom-call(s32[512]{0:T(512)S(1)} %constant_dynamic-update-slice_fusion.plan, bf16[64,208,128]{2,1,0:T(8,128)(2,1)S(1)} %all_to_all.10.arrived), custom_call_target="tpu_custom_call" | custom-call | flops 1000000 | bytes 4194304 | tf_op jit(solution)/shard_map/collect_other/pallas_call | solution.py:471
  129.2 3.0 %collective-permute-start.1 = (s16[528,128]{1,0:T(8,128)(2,1)S(1)}, s16[528,128]{1,0:T(8,128)(2,1)S(1)}, u32[]{:S(2)}, u32[]{:S(2)}) collective-permute-start(s16[528,128]{1,0:T(8,128)(2,1)S(1)} %collect_other.1.sent), channel_id=1, source_target_pairs={{0,64},{64,0},{1,65},{65,1},{2,66},{66,2},{3,67},{67,3},{4,68},{68... | collective-permute-start | bytes 405512 | tf_op jit(solution)/shard_map/ppermute | solution.py:608
  132.2 3.6 %collect_own.1 = (f32[520,128]{1,0:T(8,128)S(1)}, f32[4,8,128,128]{3,2,1,0:T(8,128)}) custom-call(s32[512]{0:T(512)S(1)} %constant_dynamic-update-slice_fusion.plan, bf16[64,208,128]{2,1,0:T(8,128)(2,1)S(1)} %all_to_all.10.arrived), custom_call_target="tpu_custom_call" | custom-call | flops 1000000 | bytes 4194304 | tf_op jit(solution)/shard_map/collect_own/pallas_call | solution.py:471
  135.8 0.8 collective-permute-done.1.theirs
  136.6 0.2 merge.1
  136.8 5.1 %collective-permute-start.2 = (s16[272,128]{1,0:T(8,128)(2,1)S(1)}, s16[272,128]{1,0:T(8,128)(2,1)S(1)}, u32[]{:S(2)}, u32[]{:S(2)}) collective-permute-start(s16[272,128]{1,0:T(8,128)(2,1)S(1)} %get-tuple-element.17), channel_id=1, source_target_pairs={{0,0},{1,8},{2,16},{3,24},{4,32},{5,40},{6,48},{7,56},{8,65},{9,9}... | collective-permute-start | bytes 208904 | tf_op jit(solution)/shard_map/ppermute | solution.py:611
  141.9 5.2 %collective-permute-start.3 = (s16[272,128]{1,0:T(8,128)(2,1)S(1)}, s16[272,128]{1,0:T(8,128)(2,1)S(1)}, u32[]{:S(2)}, u32[]{:S(2)}) collective-permute-start(s16[272,128]{1,0:T(8,128)(2,1)S(1)} %get-tuple-element.18), channel_id=1, source_target_pairs={{0,0},{8,1},{16,2},{24,3},{32,4},{40,5},{48,6},{56,7},{65,8},{9,9}... | collective-permute-start | bytes 208904 | tf_op jit(solution)/shard_map/ppermute | solution.py:612
  147.2 0.5 slice.3
  148.3 0.0 collective-permute-done.2.got_upper
  148.3 5.1 %collective-permute-done.3.got_lower = s16[272,128]{1,0:T(8,128)(2,1)S(1)} collective-permute-done((s16[272,128]{1,0:T(8,128)(2,1)S(1)}, s16[272,128]{1,0:T(8,128)(2,1)S(1)}, u32[]{:S(2)}, u32[]{:S(2)}) %collective-permute-start.3) | collective-permute-done | bytes 69664 | tf_op jit(solution)/shard_map/ppermute | solution.py:612
  153.4 1.3 place.1
  (1 shorter events, 0.0 us)
Async XLA Ops:
  0.6 1.2 copy-start
  2.4 6.9 %collective-permute-start = (bf16[528,128]{1,0:T(8,128)(2,1)S(1)}, bf16[528,128]{1,0:T(8,128)(2,1)S(1)}, u32[]{:S(2)}, u32[]{:S(2)}) collective-permute-start(bf16[528,128]{1,0:T(8,128)(2,1)S(1)} %get-tuple-element.12), channel_id=1, source_target_pairs={{0,64},{64,0},{1,65},{65,1},{2,66},{66,2},{3,67},{67,3},{4,68},{68... | collective-permute-start | bytes 405512 | tf_op jit(solution)/shard_map/ppermute | solution.py:600
  12.5 10.9 %copy-start.1 = (f32[3,256]{1,0:T(4,128)S(1)}, f32[3,256]{1,0:T(4,128)}, u32[]{:S(2)}) copy-start(f32[3,256]{1,0:T(4,128)} %param.7) | copy-start | bytes 9220
  12.5 52.8 %all-to-all-start = ((bf16[64,208,128]{2,1,0:T(8,128)(2,1)}), bf16[64,208,128]{2,1,0:T(8,128)(2,1)}, u32[]{:S(2)}, u32[]{:S(2)}) async-start(bf16[64,208,128]{2,1,0:T(8,128)(2,1)} %pack.1), calls=%async_computation | async-start | bytes 6815744 | tf_op jit(solution)/shard_map/all_to_all | solution.py:602
  129.2 7.3 %collective-permute-start.1 = (s16[528,128]{1,0:T(8,128)(2,1)S(1)}, s16[528,128]{1,0:T(8,128)(2,1)S(1)}, u32[]{:S(2)}, u32[]{:S(2)}) collective-permute-start(s16[528,128]{1,0:T(8,128)(2,1)S(1)} %collect_other.1.sent), channel_id=1, source_target_pairs={{0,64},{64,0},{1,65},{65,1},{2,66},{66,2},{3,67},{67,3},{4,68},{68... | collective-permute-start | bytes 405512 | tf_op jit(solution)/shard_map/ppermute | solution.py:608
  136.8 11.5 %collective-permute-start.2 = (s16[272,128]{1,0:T(8,128)(2,1)S(1)}, s16[272,128]{1,0:T(8,128)(2,1)S(1)}, u32[]{:S(2)}, u32[]{:S(2)}) collective-permute-start(s16[272,128]{1,0:T(8,128)(2,1)S(1)} %get-tuple-element.17), channel_id=1, source_target_pairs={{0,0},{1,8},{2,16},{3,24},{4,32},{5,40},{6,48},{7,56},{8,65},{9,9}... | collective-permute-start | bytes 208904 | tf_op jit(solution)/shard_map/ppermute | solution.py:611
  141.9 11.5 %collective-permute-start.3 = (s16[272,128]{1,0:T(8,128)(2,1)S(1)}, s16[272,128]{1,0:T(8,128)(2,1)S(1)}, u32[]{:S(2)}, u32[]{:S(2)}) collective-permute-start(s16[272,128]{1,0:T(8,128)(2,1)S(1)} %get-tuple-element.18), channel_id=1, source_target_pairs={{0,0},{8,1},{16,2},{24,3},{32,4},{40,5},{48,6},{56,7},{65,8},{9,9}... | collective-permute-start | bytes 208904 | tf_op jit(solution)/shard_map/ppermute | solution.py:612

commit v5 on v4

--- a/solution.py
+++ b/solution.py
@@ -58,6 +58,14 @@
     return jnp.concatenate([top, jnp.where(c < HB, flip[HB:], corner)], axis=0)
 
 
+def split_symmetric(packed, row):
+    r, c = lanes((HB, BF))
+    low = jnp.where((c >= HB) & (c - HB < r), pltpu.roll(packed, HB, 1), 0.0)
+    first = [jnp.where((c >= HB) | (r <= c), packed, 0.0), jnp.where(c - HB == r, row, low)]
+    second = [jnp.where((c >= HB) | (r < c), packed, 0.0), low]
+    return jnp.concatenate(first, axis=0), jnp.concatenate(second, axis=0)
+
+
 def pick_row(rows, index):
     r, _ = lanes(rows.shape)
     return jnp.sum(jnp.where(r == index, rows, 0.0), axis=0, keepdims=True)
@@ -221,16 +229,72 @@
     )(plan, mine, theirs)
 
 
+def turn_kernel(plan, basis, out, held, turned, sem_in, sem_out):
+    row_id, col_id, _ = position()
+    count = live(plan, row_id * N_COL + col_id)
+
+    def load(slot):
+        return pltpu.make_async_copy(basis.at[slot], held.at[slot], sem_in.at[slot])
+
+    def store(slot):
+        return pltpu.make_async_copy(turned.at[slot], out.at[slot], sem_out.at[slot])
+
+    def fetch(slot, carry):
+        load(slot).start()
+        return carry
+
+    def work(slot, carry):
+        load(slot).wait()
+        for k in range(4):
+            for o in range(KB):
+                span = slice(o * BF, (o + 1) * BF)
+                turned[slot, k, span, :] = held[slot, k, :, span].T
+        store(slot).start()
+        return carry
+
+    def drain(slot, carry):
+        store(slot).wait()
+        return carry
+
+    lax.fori_loop(0, count, fetch, 0)
+    lax.fori_loop(0, count, work, 0)
+    lax.fori_loop(0, count, drain, 0)
+
+
+def turn(plan, basis):
+    return pl.pallas_call(
+        turn_kernel,
+        out_shape=jax.ShapeDtypeStruct((SLOTS, 4, KF, G), BF16),
+        grid_spec=scalars(
+            1,
+            [HBM],
+            HBM,
+            [
+                pltpu.VMEM((SLOTS, 4, G, KF), BF16),
+                pltpu.VMEM((SLOTS, 4, KF, G), BF16),
+                pltpu.SemaphoreType.DMA((SLOTS,)),
+                pltpu.SemaphoreType.DMA((SLOTS,)),
+            ],
+        ),
+        compiler_params=limit(48),
+        cost_estimate=pl.CostEstimate(flops=10**6, bytes_accessed=24 * MIB, transcendentals=0),
+        name="turn",
+    )(plan, basis)
+
+
+def dot_nt(x, y):
+    return lax.dot_general(x, y, (((1,), (1,)), ((), ())), preferred_element_type=F32)
+
+
 def batch_kernel(
-    plan, weights, basis, window, out,
-    quads, phis, win, win_ext, mat, pair, lines, sem_e, sem_w, sem_b,
+    plan, weights, basis, flipped, window, out,
+    phis, turned, win, win_ext, mat, corner, left, right, lines, sem_e, sem_w, sem_b, sem_t,
 ):
     row_id, col_id, _ = position()
     me = row_id * N_COL + col_id
     count = live(plan, me)
     row, lane = lanes((16, BF))
-    weights_copy = pltpu.make_async_copy(weights, quads, sem_e.at[0])
-    ext_copy = pltpu.make_async_copy(window.at[:, pl.ds(EXT, 16)], win_ext, sem_e.at[1])
+    ext_copy = pltpu.make_async_copy(window.at[:, pl.ds(EXT, 16)], win_ext, sem_e)
 
     def window_copy(slot):
         span = pl.ds(pl.multiple_of(slot * HB, HB), HB)
@@ -239,17 +303,23 @@
     def basis_copy(slot):
         return pltpu.make_async_copy(basis.at[slot], phis.at[slot], sem_b.at[slot])
 
+    def flipped_copy(slot):
+        return pltpu.make_async_copy(flipped.at[slot], turned.at[slot], sem_t.at[slot])
+
     def fetch(slot, carry):
         window_copy(slot).start()
         basis_copy(slot).start()
+        flipped_copy(slot).start()
         return carry
 
     ext_copy.start()
-    weights_copy.start()
     lax.fori_loop(0, count, fetch, 0)
     lines[...] = jnp.zeros(lines.shape, F32)
+    for t in range(4):
+        lo = 256 * t
+        mat[lo + BF : lo + 256, lo : lo + BF] = jnp.zeros((BF, BF), BF16)
+        corner[t, BF:, :BF] = jnp.zeros((BF, BF), BF16)
     ext_copy.wait()
-    weights_copy.wait()
 
     def work(slot, total):
         start = plan[me * SLOTS + slot]
@@ -257,40 +327,36 @@
         span = pl.ds(pl.multiple_of(slot * HB, HB), HB)
         window_copy(slot).wait()
         for o1 in range(KB):
-            r1 = o1 * BF
+            r1, t, c1 = o1 * BF, o1 // 2, o1 % 2 * BF
             for o2 in range(o1 + 1, KB):
                 top = win[slot, cls[o1] * KB + cls[o2]]
                 bottom = win[slot, cls[o2] * KB + cls[o1]]
                 mat[r1 : r1 + HB, o2 * BF : (o2 + 1) * BF] = top
                 mat[r1 + HB : r1 + BF, o2 * BF : (o2 + 1) * BF] = bottom
                 if o2 == o1 + 1 and o1 % 2 == 0:
-                    mat[o2 * BF : (o2 + 1) * BF, r1 : r1 + BF] = jnp.concatenate(
-                        [top, bottom], axis=0
-                    ).T
+                    corner[t, :HB, BF:] = top
+                    corner[t, HB:BF, BF:] = bottom
             diagonal = cls[o1] * (KB + 1)
             line = pick_row(win_ext[diagonal].astype(F32), slot)
-            block = unpack_symmetric(win[slot, diagonal].astype(F32), line)
-            mat[r1 : r1 + BF, r1 : r1 + BF] = block.astype(BF16)
+            first, second = split_symmetric(win[slot, diagonal].astype(F32), line)
+            mat[r1 : r1 + BF, r1 : r1 + BF] = first.astype(BF16)
+            corner[t, c1 : c1 + BF, c1 : c1 + BF] = second.astype(BF16)
         basis_copy(slot).wait()
         sums = [jnp.zeros((G, BF), F32) for _ in range(4)]
         for t in range(4):
             lo, hi = 256 * t, 256 * (t + 1)
             product = jnp.dot(phis[slot, 0, :, :hi], mat[:hi, lo:hi], preferred_element_type=F32)
+            product += dot_nt(phis[slot, 0, :, lo:hi], corner[t])
             if hi < KF:
-                product += lax.dot_general(
-                    phis[slot, 0, :, hi:],
-                    mat[lo:hi, hi:],
-                    (((1,), (1,)), ((), ())),
-                    preferred_element_type=F32,
-                )
+                product += dot_nt(phis[slot, 0, :, hi:], mat[lo:hi, hi:])
             for k in range(4):
                 terms = phis[slot, k, :, lo:hi].astype(F32) * product
                 sums[k] += terms[:, :BF] + terms[:, BF:]
-        sums = [jnp.sum(x, axis=1, keepdims=True) for x in sums]
+        sums = [jnp.sum(x.T, axis=0, keepdims=True) for x in sums]
         rho = sums[0]
         grads = [2.0 * x for x in sums[1:]]
         sigma = grads[0] * grads[0] + grads[1] * grads[1] + grads[2] * grads[2]
-        quad = quads[slot]
+        quad = weights[pl.ds(slot, 1), :]
         square = rho * rho + 1.0
         logs = jnp.log(square)
         cube = jnp.exp(logs * (1.0 / 3.0))
@@ -306,19 +372,21 @@
         ws = 2.0 * quad * by_sigma
         total = total + jnp.sum(quad * point)
         coeffs = [wr] + [ws * x for x in grads]
+        flipped_copy(slot).wait()
         for t in range(4):
             lo, hi = 256 * t, 256 * (t + 1)
-            mixed = coeffs[0] * phis[slot, 0, :, lo:hi].astype(F32)
+            phi = turned[slot, 0, lo:hi, :]
+            mixed = coeffs[0] * phi.astype(F32)
             for k in range(1, 4):
-                mixed += coeffs[k] * phis[slot, k, :, lo:hi].astype(F32)
-            pair[:G, lo:hi] = mixed.astype(BF16)
-        pair[G:, :] = phis[slot, 0]
+                mixed += coeffs[k] * turned[slot, k, lo:hi, :].astype(F32)
+            mixed = mixed.astype(BF16)
+            left[lo:hi, :G] = phi
+            left[lo:hi, G:] = mixed
+            right[lo:hi, :G] = mixed
+            right[lo:hi, G:] = phi
         for t in range(4):
             lo, hi = 256 * t, 256 * (t + 1)
-            left = jnp.concatenate([pair[G:, lo:hi], pair[:G, lo:hi]], axis=0)
-            rows = lax.dot_general(
-                left, pair[:, lo:], (((0,), (0,)), ((), ())), preferred_element_type=F32
-            )
+            rows = dot_nt(left[lo:hi, :], right[lo:, :])
             for k in range(2):
                 o1 = 2 * t + k
                 for o2 in range(o1, KB):
@@ -346,30 +414,33 @@
             out[peer, EXT:, :] = energy.astype(BF16)
 
 
-def batches(plan, weights, basis, window):
+def batches(plan, weights, basis, flipped, window):
     return pl.pallas_call(
         batch_kernel,
         out_shape=jax.ShapeDtypeStruct((PEERS, ROWS, BF), BF16),
         grid_spec=scalars(
             1,
-            [HBM, HBM, HBM],
+            [VMEM, HBM, HBM, HBM],
             VMEM,
             [
-                pltpu.VMEM((SLOTS, G, 1), F32),
                 pltpu.VMEM((SLOTS, 4, G, KF), BF16),
+                pltpu.VMEM((SLOTS, 4, KF, G), BF16),
                 pltpu.VMEM((SLOTS, PEERS, HB, BF), BF16),
                 pltpu.VMEM((PEERS, 16, BF), BF16),
                 pltpu.VMEM((KF, KF), BF16),
-                pltpu.VMEM((2 * G, KF), BF16),
+                pltpu.VMEM((4, 256, 256), BF16),
+                pltpu.VMEM((KF, 2 * G), BF16),
+                pltpu.VMEM((KF, 2 * G), BF16),
                 pltpu.VMEM((KB, 16, BF), F32),
-                pltpu.SemaphoreType.DMA((2,)),
+                pltpu.SemaphoreType.DMA,
+                pltpu.SemaphoreType.DMA((SLOTS,)),
                 pltpu.SemaphoreType.DMA((SLOTS,)),
                 pltpu.SemaphoreType.DMA((SLOTS,)),
             ],
         ),
         compiler_params=limit(48),
         name="batches",
-    )(plan, weights, basis, window)
+    )(plan, weights, basis, flipped, window)
 
 
 STEP = math.log(2.0) / 128.0
@@ -601,7 +672,7 @@
     packed = pack(plan, held, theirs)
     window = lax.all_to_all(packed, GROUP, split_axis=0, concat_axis=0, tiled=True)
 
-    outgoing = batches(plan, weights.reshape(SLOTS, G, 1), basis, window)
+    outgoing = batches(plan, weights, basis, turn(plan, basis), window)
     arrived = lax.all_to_all(outgoing, GROUP, split_axis=0, concat_axis=0, tiled=True)
 
     sent = collect(1, plan, arrived)

time: 156 us -> 157 us (level)
  Pallas kernels: 17.6 us -> 21.9 us
  waiting for transfers between devices: 51 us -> 47 us
  blocking collectives: 55.1 us -> 56.7 us
    pallas_call x0 -> x1, Pallas kernels: none -> 4.16 us  [turn(): pl.pallas_call(turn_kernel, out_shape=jax.ShapeDtypeStruct((SLOTS, 4, KF,...]
    all_to_all x1, waiting for transfers between devices: 41.7 us -> 37.8 us  [shards(): lax.all_to_all(packed, GROUP, split_axis=0, concat_axis=0, tiled=True)]
  transfers between devices with their start and end apart: 5 -> 5, of which waited for: 4 -> 4; matrix products, arithmetic and copies ran while one was open for 1% -> 1% of each run, Pallas kernels for 2% -> 5%
where the time goes in v5:
time: 157 us
  blocking collectives  56.7 us (36%)
  waiting for transfers between devices  47 us (30%)
  starting transfers between devices  25.8 us (16%)
  Pallas kernels  21.9 us (14%)
  local copies, waits for them, and re-layouts  3.1 us (2%)
  between operations  2.52 us (2%)
    all_to_all x1, blocking collectives, shards(): lax.all_to_all(outgoing, GROUP, split_axis=0, concat_axis=0, tiled=True)  56.7 us
    all_to_all x1, waiting for transfers between devices, shards(): lax.all_to_all(packed, GROUP, split_axis=0, concat_axis=0, tiled=True)  37.8 us
    all_to_all x1, starting transfers between devices, shards(): lax.all_to_all(packed, GROUP, split_axis=0, concat_axis=0, tiled=True)  10.9 us
    pallas_call x2, Pallas kernels, collect(): pl.pallas_call(functools.partial(collect_kernel, which), out_shape=out_sh...  7.16 us
    ppermute x1, starting transfers between devices, shards(): got_lower = lax.ppermute(low_words, ALL, [(d, s) for s, d in there])  5.77 us
    pallas_call x1, Pallas kernels, batches(): pl.pallas_call(batch_kernel, out_shape=jax.ShapeDtypeStruct((PEERS, ROWS,...  5.37 us
    ppermute x2, waiting for transfers between devices, shards(): theirs = lax.ppermute(sent, 'h', swap)  4.77 us
    ppermute x1, starting transfers between devices, shards(): got_upper = lax.ppermute(up_words, ALL, there)  4.59 us
  transfers between devices with their start and end apart: 5, of which 4 were waited for; matrix products, arithmetic and copies ran while one was open for 1% of the time, Pallas kernels for 5%

profile of v5, /device:TPU:18, one launch (start us, length us, event | category | flops | bytes accessed | tf_op | source)
XLA Modules:
  0.0 157.0 jit_solution(5445548157150214838)
XLA Ops:
  0.6 0.0 copy-start
  0.6 1.2 copy-done
  1.9 0.5 share.1
  2.4 2.2 %collective-permute-start = (bf16[528,128]{1,0:T(8,128)(2,1)S(1)}, bf16[528,128]{1,0:T(8,128)(2,1)S(1)}, u32[]{:S(2)}, u32[]{:S(2)}) collective-permute-start(bf16[528,128]{1,0:T(8,128)(2,1)S(1)} %get-tuple-element.12), channel_id=1, source_target_pairs={{0,64},{64,0},{1,65},{65,1},{2,66},{66,2},{3,67},{67,3},{4,68},{68... | collective-permute-start | bytes 405512 | tf_op jit(solution)/shard_map/ppermute | solution.py:671
  4.6 0.7 constant_dynamic-update-slice_fusion.1
  5.3 0.7 constant_dynamic-update-slice_fusion.plan
  5.9 3.3 %collective-permute-done.theirs = bf16[528,128]{1,0:T(8,128)(2,1)S(1)} collective-permute-done((bf16[528,128]{1,0:T(8,128)(2,1)S(1)}, bf16[528,128]{1,0:T(8,128)(2,1)S(1)}, u32[]{:S(2)}, u32[]{:S(2)}) %collective-permute-start) | collective-permute-done | bytes 135200 | tf_op jit(solution)/shard_map/ppermute | solution.py:671
  9.3 3.2 %pack.1 = bf16[64,208,128]{2,1,0:T(8,128)(2,1)} custom-call(s32[512]{0:T(512)S(1)} %constant_dynamic-update-slice_fusion.plan, bf16[528,128]{1,0:T(8,128)(2,1)S(1)} %get-tuple-element.11.mine, bf16[528,128]{1,0:T(8,128)(2,1)S(1)} %collective-permute-done.theirs), custom_call_target="tpu_custom_call" | custom-call | tf_op jit(solution)/shard_map/pack/pallas_call | solution.py:213
  12.5 10.9 %all-to-all-start = ((bf16[64,208,128]{2,1,0:T(8,128)(2,1)}), bf16[64,208,128]{2,1,0:T(8,128)(2,1)}, u32[]{:S(2)}, u32[]{:S(2)}) async-start(bf16[64,208,128]{2,1,0:T(8,128)(2,1)} %pack.1), calls=%async_computation | async-start | bytes 6815744 | tf_op jit(solution)/shard_map/all_to_all | solution.py:673
  23.3 0.0 copy-start.1
  23.4 4.2 %turn.1.flipped = bf16[3,4,1024,256]{3,2,1,0:T(8,128)(2,1)} custom-call(s32[512]{0:T(512)S(1)} %constant_dynamic-update-slice_fusion.plan, bf16[3,4,256,1024]{3,2,1,0:T(8,128)(2,1)} %basis.3), custom_call_target="tpu_custom_call" | custom-call | flops 1000000 | bytes 25165824 | tf_op jit(solution)/shard_map/turn/pallas_call | solution.py:265
  27.5 37.8 %all-to-all-done.window = bf16[64,208,128]{2,1,0:T(8,128)(2,1)} async-done(((bf16[64,208,128]{2,1,0:T(8,128)(2,1)}), bf16[64,208,128]{2,1,0:T(8,128)(2,1)}, u32[]{:S(2)}, u32[]{:S(2)}) %all-to-all-start) | async-done | bytes 3407904 | tf_op jit(solution)/shard_map/all_to_all | solution.py:673
  65.3 0.0 copy-done.1
  65.3 5.4 %batches.1 = bf16[64,208,128]{2,1,0:T(8,128)(2,1)S(1)} custom-call(s32[512]{0:T(512)S(1)} %constant_dynamic-update-slice_fusion.plan, f32[3,256]{1,0:T(4,128)S(1)} %copy-done.1, bf16[3,4,256,1024]{3,2,1,0:T(8,128)(2,1)} %basis.3, bf16[3,4,1024,256]{3,2,1,0:T(8,128)(2,1)} %turn.1.flipped, bf16[64,208,128]{2,1,0:T(8,128)(2,1)} %all-to-all-done.window), custom_call_target="tpu_custom_call" | custom-call | tf_op jit(solution)/shard_map/batches/pallas_call | solution.py:418
  70.7 56.7 %all_to_all.10.arrived = bf16[64,208,128]{2,1,0:T(8,128)(2,1)S(1)} all-to-all(bf16[64,208,128]{2,1,0:T(8,128)(2,1)S(1)} %batches.1), channel_id=1, replica_groups=mesh['h'=2,'xl'=2,'y'=4,'z'=4,'c'=2] {'xl','y','z','c'}, dimensions={0} | all-to-all | bytes 6815744 | tf_op jit(solution)/shard_map/all_to_all | solution.py:676
  127.3 3.6 %collect_other.1.sent = s16[528,128]{1,0:T(8,128)(2,1)S(1)} custom-call(s32[512]{0:T(512)S(1)} %constant_dynamic-update-slice_fusion.plan, bf16[64,208,128]{2,1,0:T(8,128)(2,1)S(1)} %all_to_all.10.arrived), custom_call_target="tpu_custom_call" | custom-call | flops 1000000 | bytes 4194304 | tf_op jit(solution)/shard_map/collect_other/pallas_call | solution.py:542
  131.0 2.4 %collective-permute-start.1 = (s16[528,128]{1,0:T(8,128)(2,1)S(1)}, s16[528,128]{1,0:T(8,128)(2,1)S(1)}, u32[]{:S(2)}, u32[]{:S(2)}) collective-permute-start(s16[528,128]{1,0:T(8,128)(2,1)S(1)} %collect_other.1.sent), channel_id=1, source_target_pairs={{0,64},{64,0},{1,65},{65,1},{2,66},{66,2},{3,67},{67,3},{4,68},{68... | collective-permute-start | bytes 405512 | tf_op jit(solution)/shard_map/ppermute | solution.py:679
  133.3 3.5 %collect_own.1 = (f32[520,128]{1,0:T(8,128)S(1)}, f32[4,8,128,128]{3,2,1,0:T(8,128)}) custom-call(s32[512]{0:T(512)S(1)} %constant_dynamic-update-slice_fusion.plan, bf16[64,208,128]{2,1,0:T(8,128)(2,1)S(1)} %all_to_all.10.arrived), custom_call_target="tpu_custom_call" | custom-call | flops 1000000 | bytes 4194304 | tf_op jit(solution)/shard_map/collect_own/pallas_call | solution.py:542
  136.9 1.4 collective-permute-done.1.theirs
  138.3 0.2 merge.1
  138.5 4.6 %collective-permute-start.2 = (s16[272,128]{1,0:T(8,128)(2,1)S(1)}, s16[272,128]{1,0:T(8,128)(2,1)S(1)}, u32[]{:S(2)}, u32[]{:S(2)}) collective-permute-start(s16[272,128]{1,0:T(8,128)(2,1)S(1)} %get-tuple-element.17), channel_id=1, source_target_pairs={{0,0},{1,8},{2,16},{3,24},{4,32},{5,40},{6,48},{7,56},{8,65},{9,9}... | collective-permute-start | bytes 208904 | tf_op jit(solution)/shard_map/ppermute | solution.py:682
  143.1 5.8 %collective-permute-start.3 = (s16[272,128]{1,0:T(8,128)(2,1)S(1)}, s16[272,128]{1,0:T(8,128)(2,1)S(1)}, u32[]{:S(2)}, u32[]{:S(2)}) collective-permute-start(s16[272,128]{1,0:T(8,128)(2,1)S(1)} %get-tuple-element.18), channel_id=1, source_target_pairs={{0,0},{8,1},{16,2},{24,3},{32,4},{40,5},{48,6},{56,7},{65,8},{9,9}... | collective-permute-start | bytes 208904 | tf_op jit(solution)/shard_map/ppermute | solution.py:683
  148.9 0.5 slice.3
  150.1 0.0 collective-permute-done.2.got_upper
  150.1 4.5 %collective-permute-done.3.got_lower = s16[272,128]{1,0:T(8,128)(2,1)S(1)} collective-permute-done((s16[272,128]{1,0:T(8,128)(2,1)S(1)}, s16[272,128]{1,0:T(8,128)(2,1)S(1)}, u32[]{:S(2)}, u32[]{:S(2)}) %collective-permute-start.3) | collective-permute-done | bytes 69664 | tf_op jit(solution)/shard_map/ppermute | solution.py:683
  154.6 1.3 place.1
  (1 shorter events, 0.0 us)
Async XLA Ops:
  0.6 1.2 copy-start
  2.4 6.9 %collective-permute-start = (bf16[528,128]{1,0:T(8,128)(2,1)S(1)}, bf16[528,128]{1,0:T(8,128)(2,1)S(1)}, u32[]{:S(2)}, u32[]{:S(2)}) collective-permute-start(bf16[528,128]{1,0:T(8,128)(2,1)S(1)} %get-tuple-element.12), channel_id=1, source_target_pairs={{0,64},{64,0},{1,65},{65,1},{2,66},{66,2},{3,67},{67,3},{4,68},{68... | collective-permute-start | bytes 405512 | tf_op jit(solution)/shard_map/ppermute | solution.py:671
  12.5 52.8 %all-to-all-start = ((bf16[64,208,128]{2,1,0:T(8,128)(2,1)}), bf16[64,208,128]{2,1,0:T(8,128)(2,1)}, u32[]{:S(2)}, u32[]{:S(2)}) async-start(bf16[64,208,128]{2,1,0:T(8,128)(2,1)} %pack.1), calls=%async_computation | async-start | bytes 6815744 | tf_op jit(solution)/shard_map/all_to_all | solution.py:673
  23.3 42.0 %copy-start.1 = (f32[3,256]{1,0:T(4,128)S(1)}, f32[3,256]{1,0:T(4,128)}, u32[]{:S(2)}) copy-start(f32[3,256]{1,0:T(4,128)} %weights.1) | copy-start | bytes 9220
  131.0 7.3 %collective-permute-start.1 = (s16[528,128]{1,0:T(8,128)(2,1)S(1)}, s16[528,128]{1,0:T(8,128)(2,1)S(1)}, u32[]{:S(2)}, u32[]{:S(2)}) collective-permute-start(s16[528,128]{1,0:T(8,128)(2,1)S(1)} %collect_other.1.sent), channel_id=1, source_target_pairs={{0,64},{64,0},{1,65},{65,1},{2,66},{66,2},{3,67},{67,3},{4,68},{68... | collective-permute-start | bytes 405512 | tf_op jit(solution)/shard_map/ppermute | solution.py:679
  138.5 11.5 %collective-permute-start.2 = (s16[272,128]{1,0:T(8,128)(2,1)S(1)}, s16[272,128]{1,0:T(8,128)(2,1)S(1)}, u32[]{:S(2)}, u32[]{:S(2)}) collective-permute-start(s16[272,128]{1,0:T(8,128)(2,1)S(1)} %get-tuple-element.17), channel_id=1, source_target_pairs={{0,0},{1,8},{2,16},{3,24},{4,32},{5,40},{6,48},{7,56},{8,65},{9,9}... | collective-permute-start | bytes 208904 | tf_op jit(solution)/shard_map/ppermute | solution.py:682
  143.1 11.5 %collective-permute-start.3 = (s16[272,128]{1,0:T(8,128)(2,1)S(1)}, s16[272,128]{1,0:T(8,128)(2,1)S(1)}, u32[]{:S(2)}, u32[]{:S(2)}) collective-permute-start(s16[272,128]{1,0:T(8,128)(2,1)S(1)} %get-tuple-element.18), channel_id=1, source_target_pairs={{0,0},{8,1},{16,2},{24,3},{32,4},{40,5},{48,6},{56,7},{65,8},{9,9}... | collective-permute-start | bytes 208904 | tf_op jit(solution)/shard_map/ppermute | solution.py:683

commit v6 on v5

--- a/solution.py
+++ b/solution.py
@@ -58,14 +58,6 @@
     return jnp.concatenate([top, jnp.where(c < HB, flip[HB:], corner)], axis=0)
 
 
-def split_symmetric(packed, row):
-    r, c = lanes((HB, BF))
-    low = jnp.where((c >= HB) & (c - HB < r), pltpu.roll(packed, HB, 1), 0.0)
-    first = [jnp.where((c >= HB) | (r <= c), packed, 0.0), jnp.where(c - HB == r, row, low)]
-    second = [jnp.where((c >= HB) | (r < c), packed, 0.0), low]
-    return jnp.concatenate(first, axis=0), jnp.concatenate(second, axis=0)
-
-
 def pick_row(rows, index):
     r, _ = lanes(rows.shape)
     return jnp.sum(jnp.where(r == index, rows, 0.0), axis=0, keepdims=True)
@@ -155,7 +147,7 @@
             pltpu.VMEM((TURNS, BF, BF), BF16),
             pltpu.SemaphoreType.DMA((2 * TURNS,)),
         ],
-        compiler_params=limit(4),
+        compiler_params=limit(60),
         name="share",
     )(density)
 
@@ -229,15 +221,12 @@
     )(plan, mine, theirs)
 
 
-def turn_kernel(plan, basis, out, held, turned, sem_in, sem_out):
+def turn_kernel(plan, basis, out, held, sems):
     row_id, col_id, _ = position()
     count = live(plan, row_id * N_COL + col_id)
 
     def load(slot):
-        return pltpu.make_async_copy(basis.at[slot], held.at[slot], sem_in.at[slot])
-
-    def store(slot):
-        return pltpu.make_async_copy(turned.at[slot], out.at[slot], sem_out.at[slot])
+        return pltpu.make_async_copy(basis.at[slot], held.at[slot], sems.at[slot])
 
     def fetch(slot, carry):
         load(slot).start()
@@ -248,17 +237,11 @@
         for k in range(4):
             for o in range(KB):
                 span = slice(o * BF, (o + 1) * BF)
-                turned[slot, k, span, :] = held[slot, k, :, span].T
-        store(slot).start()
-        return carry
-
-    def drain(slot, carry):
-        store(slot).wait()
+                out[slot, k, span, :] = held[slot, k, :, span].T
         return carry
 
     lax.fori_loop(0, count, fetch, 0)
     lax.fori_loop(0, count, work, 0)
-    lax.fori_loop(0, count, drain, 0)
 
 
 def turn(plan, basis):
@@ -268,15 +251,13 @@
         grid_spec=scalars(
             1,
             [HBM],
-            HBM,
+            VMEM,
             [
                 pltpu.VMEM((SLOTS, 4, G, KF), BF16),
-                pltpu.VMEM((SLOTS, 4, KF, G), BF16),
-                pltpu.SemaphoreType.DMA((SLOTS,)),
                 pltpu.SemaphoreType.DMA((SLOTS,)),
             ],
         ),
-        compiler_params=limit(48),
+        compiler_params=limit(44),
         cost_estimate=pl.CostEstimate(flops=10**6, bytes_accessed=24 * MIB, transcendentals=0),
         name="turn",
     )(plan, basis)
@@ -287,72 +268,41 @@
 
 
 def batch_kernel(
-    plan, weights, basis, flipped, window, out,
-    phis, turned, win, win_ext, mat, corner, left, right, lines, sem_e, sem_w, sem_b, sem_t,
+    plan, weights, turned, window, out, mat, product, left, right, lines
 ):
     row_id, col_id, _ = position()
     me = row_id * N_COL + col_id
     count = live(plan, me)
     row, lane = lanes((16, BF))
-    ext_copy = pltpu.make_async_copy(window.at[:, pl.ds(EXT, 16)], win_ext, sem_e)
-
-    def window_copy(slot):
-        span = pl.ds(pl.multiple_of(slot * HB, HB), HB)
-        return pltpu.make_async_copy(window.at[:, span], win.at[slot], sem_w.at[slot])
-
-    def basis_copy(slot):
-        return pltpu.make_async_copy(basis.at[slot], phis.at[slot], sem_b.at[slot])
-
-    def flipped_copy(slot):
-        return pltpu.make_async_copy(flipped.at[slot], turned.at[slot], sem_t.at[slot])
-
-    def fetch(slot, carry):
-        window_copy(slot).start()
-        basis_copy(slot).start()
-        flipped_copy(slot).start()
-        return carry
-
-    ext_copy.start()
-    lax.fori_loop(0, count, fetch, 0)
     lines[...] = jnp.zeros(lines.shape, F32)
-    for t in range(4):
-        lo = 256 * t
-        mat[lo + BF : lo + 256, lo : lo + BF] = jnp.zeros((BF, BF), BF16)
-        corner[t, BF:, :BF] = jnp.zeros((BF, BF), BF16)
-    ext_copy.wait()
 
     def work(slot, total):
         start = plan[me * SLOTS + slot]
         cls = [(start + o) & (KB - 1) for o in range(KB)]
         span = pl.ds(pl.multiple_of(slot * HB, HB), HB)
-        window_copy(slot).wait()
         for o1 in range(KB):
-            r1, t, c1 = o1 * BF, o1 // 2, o1 % 2 * BF
+            r1 = slice(o1 * BF, (o1 + 1) * BF)
             for o2 in range(o1 + 1, KB):
-                top = win[slot, cls[o1] * KB + cls[o2]]
-                bottom = win[slot, cls[o2] * KB + cls[o1]]
-                mat[r1 : r1 + HB, o2 * BF : (o2 + 1) * BF] = top
-                mat[r1 + HB : r1 + BF, o2 * BF : (o2 + 1) * BF] = bottom
-                if o2 == o1 + 1 and o1 % 2 == 0:
-                    corner[t, :HB, BF:] = top
-                    corner[t, HB:BF, BF:] = bottom
+                r2 = slice(o2 * BF, (o2 + 1) * BF)
+                top = window[cls[o1] * KB + cls[o2], span, :]
+                bottom = window[cls[o2] * KB + cls[o1], span, :]
+                block = jnp.concatenate([top, bottom], axis=0)
+                mat[r1, r2] = block
+                mat[r2, r1] = block.T
             diagonal = cls[o1] * (KB + 1)
-            line = pick_row(win_ext[diagonal].astype(F32), slot)
-            first, second = split_symmetric(win[slot, diagonal].astype(F32), line)
-            mat[r1 : r1 + BF, r1 : r1 + BF] = first.astype(BF16)
-            corner[t, c1 : c1 + BF, c1 : c1 + BF] = second.astype(BF16)
-        basis_copy(slot).wait()
-        sums = [jnp.zeros((G, BF), F32) for _ in range(4)]
+            line = pick_row(window[diagonal, EXT:, :].astype(F32), slot)
+            block = unpack_symmetric(window[diagonal, span, :].astype(F32), line)
+            mat[r1, r1] = block.astype(BF16)
         for t in range(4):
-            lo, hi = 256 * t, 256 * (t + 1)
-            product = jnp.dot(phis[slot, 0, :, :hi], mat[:hi, lo:hi], preferred_element_type=F32)
-            product += dot_nt(phis[slot, 0, :, lo:hi], corner[t])
-            if hi < KF:
-                product += dot_nt(phis[slot, 0, :, hi:], mat[lo:hi, hi:])
+            part = slice(256 * t, 256 * (t + 1))
+            product[part, :] = jnp.dot(mat[part, :], turned[slot, 0], preferred_element_type=F32)
+        sums = [jnp.zeros((8, G), F32) for _ in range(4)]
+        for t in range(KF // BF):
+            span_t = slice(t * BF, (t + 1) * BF)
             for k in range(4):
-                terms = phis[slot, k, :, lo:hi].astype(F32) * product
-                sums[k] += terms[:, :BF] + terms[:, BF:]
-        sums = [jnp.sum(x.T, axis=0, keepdims=True) for x in sums]
+                terms = turned[slot, k, span_t, :].astype(F32) * product[span_t, :]
+                sums[k] += jnp.sum(terms.reshape(BF // 8, 8, G), axis=0)
+        sums = [jnp.sum(x, axis=0, keepdims=True) for x in sums]
         rho = sums[0]
         grads = [2.0 * x for x in sums[1:]]
         sigma = grads[0] * grads[0] + grads[1] * grads[1] + grads[2] * grads[2]
@@ -372,7 +322,6 @@
         ws = 2.0 * quad * by_sigma
         total = total + jnp.sum(quad * point)
         coeffs = [wr] + [ws * x for x in grads]
-        flipped_copy(slot).wait()
         for t in range(4):
             lo, hi = 256 * t, 256 * (t + 1)
             phi = turned[slot, 0, lo:hi, :]
@@ -414,33 +363,25 @@
             out[peer, EXT:, :] = energy.astype(BF16)
 
 
-def batches(plan, weights, basis, flipped, window):
+def batches(plan, weights, flipped, window):
     return pl.pallas_call(
         batch_kernel,
         out_shape=jax.ShapeDtypeStruct((PEERS, ROWS, BF), BF16),
         grid_spec=scalars(
             1,
-            [VMEM, HBM, HBM, HBM],
+            [VMEM, VMEM, VMEM],
             VMEM,
             [
-                pltpu.VMEM((SLOTS, 4, G, KF), BF16),
-                pltpu.VMEM((SLOTS, 4, KF, G), BF16),
-                pltpu.VMEM((SLOTS, PEERS, HB, BF), BF16),
-                pltpu.VMEM((PEERS, 16, BF), BF16),
                 pltpu.VMEM((KF, KF), BF16),
-                pltpu.VMEM((4, 256, 256), BF16),
+                pltpu.VMEM((KF, G), F32),
                 pltpu.VMEM((KF, 2 * G), BF16),
                 pltpu.VMEM((KF, 2 * G), BF16),
                 pltpu.VMEM((KB, 16, BF), F32),
-                pltpu.SemaphoreType.DMA,
-                pltpu.SemaphoreType.DMA((SLOTS,)),
-                pltpu.SemaphoreType.DMA((SLOTS,)),
-                pltpu.SemaphoreType.DMA((SLOTS,)),
             ],
         ),
-        compiler_params=limit(48),
+        compiler_params=limit(28),
         name="batches",
-    )(plan, weights, basis, flipped, window)
+    )(plan, weights, flipped, window)
 
 
 STEP = math.log(2.0) / 128.0
@@ -672,7 +613,7 @@
     packed = pack(plan, held, theirs)
     window = lax.all_to_all(packed, GROUP, split_axis=0, concat_axis=0, tiled=True)
 
-    outgoing = batches(plan, weights, basis, turn(plan, basis), window)
+    outgoing = batches(plan, weights, turn(plan, basis), window)
     arrived = lax.all_to_all(outgoing, GROUP, split_axis=0, concat_axis=0, tiled=True)
 
     sent = collect(1, plan, arrived)

time: 157 us -> 157 us (level)
  local copies, waits for them, and re-layouts: 3.1 us -> 8.21 us
  Pallas kernels: 21.9 us -> 19.5 us
  blocking collectives: 56.7 us -> 54.4 us
    unnamed x5 -> x9, local copies, waits for them, and re-layouts: 1.92 us -> 7.03 us
    all_to_all x1, blocking collectives: 56.7 us -> 54.4 us  [shards(): lax.all_to_all(outgoing, GROUP, split_axis=0, concat_axis=0, tiled=True)]
    pallas_call x1, Pallas kernels: 5.37 us -> 3.15 us  [batches(): pl.pallas_call(batch_kernel, out_shape=jax.ShapeDtypeStruct((PEERS, ROWS,...]
  transfers between devices with their start and end apart: 5 -> 5, of which waited for: 4 -> 4; matrix products, arithmetic and copies ran while one was open for 1% -> 1% of each run, Pallas kernels for 5% -> 4%
where the time goes in v6:
time: 157 us
  blocking collectives  54.4 us (35%)
  waiting for transfers between devices  46 us (29%)
  starting transfers between devices  26.6 us (17%)
  Pallas kernels  19.5 us (12%)
  local copies, waits for them, and re-layouts  8.21 us (5%)
  between operations  2.53 us (2%)
    all_to_all x1, blocking collectives, shards(): lax.all_to_all(outgoing, GROUP, split_axis=0, concat_axis=0, tiled=True)  54.4 us
    all_to_all x1, waiting for transfers between devices, shards(): lax.all_to_all(packed, GROUP, split_axis=0, concat_axis=0, tiled=True)  36.5 us
    all_to_all x1, starting transfers between devices, shards(): lax.all_to_all(packed, GROUP, split_axis=0, concat_axis=0, tiled=True)  10.7 us
    pallas_call x2, Pallas kernels, collect(): pl.pallas_call(functools.partial(collect_kernel, which), out_shape=out_sh...  7.16 us
    unnamed x9, local copies, waits for them, and re-layouts  7.03 us
    ppermute x2, starting transfers between devices, shards(): theirs = lax.ppermute(sent, 'h', swap)  5.58 us
    ppermute x1, starting transfers between devices, shards(): got_upper = lax.ppermute(up_words, ALL, there)  5.51 us
    ppermute x1, waiting for transfers between devices, shards(): got_lower = lax.ppermute(low_words, ALL, [(d, s) for s, d in there])  5.44 us
  transfers between devices with their start and end apart: 5, of which 4 were waited for; matrix products, arithmetic and copies ran while one was open for 1% of the time, Pallas kernels for 4%

profile of v6, /device:TPU:18, one launch (start us, length us, event | category | flops | bytes accessed | tf_op | source)
XLA Modules:
  0.0 157.2 jit_solution(5614930977489420567)
XLA Ops:
  0.6 1.8 %share.1 = (bf16[528,128]{1,0:T(8,128)(2,1)}, bf16[528,128]{1,0:T(8,128)(2,1)}) custom-call(bf16[4,8,128,128]{3,2,1,0:T(8,128)(2,1)} %density.1), custom_call_target="tpu_custom_call" | custom-call | tf_op jit(solution)/shard_map/share/pallas_call | solution.py:140
  2.4 2.2 %collective-permute-start = (bf16[528,128]{1,0:T(8,128)(2,1)}, bf16[528,128]{1,0:T(8,128)(2,1)S(1)}, u32[]{:S(2)}, u32[]{:S(2)}) collective-permute-start(bf16[528,128]{1,0:T(8,128)(2,1)} %get-tuple-element.12), channel_id=1, source_target_pairs={{0,64},{64,0},{1,65},{65,1},{2,66},{66,2},{3,67},{67,3},{4,68},{68... | collective-permute-start | bytes 405512 | tf_op jit(solution)/shard_map/ppermute | solution.py:612
  4.6 0.7 constant_dynamic-update-slice_fusion.1
  5.3 0.7 constant_dynamic-update-slice_fusion.plan
  6.0 3.5 %collective-permute-done.theirs = bf16[528,128]{1,0:T(8,128)(2,1)S(1)} collective-permute-done((bf16[528,128]{1,0:T(8,128)(2,1)}, bf16[528,128]{1,0:T(8,128)(2,1)S(1)}, u32[]{:S(2)}, u32[]{:S(2)}) %collective-permute-start) | collective-permute-done | bytes 135200 | tf_op jit(solution)/shard_map/ppermute | solution.py:612
  9.5 0.0 copy-start.2
  9.5 0.9 copy-done.2
  10.4 3.1 %pack.1 = bf16[64,208,128]{2,1,0:T(8,128)(2,1)} custom-call(s32[512]{0:T(512)S(1)} %constant_dynamic-update-slice_fusion.plan, bf16[528,128]{1,0:T(8,128)(2,1)S(1)} %copy-done.2, bf16[528,128]{1,0:T(8,128)(2,1)S(1)} %collective-permute-done.theirs), custom_call_target="tpu_custom_call" | custom-call | tf_op jit(solution)/shard_map/pack/pallas_call | solution.py:205
  13.6 10.7 %all-to-all-start = ((bf16[64,208,128]{2,1,0:T(8,128)(2,1)}), bf16[64,208,128]{2,1,0:T(8,128)(2,1)S(1)}, u32[]{:S(2)}, u32[]{:S(2)}) async-start(bf16[64,208,128]{2,1,0:T(8,128)(2,1)} %pack.1), calls=%async_computation | async-start | bytes 6815744 | tf_op jit(solution)/shard_map/all_to_all | solution.py:614
  24.3 0.0 copy-start.3
  24.3 2.8 %turn.1.turned = bf16[3,4,1024,256]{3,2,1,0:T(8,128)(2,1)S(1)} custom-call(s32[512]{0:T(512)S(1)} %constant_dynamic-update-slice_fusion.plan, bf16[3,4,256,1024]{3,2,1,0:T(8,128)(2,1)} %basis.1), custom_call_target="tpu_custom_call" | custom-call | flops 1000000 | bytes 25165824 | tf_op jit(solution)/shard_map/turn/pallas_call | solution.py:248
  27.1 0.0 copy-start
  27.1 2.6 %copy-done = bf16[3,4,1024,256]{3,2,1,0:T(8,128)(2,1)} copy-done((bf16[3,4,1024,256]{3,2,1,0:T(8,128)(2,1)}, bf16[3,4,1024,256]{3,2,1,0:T(8,128)(2,1)S(1)}, u32[]{:S(2)}) %copy-start) | copy-done | bytes 6291480
  29.8 36.5 %all-to-all-done.window = bf16[64,208,128]{2,1,0:T(8,128)(2,1)S(1)} async-done(((bf16[64,208,128]{2,1,0:T(8,128)(2,1)}), bf16[64,208,128]{2,1,0:T(8,128)(2,1)S(1)}, u32[]{:S(2)}, u32[]{:S(2)}) %all-to-all-start) | async-done | bytes 3407904 | tf_op jit(solution)/shard_map/all_to_all | solution.py:614
  66.3 0.0 copy-done.3
  66.3 0.0 copy-start.1
  66.3 2.8 %copy-done.1 = bf16[3,4,1024,256]{3,2,1,0:T(8,128)(2,1)S(1)} copy-done((bf16[3,4,1024,256]{3,2,1,0:T(8,128)(2,1)S(1)}, bf16[3,4,1024,256]{3,2,1,0:T(8,128)(2,1)}, u32[]{:S(2)}) %copy-start.1) | copy-done | bytes 6291480
  69.1 3.2 %batches.1 = bf16[64,208,128]{2,1,0:T(8,128)(2,1)S(1)} custom-call(s32[512]{0:T(512)S(1)} %constant_dynamic-update-slice_fusion.plan, f32[3,256]{1,0:T(4,128)S(1)} %copy-done.3, bf16[3,4,1024,256]{3,2,1,0:T(8,128)(2,1)S(1)} %copy-done.1, bf16[64,208,128]{2,1,0:T(8,128)(2,1)S(1)} %all-to-all-done.window), custom_call_target="tpu_custom_call" | custom-call | tf_op jit(solution)/shard_map/batches/pallas_call | solution.py:367
  72.3 54.4 %all_to_all.10.arrived = bf16[64,208,128]{2,1,0:T(8,128)(2,1)S(1)} all-to-all(bf16[64,208,128]{2,1,0:T(8,128)(2,1)S(1)} %batches.1), channel_id=1, replica_groups=mesh['h'=2,'xl'=2,'y'=4,'z'=4,'c'=2] {'xl','y','z','c'}, dimensions={0} | all-to-all | bytes 6815744 | tf_op jit(solution)/shard_map/all_to_all | solution.py:617
  126.6 3.6 %collect_other.1.sent = s16[528,128]{1,0:T(8,128)(2,1)S(1)} custom-call(s32[512]{0:T(512)S(1)} %constant_dynamic-update-slice_fusion.plan, bf16[64,208,128]{2,1,0:T(8,128)(2,1)S(1)} %all_to_all.10.arrived), custom_call_target="tpu_custom_call" | custom-call | flops 1000000 | bytes 4194304 | tf_op jit(solution)/shard_map/collect_other/pallas_call | solution.py:483
  130.2 3.3 %collective-permute-start.1 = (s16[528,128]{1,0:T(8,128)(2,1)S(1)}, s16[528,128]{1,0:T(8,128)(2,1)S(1)}, u32[]{:S(2)}, u32[]{:S(2)}) collective-permute-start(s16[528,128]{1,0:T(8,128)(2,1)S(1)} %collect_other.1.sent), channel_id=1, source_target_pairs={{0,64},{64,0},{1,65},{65,1},{2,66},{66,2},{3,67},{67,3},{4,68},{68... | collective-permute-start | bytes 405512 | tf_op jit(solution)/shard_map/ppermute | solution.py:620
  133.6 3.5 %collect_own.1 = (f32[520,128]{1,0:T(8,128)S(1)}, f32[4,8,128,128]{3,2,1,0:T(8,128)}) custom-call(s32[512]{0:T(512)S(1)} %constant_dynamic-update-slice_fusion.plan, bf16[64,208,128]{2,1,0:T(8,128)(2,1)S(1)} %all_to_all.10.arrived), custom_call_target="tpu_custom_call" | custom-call | flops 1000000 | bytes 4194304 | tf_op jit(solution)/shard_map/collect_own/pallas_call | solution.py:483
  137.1 0.5 collective-permute-done.1.theirs
  137.6 0.2 merge.1
  137.8 5.5 %collective-permute-start.2 = (s16[272,128]{1,0:T(8,128)(2,1)S(1)}, s16[272,128]{1,0:T(8,128)(2,1)S(1)}, u32[]{:S(2)}, u32[]{:S(2)}) collective-permute-start(s16[272,128]{1,0:T(8,128)(2,1)S(1)} %get-tuple-element.17), channel_id=1, source_target_pairs={{0,0},{1,8},{2,16},{3,24},{4,32},{5,40},{6,48},{7,56},{8,65},{9,9}... | collective-permute-start | bytes 208904 | tf_op jit(solution)/shard_map/ppermute | solution.py:623
  143.3 4.8 %collective-permute-start.3 = (s16[272,128]{1,0:T(8,128)(2,1)S(1)}, s16[272,128]{1,0:T(8,128)(2,1)S(1)}, u32[]{:S(2)}, u32[]{:S(2)}) collective-permute-start(s16[272,128]{1,0:T(8,128)(2,1)S(1)} %get-tuple-element.18), channel_id=1, source_target_pairs={{0,0},{8,1},{16,2},{24,3},{32,4},{40,5},{48,6},{56,7},{65,8},{9,9}... | collective-permute-start | bytes 208904 | tf_op jit(solution)/shard_map/ppermute | solution.py:624
  148.2 0.5 slice.3
  149.3 0.0 collective-permute-done.2.got_upper
  149.4 5.4 %collective-permute-done.3.got_lower = s16[272,128]{1,0:T(8,128)(2,1)S(1)} collective-permute-done((s16[272,128]{1,0:T(8,128)(2,1)S(1)}, s16[272,128]{1,0:T(8,128)(2,1)S(1)}, u32[]{:S(2)}, u32[]{:S(2)}) %collective-permute-start.3) | collective-permute-done | bytes 69664 | tf_op jit(solution)/shard_map/ppermute | solution.py:624
  154.8 1.3 place.1
  (1 shorter events, 0.0 us)
Async XLA Ops:
  2.4 7.1 %collective-permute-start = (bf16[528,128]{1,0:T(8,128)(2,1)}, bf16[528,128]{1,0:T(8,128)(2,1)S(1)}, u32[]{:S(2)}, u32[]{:S(2)}) collective-permute-start(bf16[528,128]{1,0:T(8,128)(2,1)} %get-tuple-element.12), channel_id=1, source_target_pairs={{0,64},{64,0},{1,65},{65,1},{2,66},{66,2},{3,67},{67,3},{4,68},{68... | collective-permute-start | bytes 405512 | tf_op jit(solution)/shard_map/ppermute | solution.py:612
  9.5 0.9 copy-start.2
  13.6 52.7 %all-to-all-start = ((bf16[64,208,128]{2,1,0:T(8,128)(2,1)}), bf16[64,208,128]{2,1,0:T(8,128)(2,1)S(1)}, u32[]{:S(2)}, u32[]{:S(2)}) async-start(bf16[64,208,128]{2,1,0:T(8,128)(2,1)} %pack.1), calls=%async_computation | async-start | bytes 6815744 | tf_op jit(solution)/shard_map/all_to_all | solution.py:614
  24.3 42.0 %copy-start.3 = (f32[3,256]{1,0:T(4,128)S(1)}, f32[3,256]{1,0:T(4,128)}, u32[]{:S(2)}) copy-start(f32[3,256]{1,0:T(4,128)} %weights.1) | copy-start | bytes 9220
  27.1 2.7 %copy-start = (bf16[3,4,1024,256]{3,2,1,0:T(8,128)(2,1)}, bf16[3,4,1024,256]{3,2,1,0:T(8,128)(2,1)S(1)}, u32[]{:S(2)}) copy-start(bf16[3,4,1024,256]{3,2,1,0:T(8,128)(2,1)S(1)} %turn.1.turned) | copy-start | bytes 18874372
  66.3 2.8 %copy-start.1 = (bf16[3,4,1024,256]{3,2,1,0:T(8,128)(2,1)S(1)}, bf16[3,4,1024,256]{3,2,1,0:T(8,128)(2,1)}, u32[]{:S(2)}) copy-start(bf16[3,4,1024,256]{3,2,1,0:T(8,128)(2,1)} %copy-done) | copy-start | bytes 18874372
  130.2 7.3 %collective-permute-start.1 = (s16[528,128]{1,0:T(8,128)(2,1)S(1)}, s16[528,128]{1,0:T(8,128)(2,1)S(1)}, u32[]{:S(2)}, u32[]{:S(2)}) collective-permute-start(s16[528,128]{1,0:T(8,128)(2,1)S(1)} %collect_other.1.sent), channel_id=1, source_target_pairs={{0,64},{64,0},{1,65},{65,1},{2,66},{66,2},{3,67},{67,3},{4,68},{68... | collective-permute-start | bytes 405512 | tf_op jit(solution)/shard_map/ppermute | solution.py:620
  137.8 11.5 %collective-permute-start.2 = (s16[272,128]{1,0:T(8,128)(2,1)S(1)}, s16[272,128]{1,0:T(8,128)(2,1)S(1)}, u32[]{:S(2)}, u32[]{:S(2)}) collective-permute-start(s16[272,128]{1,0:T(8,128)(2,1)S(1)} %get-tuple-element.17), channel_id=1, source_target_pairs={{0,0},{1,8},{2,16},{3,24},{4,32},{5,40},{6,48},{7,56},{8,65},{9,9}... | collective-permute-start | bytes 208904 | tf_op jit(solution)/shard_map/ppermute | solution.py:623
  143.3 11.5 %collective-permute-start.3 = (s16[272,128]{1,0:T(8,128)(2,1)S(1)}, s16[272,128]{1,0:T(8,128)(2,1)S(1)}, u32[]{:S(2)}, u32[]{:S(2)}) collective-permute-start(s16[272,128]{1,0:T(8,128)(2,1)S(1)} %get-tuple-element.18), channel_id=1, source_target_pairs={{0,0},{8,1},{16,2},{24,3},{32,4},{40,5},{48,6},{56,7},{65,8},{9,9}... | collective-permute-start | bytes 208904 | tf_op jit(solution)/shard_map/ppermute | solution.py:624

commit v7 on v6

--- a/solution.py
+++ b/solution.py
@@ -81,7 +81,7 @@
     other = ((i >> 3) & 1) ^ h
     turn = i >> 4
     below = jnp.where(j < i, TURNS, 0)
-    return other, turn, pl.multiple_of((below + turn) * HB, HB)
+    return other, turn, below + turn
 
 
 def scalars(count, in_specs, out_specs, scratch_shapes=()):
@@ -147,48 +147,98 @@
             pltpu.VMEM((TURNS, BF, BF), BF16),
             pltpu.SemaphoreType.DMA((2 * TURNS,)),
         ],
-        compiler_params=limit(60),
+        compiler_params=limit(4),
         name="share",
     )(density)
 
 
 CHUNK = 8
-
-
-def pack_kernel(plan, mine, theirs, out, table, lines, buf, sems):
+ALL_SLOTS = PEERS * SLOTS
+BOUNDS = 2 * ALL_SLOTS
+STRIDE = 16
+
+
+def route_kernel(plan, table):
     where = position()
-    on_diagonal = ((where[1] - where[0]) & (KB - 1)) == 0
-    table[0] = mine[:BAND, :]
-    table[1] = theirs[:BAND, :]
-    lines[0] = mine[BAND:, :].astype(F32)
-    lines[1] = theirs[BAND:, :].astype(F32)
+
+    def one_peer(peer, ends):
+        count = live(plan, where[2] * PEERS + peer)
+
+        @pl.when((peer & (CHUNK - 1)) == 0)
+        def _():
+            for which in range(2):
+                table[BOUNDS + which * STRIDE + peer // CHUNK] = ends[which]
+
+        for slot in range(SLOTS):
+            other, _, at = entry(plan, peer, slot, where)
+            used = jnp.where(slot < count, 1, 0)
+            index = jnp.where(other == 1, ends[1], ALL_SLOTS + ends[0])
+            table[index] = peer + slot * PEERS + at * (4 * PEERS)
+            ends = (ends[0] + used * (1 - other), ends[1] + used * other)
+        return ends
+
+    ends = lax.fori_loop(0, PEERS, one_peer, (jnp.int32(0), jnp.int32(0)))
+    for which in range(2):
+        table[BOUNDS + which * STRIDE + PEERS // CHUNK] = ends[which]
+
+
+def route(plan):
+    return pl.pallas_call(
+        route_kernel,
+        out_shape=jax.ShapeDtypeStruct((BOUNDS + 2 * STRIDE,), jnp.int32),
+        grid_spec=scalars(1, [], pl.BlockSpec(memory_space=pltpu.SMEM)),
+        compiler_params=limit(4),
+        cost_estimate=pl.CostEstimate(flops=10**6, bytes_accessed=4 * MIB, transcendentals=0),
+        name="route",
+    )(plan)
+
+
+def first_of(table, which, chunk):
+    return table[BOUNDS + which * STRIDE + chunk]
+
+
+def walk(table, which, low, high, body):
+    base = 0 if which else ALL_SLOTS
+
+    def step(index, carry):
+        code = table[base + index]
+        slot = (code >> 6) & 3
+        at = pl.multiple_of((code >> 8) * HB, HB)
+        body(code & (PEERS - 1), pl.multiple_of(slot * HB, HB), at, slot)
+        return carry
+
+    lax.fori_loop(low, high, step, 0)
+
+
+def pack_kernel(table, mine, theirs, out, buf, sems):
+    row_id, col_id, h = position()
     row, _ = lanes((16, BF))
+    held = (mine, theirs)
+
+    @pl.when(((col_id - row_id) & (KB - 1)) == 0)
+    def _():
+        ext = jnp.zeros((16, BF), F32)
+        for which in range(2):
+            lines = held[which][BAND:, :].astype(F32)
+            for turn in range(TURNS):
+                at = 2 * turn + (h ^ which)
+                ext = jnp.where(row == at, lines[turn : turn + 1, :], ext)
+        ext = ext.astype(BF16)
+        for peer in range(PEERS):
+            buf[peer, EXT:, :] = ext
 
     def send(chunk):
         span = pl.ds(pl.multiple_of(chunk * CHUNK, CHUNK), CHUNK)
         return pltpu.make_async_copy(buf.at[span], out.at[span], sems.at[chunk])
 
     def one_chunk(chunk, carry):
-        for k in range(CHUNK):
-            peer = chunk * CHUNK + k
-            count = live(plan, where[2] * PEERS + peer)
-
-            def one(slot):
-                other, _, at = entry(plan, peer, slot, where)
-                buf[peer, slot * HB : (slot + 1) * HB, :] = table[other, pl.ds(at, HB), :]
-
-            one(0)
-            for slot in range(1, SLOTS):
-                pl.when(slot < count)(lambda slot=slot: one(slot))
-
-            @pl.when(on_diagonal)
-            def _():
-                ext = jnp.zeros((16, BF), F32)
-                for slot in range(SLOTS):
-                    other, turn, _ = entry(plan, peer, slot, where)
-                    ext = jnp.where(row == slot, lines[other, pl.ds(turn, 1), :], ext)
-                buf[peer, EXT:, :] = ext.astype(BF16)
-
+        for which in range(2):
+
+            def copy(peer, span, at, slot):
+                buf[peer, pl.ds(span, HB), :] = held[which][pl.ds(at, HB), :]
+
+            low, high = first_of(table, which, chunk), first_of(table, which, chunk + 1)
+            walk(table, which, low, high, copy)
         send(chunk).start()
         return carry
 
@@ -201,7 +251,7 @@
     lax.fori_loop(0, PEERS // CHUNK, drain, 0)
 
 
-def pack(plan, mine, theirs):
+def pack(table, mine, theirs):
     return pl.pallas_call(
         pack_kernel,
         out_shape=jax.ShapeDtypeStruct((PEERS, ROWS, BF), BF16),
@@ -210,23 +260,24 @@
             [VMEM, VMEM],
             HBM,
             [
-                pltpu.VMEM((2, BAND, BF), BF16),
-                pltpu.VMEM((2, 16, BF), F32),
                 pltpu.VMEM((PEERS, ROWS, BF), BF16),
                 pltpu.SemaphoreType.DMA((PEERS // CHUNK,)),
             ],
         ),
         compiler_params=limit(8),
         name="pack",
-    )(plan, mine, theirs)
-
-
-def turn_kernel(plan, basis, out, held, sems):
+    )(table, mine, theirs)
+
+
+def turn_kernel(plan, basis, out, held, turned, sem_in, sem_out):
     row_id, col_id, _ = position()
     count = live(plan, row_id * N_COL + col_id)
 
     def load(slot):
-        return pltpu.make_async_copy(basis.at[slot], held.at[slot], sems.at[slot])
+        return pltpu.make_async_copy(basis.at[slot], held.at[slot], sem_in.at[slot])
+
+    def store(slot):
+        return pltpu.make_async_copy(turned.at[slot], out.at[slot], sem_out.at[slot])
 
     def fetch(slot, carry):
         load(slot).start()
@@ -237,11 +288,17 @@
         for k in range(4):
             for o in range(KB):
                 span = slice(o * BF, (o + 1) * BF)
-                out[slot, k, span, :] = held[slot, k, :, span].T
+                turned[slot, k, span, :] = held[slot, k, :, span].T
+        store(slot).start()
+        return carry
+
+    def drain(slot, carry):
+        store(slot).wait()
         return carry
 
     lax.fori_loop(0, count, fetch, 0)
     lax.fori_loop(0, count, work, 0)
+    lax.fori_loop(0, count, drain, 0)
 
 
 def turn(plan, basis):
@@ -251,13 +308,15 @@
         grid_spec=scalars(
             1,
             [HBM],
-            VMEM,
+            HBM,
             [
                 pltpu.VMEM((SLOTS, 4, G, KF), BF16),
+                pltpu.VMEM((SLOTS, 4, KF, G), BF16),
+                pltpu.SemaphoreType.DMA((SLOTS,)),
                 pltpu.SemaphoreType.DMA((SLOTS,)),
             ],
         ),
-        compiler_params=limit(44),
+        compiler_params=limit(48),
         cost_estimate=pl.CostEstimate(flops=10**6, bytes_accessed=24 * MIB, transcendentals=0),
         name="turn",
     )(plan, basis)
@@ -268,18 +327,34 @@
 
 
 def batch_kernel(
-    plan, weights, turned, window, out, mat, product, left, right, lines
+    plan, weights, flipped, window, out, turned, mat, product, left, right, lines, sems
 ):
     row_id, col_id, _ = position()
     me = row_id * N_COL + col_id
     count = live(plan, me)
     row, lane = lanes((16, BF))
+
+    def flipped_copy(slot, k):
+        return pltpu.make_async_copy(flipped.at[slot, k], turned.at[slot, k], sems.at[slot, k])
+
+    def fetch(slot, carry):
+        for k in range(4):
+            flipped_copy(slot, k).start()
+        return carry
+
+    lax.fori_loop(0, count, fetch, 0)
     lines[...] = jnp.zeros(lines.shape, F32)
 
-    def work(slot, total):
+    def classes(slot):
         start = plan[me * SLOTS + slot]
-        cls = [(start + o) & (KB - 1) for o in range(KB)]
-        span = pl.ds(pl.multiple_of(slot * HB, HB), HB)
+        return start, [(start + o) & (KB - 1) for o in range(KB)]
+
+    def rows_of(slot):
+        return pl.ds(pl.multiple_of(slot * HB, HB), HB)
+
+    def assemble(slot):
+        start, cls = classes(slot)
+        span = rows_of(slot)
         for o1 in range(KB):
             r1 = slice(o1 * BF, (o1 + 1) * BF)
             for o2 in range(o1 + 1, KB):
@@ -290,12 +365,21 @@
                 mat[r1, r2] = block
                 mat[r2, r1] = block.T
             diagonal = cls[o1] * (KB + 1)
-            line = pick_row(window[diagonal, EXT:, :].astype(F32), slot)
+            line = pick_row(window[diagonal, EXT:, :].astype(F32), (start + o1) >> 3)
             block = unpack_symmetric(window[diagonal, span, :].astype(F32), line)
             mat[r1, r1] = block.astype(BF16)
+
+    assemble(0)
+
+    def work(slot, total):
+        _, cls = classes(slot)
+        span = rows_of(slot)
+        flipped_copy(slot, 0).wait()
         for t in range(4):
             part = slice(256 * t, 256 * (t + 1))
             product[part, :] = jnp.dot(mat[part, :], turned[slot, 0], preferred_element_type=F32)
+        for k in range(1, 4):
+            flipped_copy(slot, k).wait()
         sums = [jnp.zeros((8, G), F32) for _ in range(4)]
         for t in range(KF // BF):
             span_t = slice(t * BF, (t + 1) * BF)
@@ -348,6 +432,7 @@
                     else:
                         out[cls[o1] * KB + cls[o2], span, :] = block[:HB].astype(BF16)
                         out[cls[o2] * KB + cls[o1], span, :] = block[HB:].astype(BF16)
+        assemble(jnp.minimum(slot + 1, SLOTS - 1))
         return total
 
     total = jnp.full((16, BF), lax.fori_loop(0, count, work, jnp.float32(0.0)), F32)
@@ -369,17 +454,19 @@
         out_shape=jax.ShapeDtypeStruct((PEERS, ROWS, BF), BF16),
         grid_spec=scalars(
             1,
-            [VMEM, VMEM, VMEM],
+            [VMEM, HBM, VMEM],
             VMEM,
             [
+                pltpu.VMEM((SLOTS, 4, KF, G), BF16),
                 pltpu.VMEM((KF, KF), BF16),
                 pltpu.VMEM((KF, G), F32),
                 pltpu.VMEM((KF, 2 * G), BF16),
                 pltpu.VMEM((KF, 2 * G), BF16),
                 pltpu.VMEM((KB, 16, BF), F32),
+                pltpu.SemaphoreType.DMA((SLOTS, 4)),
             ],
         ),
-        compiler_params=limit(28),
+        compiler_params=limit(44),
         name="batches",
     )(plan, weights, flipped, window)
 
@@ -403,14 +490,13 @@
     return words.astype(F32) * jnp.exp(code.astype(F32) * STEP - math.log(FULL))
 
 
-def collect_kernel(which, plan, arrived, *refs):
-    where = position()
-    on_diagonal = ((where[1] - where[0]) & (KB - 1)) == 0
+def collect_kernel(which, table, arrived, *refs):
+    row_id, col_id, _ = position()
+    on_diagonal = ((col_id - row_id) & (KB - 1)) == 0
     row, lane = lanes((16, BF))
     eight, _ = lanes((8, BF))
     if which:
-        out, acc, energy = refs
-        energy[...] = jnp.zeros(energy.shape, F32)
+        out, acc = refs
     else:
         acc, blank, zeros, sems = refs
         zeros[...] = jnp.zeros(zeros.shape, F32)
@@ -418,36 +504,17 @@
         for fill in fills:
             fill.start()
     acc[...] = jnp.zeros(acc.shape, F32)
-
-    def one_chunk(chunk, carry):
-        for k in range(CHUNK):
-            peer = chunk * CHUNK + k
-            count = live(plan, where[2] * PEERS + peer)
-            if which:
-                energy[...] += arrived[peer, EXT:, :].astype(F32)
-
-            def one(slot, used):
-                other, turn, at = entry(plan, peer, slot, where)
-                wanted = other == which
-
-                @pl.when(wanted if used is None else wanted & used)
-                def _():
-                    part = arrived[peer, slot * HB : (slot + 1) * HB, :]
-                    acc[pl.ds(at, HB), :] += part.astype(F32)
-
-                    @pl.when(on_diagonal)
-                    def _():
-                        ext = arrived[peer, EXT:, :].astype(F32)
-                        line = jnp.where((row == slot) & (lane >= HB), ext, 0.0)
-                        line = jnp.sum(line, axis=0, keepdims=True)
-                        acc[BAND:, :] += jnp.where(eight == turn, line, 0.0)
-
-            one(0, None)
-            for slot in range(1, SLOTS):
-                one(slot, slot < count)
-        return carry
-
-    lax.fori_loop(0, PEERS // CHUNK, one_chunk, 0)
+    high = first_of(table, which, PEERS // CHUNK)
+
+    def add(peer, span, at, slot):
+        acc[pl.ds(at, HB), :] += arrived[peer, pl.ds(span, HB), :].astype(F32)
+
+    def add_line(peer, span, at, slot):
+        line = jnp.where(lane >= HB, arrived[peer, EXT:, :].astype(F32), 0.0)
+        acc[BAND:, :] += jnp.where(eight == at // HB, pick_row(line, slot), 0.0)
+
+    walk(table, which, 0, high, add)
+    pl.when(on_diagonal)(lambda: walk(table, which, 0, high, add_line))
     if not which:
         for fill in fills:
             fill.wait()
@@ -456,7 +523,8 @@
     words, code = encode(acc[BAND:, :])
     ext = jnp.concatenate([words, words], axis=0)
     ext = jnp.where(row == 7, code, ext)
-    total = jnp.where((row == 0) & (lane < 3), energy[...], 0.0)
+    total = jnp.sum(arrived[:, EXT:, :].astype(F32), axis=0)
+    total = jnp.where((row == 0) & (lane < 3), total, 0.0)
     total = jnp.sum(jnp.sum(total, axis=0, keepdims=True), axis=1, keepdims=True)
     words, code = encode(total)
     first = jnp.floor(words + 0.5)
@@ -470,12 +538,12 @@
     out[BAND:, :] = integer(jnp.floor(ext + 0.5))
 
 
-def collect(which, plan, arrived):
+def collect(which, table, arrived):
     acc = jax.ShapeDtypeStruct((BAND + 8, BF), F32)
     if which:
         out_shape = jax.ShapeDtypeStruct((BAND + 16, BF), jnp.int16)
         out_specs = VMEM
-        scratch = [pltpu.VMEM((BAND + 8, BF), F32), pltpu.VMEM((16, BF), F32)]
+        scratch = [pltpu.VMEM((BAND + 8, BF), F32)]
     else:
         out_shape = [acc, jax.ShapeDtypeStruct((TURNS, N_COL, BF, BF), F32)]
         out_specs = [VMEM, HBM]
@@ -487,7 +555,7 @@
         compiler_params=limit(8),
         cost_estimate=pl.CostEstimate(flops=10**6, bytes_accessed=4 * MIB, transcendentals=0),
         name=("collect_own", "collect_other")[which],
-    )(plan, arrived)
+    )(table, arrived)
 
 
 def merge_kernel(mine, sent, theirs, upper, lower, rest, up_words, low_words):
@@ -610,15 +678,16 @@
     plan = jnp.concatenate([batch_start, batch_count])
     held, sent = share(density)
     theirs = lax.ppermute(sent, "h", swap)
-    packed = pack(plan, held, theirs)
+    table = route(plan)
+    packed = pack(table, held, theirs)
     window = lax.all_to_all(packed, GROUP, split_axis=0, concat_axis=0, tiled=True)
 
     outgoing = batches(plan, weights, turn(plan, basis), window)
     arrived = lax.all_to_all(outgoing, GROUP, split_axis=0, concat_axis=0, tiled=True)
 
-    sent = collect(1, plan, arrived)
+    sent = collect(1, table, arrived)
     theirs = lax.ppermute(sent, "h", swap)
-    mine, blank = collect(0, plan, arrived)
+    mine, blank = collect(0, table, arrived)
     upper, lower, rest, up_words, low_words = merge(mine, sent, theirs)
     got_upper = lax.ppermute(up_words, ALL, there)
     got_lower = lax.ppermute(low_words, ALL, [(d, s) for s, d in there])

time: 157 us -> 152 us (0.968)
  local copies, waits for them, and re-layouts: 8.21 us -> 3.1 us
  starting transfers between devices: 26.6 us -> 24.7 us
    unnamed x9 -> x5, local copies, waits for them, and re-layouts: 7.03 us -> 1.92 us
    pallas_call x2, Pallas kernels: 7.16 us -> 3.29 us  [collect(): pl.pallas_call(functools.partial(collect_kernel, which), out_shape=out_sh...]
    pallas_call x0 -> x1, Pallas kernels: none -> 3.62 us  [route(): pl.pallas_call(route_kernel, out_shape=jax.ShapeDtypeStruct((BOUNDS + 2 *...]
  transfers between devices with their start and end apart: 5 -> 5, of which waited for: 4 -> 3; matrix products, arithmetic and copies ran while one was open for 1% -> 1% of each run, Pallas kernels for 4% -> 6%
where the time goes in v7:
time: 152 us; the launch traced here: 151 us
  blocking collectives  55.6 us (37%)
  waiting for transfers between devices  45.3 us (30%)
  starting transfers between devices  24.7 us (16%)
  Pallas kernels  20.2 us (13%)
  local copies, waits for them, and re-layouts  3.1 us (2%)
  between operations  2.54 us (2%)
    all_to_all x1, blocking collectives, shards(): lax.all_to_all(outgoing, GROUP, split_axis=0, concat_axis=0, tiled=True)  55.6 us
    all_to_all x1, waiting for transfers between devices, shards(): lax.all_to_all(packed, GROUP, split_axis=0, concat_axis=0, tiled=True)  37.8 us
    all_to_all x1, starting transfers between devices, shards(): lax.all_to_all(packed, GROUP, split_axis=0, concat_axis=0, tiled=True)  9.96 us
    ppermute x1, starting transfers between devices, shards(): got_lower = lax.ppermute(low_words, ALL, [(d, s) for s, d in there])  6.14 us
    pallas_call x1, Pallas kernels, batches(): pl.pallas_call(batch_kernel, out_shape=jax.ShapeDtypeStruct((PEERS, ROWS,...  4.4 us
    ppermute x2, starting transfers between devices, shards(): theirs = lax.ppermute(sent, 'h', swap)  4.36 us
    ppermute x1, waiting for transfers between devices, shards(): got_lower = lax.ppermute(low_words, ALL, [(d, s) for s, d in there])  4.25 us
    ppermute x1, starting transfers between devices, shards(): got_upper = lax.ppermute(up_words, ALL, there)  4.22 us
  transfers between devices with their start and end apart: 5, of which 3 were waited for; matrix products, arithmetic and copies ran while one was open for 1% of the time, Pallas kernels for 6%

profile of v7, /device:TPU:18, one launch (start us, length us, event | category | flops | bytes accessed | tf_op | source)
XLA Modules:
  0.0 151.5 jit_solution(12516702462304333580)
XLA Ops:
  0.6 0.0 copy-start
  0.6 1.2 copy-done
  1.9 0.5 share.1
  2.4 2.2 %collective-permute-start = (bf16[528,128]{1,0:T(8,128)(2,1)S(1)}, bf16[528,128]{1,0:T(8,128)(2,1)S(1)}, u32[]{:S(2)}, u32[]{:S(2)}) collective-permute-start(bf16[528,128]{1,0:T(8,128)(2,1)S(1)} %get-tuple-element.12), channel_id=1, source_target_pairs={{0,64},{64,0},{1,65},{65,1},{2,66},{66,2},{3,67},{67,3},{4,68},{68... | collective-permute-start | bytes 405512 | tf_op jit(solution)/shard_map/ppermute | solution.py:680
  4.6 0.7 constant_dynamic-update-slice_fusion.1
  5.3 0.7 constant_dynamic-update-slice_fusion.plan
  5.9 3.6 %route.1.table = s32[416]{0:T(512)S(1)} custom-call(s32[512]{0:T(512)S(1)} %constant_dynamic-update-slice_fusion.plan), custom_call_target="tpu_custom_call" | custom-call | flops 1000000 | bytes 4194304 | tf_op jit(solution)/shard_map/route/pallas_call | solution.py:186
  9.6 0.0 collective-permute-done.theirs
  9.6 2.7 %pack.1 = bf16[64,208,128]{2,1,0:T(8,128)(2,1)} custom-call(s32[416]{0:T(512)S(1)} %route.1.table, bf16[528,128]{1,0:T(8,128)(2,1)S(1)} %get-tuple-element.11.mine, bf16[528,128]{1,0:T(8,128)(2,1)S(1)} %collective-permute-done.theirs), custom_call_target="tpu_custom_call" | custom-call | tf_op jit(solution)/shard_map/pack/pallas_call | solution.py:255
  12.3 10.0 %all-to-all-start = ((bf16[64,208,128]{2,1,0:T(8,128)(2,1)}), bf16[64,208,128]{2,1,0:T(8,128)(2,1)S(1)}, u32[]{:S(2)}, u32[]{:S(2)}) async-start(bf16[64,208,128]{2,1,0:T(8,128)(2,1)} %pack.1), calls=%async_computation | async-start | bytes 6815744 | tf_op jit(solution)/shard_map/all_to_all | solution.py:683
  22.3 0.0 copy-start.1
  22.3 4.2 %turn.1.flipped = bf16[3,4,1024,256]{3,2,1,0:T(8,128)(2,1)} custom-call(s32[512]{0:T(512)S(1)} %constant_dynamic-update-slice_fusion.plan, bf16[3,4,256,1024]{3,2,1,0:T(8,128)(2,1)} %basis.1), custom_call_target="tpu_custom_call" | custom-call | flops 1000000 | bytes 25165824 | tf_op jit(solution)/shard_map/turn/pallas_call | solution.py:305
  26.5 37.8 %all-to-all-done.window = bf16[64,208,128]{2,1,0:T(8,128)(2,1)S(1)} async-done(((bf16[64,208,128]{2,1,0:T(8,128)(2,1)}), bf16[64,208,128]{2,1,0:T(8,128)(2,1)S(1)}, u32[]{:S(2)}, u32[]{:S(2)}) %all-to-all-start) | async-done | bytes 3407904 | tf_op jit(solution)/shard_map/all_to_all | solution.py:683
  64.3 0.0 copy-done.1
  64.3 4.4 %batches.1 = bf16[64,208,128]{2,1,0:T(8,128)(2,1)S(1)} custom-call(s32[512]{0:T(512)S(1)} %constant_dynamic-update-slice_fusion.plan, f32[3,256]{1,0:T(4,128)S(1)} %copy-done.1, bf16[3,4,1024,256]{3,2,1,0:T(8,128)(2,1)} %turn.1.flipped, bf16[64,208,128]{2,1,0:T(8,128)(2,1)S(1)} %all-to-all-done.window), custom_call_target="tpu_custom_call" | custom-call | tf_op jit(solution)/shard_map/batches/pallas_call | solution.py:452
  68.7 55.6 %all_to_all.10.arrived = bf16[64,208,128]{2,1,0:T(8,128)(2,1)S(1)} all-to-all(bf16[64,208,128]{2,1,0:T(8,128)(2,1)S(1)} %batches.1), channel_id=1, replica_groups=mesh['h'=2,'xl'=2,'y'=4,'z'=4,'c'=2] {'xl','y','z','c'}, dimensions={0} | all-to-all | bytes 6815744 | tf_op jit(solution)/shard_map/all_to_all | solution.py:686
  124.4 1.4 collect_other.1.sent
  125.7 2.2 %collective-permute-start.1 = (s16[528,128]{1,0:T(8,128)(2,1)S(1)}, s16[528,128]{1,0:T(8,128)(2,1)S(1)}, u32[]{:S(2)}, u32[]{:S(2)}) collective-permute-start(s16[528,128]{1,0:T(8,128)(2,1)S(1)} %collect_other.1.sent), channel_id=1, source_target_pairs={{0,64},{64,0},{1,65},{65,1},{2,66},{66,2},{3,67},{67,3},{4,68},{68... | collective-permute-start | bytes 405512 | tf_op jit(solution)/shard_map/ppermute | solution.py:689
  127.9 1.9 %collect_own.1 = (f32[520,128]{1,0:T(8,128)S(1)}, f32[4,8,128,128]{3,2,1,0:T(8,128)}) custom-call(s32[416]{0:T(512)S(1)} %route.1.table, bf16[64,208,128]{2,1,0:T(8,128)(2,1)S(1)} %all_to_all.10.arrived), custom_call_target="tpu_custom_call" | custom-call | flops 1000000 | bytes 4194304 | tf_op jit(solution)/shard_map/collect_own/pallas_call | solution.py:551
  129.8 3.2 %collective-permute-done.1.theirs = s16[528,128]{1,0:T(8,128)(2,1)S(1)} collective-permute-done((s16[528,128]{1,0:T(8,128)(2,1)S(1)}, s16[528,128]{1,0:T(8,128)(2,1)S(1)}, u32[]{:S(2)}, u32[]{:S(2)}) %collective-permute-start.1) | collective-permute-done | bytes 135200 | tf_op jit(solution)/shard_map/ppermute | solution.py:689
  133.0 0.2 merge.1
  133.3 4.2 %collective-permute-start.2 = (s16[272,128]{1,0:T(8,128)(2,1)S(1)}, s16[272,128]{1,0:T(8,128)(2,1)S(1)}, u32[]{:S(2)}, u32[]{:S(2)}) collective-permute-start(s16[272,128]{1,0:T(8,128)(2,1)S(1)} %get-tuple-element.17), channel_id=1, source_target_pairs={{0,0},{1,8},{2,16},{3,24},{4,32},{5,40},{6,48},{7,56},{8,65},{9,9}... | collective-permute-start | bytes 208904 | tf_op jit(solution)/shard_map/ppermute | solution.py:692
  137.5 6.1 %collective-permute-start.3 = (s16[272,128]{1,0:T(8,128)(2,1)S(1)}, s16[272,128]{1,0:T(8,128)(2,1)S(1)}, u32[]{:S(2)}, u32[]{:S(2)}) collective-permute-start(s16[272,128]{1,0:T(8,128)(2,1)S(1)} %get-tuple-element.18), channel_id=1, source_target_pairs={{0,0},{8,1},{16,2},{24,3},{32,4},{40,5},{48,6},{56,7},{65,8},{9,9}... | collective-permute-start | bytes 208904 | tf_op jit(solution)/shard_map/ppermute | solution.py:693
  143.6 0.5 slice.3
  144.8 0.0 collective-permute-done.2.got_upper
  144.8 4.3 %collective-permute-done.3.got_lower = s16[272,128]{1,0:T(8,128)(2,1)S(1)} collective-permute-done((s16[272,128]{1,0:T(8,128)(2,1)S(1)}, s16[272,128]{1,0:T(8,128)(2,1)S(1)}, u32[]{:S(2)}, u32[]{:S(2)}) %collective-permute-start.3) | collective-permute-done | bytes 69664 | tf_op jit(solution)/shard_map/ppermute | solution.py:693
  149.1 1.3 place.1
  (1 shorter events, 0.0 us)
Async XLA Ops:
  0.6 1.2 copy-start
  2.4 7.2 %collective-permute-start = (bf16[528,128]{1,0:T(8,128)(2,1)S(1)}, bf16[528,128]{1,0:T(8,128)(2,1)S(1)}, u32[]{:S(2)}, u32[]{:S(2)}) collective-permute-start(bf16[528,128]{1,0:T(8,128)(2,1)S(1)} %get-tuple-element.12), channel_id=1, source_target_pairs={{0,64},{64,0},{1,65},{65,1},{2,66},{66,2},{3,67},{67,3},{4,68},{68... | collective-permute-start | bytes 405512 | tf_op jit(solution)/shard_map/ppermute | solution.py:680
  12.3 52.0 %all-to-all-start = ((bf16[64,208,128]{2,1,0:T(8,128)(2,1)}), bf16[64,208,128]{2,1,0:T(8,128)(2,1)S(1)}, u32[]{:S(2)}, u32[]{:S(2)}) async-start(bf16[64,208,128]{2,1,0:T(8,128)(2,1)} %pack.1), calls=%async_computation | async-start | bytes 6815744 | tf_op jit(solution)/shard_map/all_to_all | solution.py:683
  22.3 42.0 %copy-start.1 = (f32[3,256]{1,0:T(4,128)S(1)}, f32[3,256]{1,0:T(4,128)}, u32[]{:S(2)}) copy-start(f32[3,256]{1,0:T(4,128)} %weights.1) | copy-start | bytes 9220
  125.7 7.3 %collective-permute-start.1 = (s16[528,128]{1,0:T(8,128)(2,1)S(1)}, s16[528,128]{1,0:T(8,128)(2,1)S(1)}, u32[]{:S(2)}, u32[]{:S(2)}) collective-permute-start(s16[528,128]{1,0:T(8,128)(2,1)S(1)} %collect_other.1.sent), channel_id=1, source_target_pairs={{0,64},{64,0},{1,65},{65,1},{2,66},{66,2},{3,67},{67,3},{4,68},{68... | collective-permute-start | bytes 405512 | tf_op jit(solution)/shard_map/ppermute | solution.py:689
  133.3 11.5 %collective-permute-start.2 = (s16[272,128]{1,0:T(8,128)(2,1)S(1)}, s16[272,128]{1,0:T(8,128)(2,1)S(1)}, u32[]{:S(2)}, u32[]{:S(2)}) collective-permute-start(s16[272,128]{1,0:T(8,128)(2,1)S(1)} %get-tuple-element.17), channel_id=1, source_target_pairs={{0,0},{1,8},{2,16},{3,24},{4,32},{5,40},{6,48},{7,56},{8,65},{9,9}... | collective-permute-start | bytes 208904 | tf_op jit(solution)/shard_map/ppermute | solution.py:692
  137.5 11.6 %collective-permute-start.3 = (s16[272,128]{1,0:T(8,128)(2,1)S(1)}, s16[272,128]{1,0:T(8,128)(2,1)S(1)}, u32[]{:S(2)}, u32[]{:S(2)}) collective-permute-start(s16[272,128]{1,0:T(8,128)(2,1)S(1)} %get-tuple-element.18), channel_id=1, source_target_pairs={{0,0},{8,1},{16,2},{24,3},{32,4},{40,5},{48,6},{56,7},{65,8},{9,9}... | collective-permute-start | bytes 208904 | tf_op jit(solution)/shard_map/ppermute | solution.py:693

commit v8 on v7

--- a/solution.py
+++ b/solution.py
@@ -69,13 +69,9 @@
     return row_id, lax.axis_index("z") * 2 + lax.axis_index("c"), h
 
 
-def live(plan, device):
-    return plan[N_ROW * N_COL * SLOTS + device]
-
-
-def entry(plan, peer, slot, where):
+def entry(starts, peer, slot, where):
     row_id, col_id, h = where
-    start = plan[(h * PEERS + peer) * SLOTS + slot]
+    start = starts[(h * PEERS + peer) * SLOTS + slot]
     i = start + ((row_id - start) & (KB - 1))
     j = start + ((col_id - start) & (KB - 1))
     other = ((i >> 3) & 1) ^ h
@@ -156,41 +152,49 @@
 ALL_SLOTS = PEERS * SLOTS
 BOUNDS = 2 * ALL_SLOTS
 STRIDE = 16
-
-
-def route_kernel(plan, table):
+OWN = BOUNDS + 2 * STRIDE
+
+
+def route_kernel(starts, counts, table):
     where = position()
-
-    def one_peer(peer, ends):
-        count = live(plan, where[2] * PEERS + peer)
-
-        @pl.when((peer & (CHUNK - 1)) == 0)
-        def _():
-            for which in range(2):
-                table[BOUNDS + which * STRIDE + peer // CHUNK] = ends[which]
-
-        for slot in range(SLOTS):
-            other, _, at = entry(plan, peer, slot, where)
-            used = jnp.where(slot < count, 1, 0)
-            index = jnp.where(other == 1, ends[1], ALL_SLOTS + ends[0])
-            table[index] = peer + slot * PEERS + at * (4 * PEERS)
-            ends = (ends[0] + used * (1 - other), ends[1] + used * other)
+    me = where[0] * N_COL + where[1]
+    for slot in range(SLOTS):
+        table[OWN + slot] = starts[me * SLOTS + slot]
+    table[OWN + SLOTS] = counts[me]
+
+    def one_chunk(chunk, ends):
+        for which in range(2):
+            table[BOUNDS + which * STRIDE + chunk] = ends[which]
+
+        for k in range(CHUNK):
+            peer = chunk * CHUNK + k
+
+            def one(slot, ends):
+                other, _, at = entry(starts, peer, slot, where)
+                index = jnp.where(other == 1, ends[1], ALL_SLOTS + ends[0])
+                table[index] = peer + slot * PEERS + at * (4 * PEERS)
+                return ends[0] + 1 - other, ends[1] + other
+
+            ends = one(0, ends)
+            ends = lax.fori_loop(1, counts[where[2] * PEERS + peer], one, ends)
         return ends
 
-    ends = lax.fori_loop(0, PEERS, one_peer, (jnp.int32(0), jnp.int32(0)))
+    ends = lax.fori_loop(0, PEERS // CHUNK, one_chunk, (jnp.int32(0), jnp.int32(0)))
     for which in range(2):
         table[BOUNDS + which * STRIDE + PEERS // CHUNK] = ends[which]
 
 
-def route(plan):
+def route(starts, counts):
+    scalar = pl.BlockSpec(memory_space=pltpu.SMEM)
     return pl.pallas_call(
         route_kernel,
-        out_shape=jax.ShapeDtypeStruct((BOUNDS + 2 * STRIDE,), jnp.int32),
-        grid_spec=scalars(1, [], pl.BlockSpec(memory_space=pltpu.SMEM)),
+        out_shape=jax.ShapeDtypeStruct((OWN + STRIDE,), jnp.int32),
+        in_specs=[scalar, scalar],
+        out_specs=scalar,
         compiler_params=limit(4),
         cost_estimate=pl.CostEstimate(flops=10**6, bytes_accessed=4 * MIB, transcendentals=0),
         name="route",
-    )(plan)
+    )(starts, counts)
 
 
 def first_of(table, which, chunk):
@@ -269,9 +273,8 @@
     )(table, mine, theirs)
 
 
-def turn_kernel(plan, basis, out, held, turned, sem_in, sem_out):
-    row_id, col_id, _ = position()
-    count = live(plan, row_id * N_COL + col_id)
+def turn_kernel(table, basis, out, held, turned, sem_in, sem_out):
+    count = table[OWN + SLOTS]
 
     def load(slot):
         return pltpu.make_async_copy(basis.at[slot], held.at[slot], sem_in.at[slot])
@@ -301,7 +304,7 @@
     lax.fori_loop(0, count, drain, 0)
 
 
-def turn(plan, basis):
+def turn(table, basis):
     return pl.pallas_call(
         turn_kernel,
         out_shape=jax.ShapeDtypeStruct((SLOTS, 4, KF, G), BF16),
@@ -319,7 +322,7 @@
         compiler_params=limit(48),
         cost_estimate=pl.CostEstimate(flops=10**6, bytes_accessed=24 * MIB, transcendentals=0),
         name="turn",
-    )(plan, basis)
+    )(table, basis)
 
 
 def dot_nt(x, y):
@@ -327,11 +330,9 @@
 
 
 def batch_kernel(
-    plan, weights, flipped, window, out, turned, mat, product, left, right, lines, sems
+    table, weights, flipped, window, out, turned, mat, product, left, right, lines, sems
 ):
-    row_id, col_id, _ = position()
-    me = row_id * N_COL + col_id
-    count = live(plan, me)
+    count = table[OWN + SLOTS]
     row, lane = lanes((16, BF))
 
     def flipped_copy(slot, k):
@@ -346,7 +347,7 @@
     lines[...] = jnp.zeros(lines.shape, F32)
 
     def classes(slot):
-        start = plan[me * SLOTS + slot]
+        start = table[OWN + slot]
         return start, [(start + o) & (KB - 1) for o in range(KB)]
 
     def rows_of(slot):
@@ -448,7 +449,7 @@
             out[peer, EXT:, :] = energy.astype(BF16)
 
 
-def batches(plan, weights, flipped, window):
+def batches(table, weights, flipped, window):
     return pl.pallas_call(
         batch_kernel,
         out_shape=jax.ShapeDtypeStruct((PEERS, ROWS, BF), BF16),
@@ -468,7 +469,7 @@
         ),
         compiler_params=limit(44),
         name="batches",
-    )(plan, weights, flipped, window)
+    )(table, weights, flipped, window)
 
 
 STEP = math.log(2.0) / 128.0
@@ -558,7 +559,7 @@
     )(table, arrived)
 
 
-def merge_kernel(mine, sent, theirs, upper, lower, rest, up_words, low_words):
+def merge_kernel(mine, sent, theirs, upper, lower, rest, near, far):
     eight, _ = lanes((8, BF))
     row, _ = lanes((16, BF))
     got = theirs[BAND:, :].astype(F32)
@@ -572,17 +573,24 @@
 
     more = jnp.where(eight < TURNS, decode(got[:8, :], line(got, 7)), 0.0)
     rest[...] = jnp.where(eight == TURNS, energy(own) + energy(got), mine[BAND:, :] + more)
-    for low, full, words in ((0, upper, up_words), (1, lower, low_words)):
-        codes = jnp.zeros((16, BF), F32)
-        for t in range(TURNS):
+    row_id, col_id, _ = position()
+    ahead = (row_id & (KB - 1)) < col_id
+    codes = [jnp.zeros((16, BF), F32)] * 2
+    for t in range(TURNS):
+        span = slice(t * HB, (t + 1) * HB)
+        words = []
+        for low, full in ((0, upper), (1, lower)):
             k = low * TURNS + t
-            span = slice(k * HB, (k + 1) * HB)
-            total = mine[span, :] + decode(theirs[span, :].astype(F32), line(got, 8 + k))
-            full[t * HB : (t + 1) * HB, :] = total
+            whole = slice(k * HB, (k + 1) * HB)
+            total = mine[whole, :] + decode(theirs[whole, :].astype(F32), line(got, 8 + k))
+            full[span, :] = total
             scaled, code = encode(total)
-            words[t * HB : (t + 1) * HB, :] = integer(jnp.floor(scaled + 0.5))
-            codes = jnp.where(row == t, code, codes)
-        words[TURNS * HB :, :] = integer(jnp.floor(codes + 0.5))
+            words.append(scaled)
+            codes[low] = jnp.where(row == t, code, codes[low])
+        near[span, :] = integer(jnp.floor(jnp.where(ahead, words[0], words[1]) + 0.5))
+        far[span, :] = integer(jnp.floor(jnp.where(ahead, words[1], words[0]) + 0.5))
+    near[TURNS * HB :, :] = integer(jnp.floor(jnp.where(ahead, codes[0], codes[1]) + 0.5))
+    far[TURNS * HB :, :] = integer(jnp.floor(jnp.where(ahead, codes[1], codes[0]) + 0.5))
 
 
 def merge(mine, sent, theirs):
@@ -598,7 +606,7 @@
     )(mine, sent, theirs)
 
 
-def place_kernel(upper, lower, rest, got_upper, got_lower, blank, out, blocks, sems):
+def place_kernel(upper, lower, rest, near, far, blank, out, blocks, sems):
     del blank
     row_id, col_id, _ = position()
     shift = (col_id - row_id) & (N_COL - 1)
@@ -606,9 +614,12 @@
     def part(ref, turn):
         return ref[pl.ds(pl.multiple_of(turn * HB, HB), HB), :]
 
-    def coded(ref, turn):
-        code = pick_row(ref[TURNS * HB :, :].astype(F32), turn)
-        return decode(part(ref, turn).astype(F32), code)
+    ahead = (row_id & (KB - 1)) < col_id
+
+    def coded(from_near, turn):
+        code = jnp.where(from_near, near[TURNS * HB :, :].astype(F32), far[TURNS * HB :, :].astype(F32))
+        words = jnp.where(from_near, part(near, turn).astype(F32), part(far, turn).astype(F32))
+        return decode(words, pick_row(code, turn))
 
     def write(t, low, at):
         slot = TURNS * low + t
@@ -625,7 +636,7 @@
                 else:
                     turn = t + jnp.where(row_id + shift >= N_ROW, 1, 0)
                     blocks[t, :HB, :] = part(upper, t)
-                    blocks[t, HB:, :] = coded(got_lower, jnp.minimum(turn, TURNS - 1))
+                    blocks[t, HB:, :] = coded(ahead, jnp.minimum(turn, TURNS - 1))
                     write(t, 0, at).start()
 
             @pl.when((shift > 0) & (at > 0))
@@ -634,7 +645,7 @@
                     write(t, 1, at - 1).wait()
                 else:
                     turn = t - jnp.where(row_id + shift < N_COL, 1, 0)
-                    top = coded(got_upper, jnp.maximum(turn, 0))
+                    top = coded(jnp.logical_not(ahead), jnp.maximum(turn, 0))
                     blocks[TURNS + t] = jnp.concatenate([top, part(lower, t)], axis=0).T
                     write(t, 1, at - 1).start()
 
@@ -647,7 +658,7 @@
                     write(t, 0, at).start()
 
 
-def place(upper, lower, rest, got_upper, got_lower, blank):
+def place(upper, lower, rest, near, far, blank):
     return pl.pallas_call(
         place_kernel,
         out_shape=jax.ShapeDtypeStruct((TURNS, N_COL, BF, BF), F32),
@@ -660,38 +671,36 @@
         input_output_aliases={5: 0},
         compiler_params=limit(4),
         name="place",
-    )(upper, lower, rest, got_upper, got_lower, blank)
-
-
-def mirror_pairs():
+    )(upper, lower, rest, near, far, blank)
+
+
+def mirror_pairs(across):
     pairs = []
     for row in range(N_ROW):
         for col in range(N_COL):
-            shift = (col - row) % N_COL
-            pairs.append((row * N_COL + col, (row + shift) % N_ROW * N_COL + row % N_COL))
+            half = (row // KB) ^ across
+            pairs.append((row * N_COL + col, (half * KB + col) * N_COL + row % KB))
     return pairs
 
 
 def shards(density, basis, weights, batch_start, batch_count):
     swap = [(0, 1), (1, 0)]
-    there = mirror_pairs()
-    plan = jnp.concatenate([batch_start, batch_count])
     held, sent = share(density)
     theirs = lax.ppermute(sent, "h", swap)
-    table = route(plan)
+    table = route(batch_start, batch_count)
     packed = pack(table, held, theirs)
     window = lax.all_to_all(packed, GROUP, split_axis=0, concat_axis=0, tiled=True)
 
-    outgoing = batches(plan, weights, turn(plan, basis), window)
+    outgoing = batches(table, weights, turn(table, basis), window)
     arrived = lax.all_to_all(outgoing, GROUP, split_axis=0, concat_axis=0, tiled=True)
 
     sent = collect(1, table, arrived)
     theirs = lax.ppermute(sent, "h", swap)
     mine, blank = collect(0, table, arrived)
-    upper, lower, rest, up_words, low_words = merge(mine, sent, theirs)
-    got_upper = lax.ppermute(up_words, ALL, there)
-    got_lower = lax.ppermute(low_words, ALL, [(d, s) for s, d in there])
-    potential = place(upper, lower, rest, got_upper, got_lower, blank)
+    upper, lower, rest, near, far = merge(mine, sent, theirs)
+    near = lax.ppermute(near, ALL, mirror_pairs(0))
+    far = lax.ppermute(far, ALL, mirror_pairs(1))
+    potential = place(upper, lower, rest, near, far, blank)
     return potential, rest[TURNS, 0] / (NBLK * BF)
 
 

time: 152 us -> 150 us (0.987)
    ppermute x2, waiting for transfers between devices: 4.25 us -> 2.48 us  [the longest x1 1.77 us: shards(): far = lax.ppermute(far, ALL, mirror_pairs(1))]
  transfers between devices with their start and end apart: 5 -> 5, of which waited for: 3 -> 5; matrix products, arithmetic and copies ran while one was open for 1% -> 0% of each run, Pallas kernels for 6% -> 6%
where the time goes in v8:
time: 150 us; the launch traced here: 149 us
  blocking collectives  56 us (37%)
  waiting for transfers between devices  44 us (29%)
  starting transfers between devices  23.6 us (16%)
  Pallas kernels  19.5 us (13%)
  local copies, waits for them, and re-layouts  3.07 us (2%)
  between operations  2.51 us (2%)
    all_to_all x1, blocking collectives, shards(): lax.all_to_all(outgoing, GROUP, split_axis=0, concat_axis=0, tiled=True)  56 us
    all_to_all x1, waiting for transfers between devices, shards(): lax.all_to_all(packed, GROUP, split_axis=0, concat_axis=0, tiled=True)  37.8 us
    all_to_all x1, starting transfers between devices, shards(): lax.all_to_all(packed, GROUP, split_axis=0, concat_axis=0, tiled=True)  9.98 us
    ppermute x1, starting transfers between devices, shards(): far = lax.ppermute(far, ALL, mirror_pairs(1))  5.29 us
    ppermute x2, starting transfers between devices, shards(): theirs = lax.ppermute(sent, 'h', swap)  4.42 us
    pallas_call x1, Pallas kernels, batches(): pl.pallas_call(batch_kernel, out_shape=jax.ShapeDtypeStruct((PEERS, ROWS,...  4.38 us
    pallas_call x1, Pallas kernels, turn(): pl.pallas_call(turn_kernel, out_shape=jax.ShapeDtypeStruct((SLOTS, 4, KF,...  4.14 us
    ppermute x1, starting transfers between devices, shards(): near = lax.ppermute(near, ALL, mirror_pairs(0))  3.92 us
  transfers between devices with their start and end apart: 5, of which 5 were waited for; matrix products, arithmetic and copies ran while one was open for 0% of the time, Pallas kernels for 6%

profile of v8, /device:TPU:18, one launch (start us, length us, event | category | flops | bytes accessed | tf_op | source)
XLA Modules:
  0.0 148.7 jit_solution(5982989691023740188)
XLA Ops:
  0.6 0.0 copy-start
  0.6 1.2 copy-done
  1.9 0.5 share.1
  2.4 2.2 %collective-permute-start = (bf16[528,128]{1,0:T(8,128)(2,1)S(1)}, bf16[528,128]{1,0:T(8,128)(2,1)S(1)}, u32[]{:S(2)}, u32[]{:S(2)}) collective-permute-start(bf16[528,128]{1,0:T(8,128)(2,1)S(1)} %get-tuple-element.12), channel_id=1, source_target_pairs={{0,64},{64,0},{1,65},{65,1},{2,66},{66,2},{3,67},{67,3},{4,68},{68... | collective-permute-start | bytes 405512 | tf_op jit(solution)/shard_map/ppermute | solution.py:689
  4.6 0.0 copy-start.2
  4.6 0.7 copy-done.2
  5.3 0.0 copy-start.3
  5.3 0.7 copy-done.3
  5.9 2.8 %route.1.table = s32[432]{0:T(512)S(1)} custom-call(s32[384]{0:T(512)S(1)} %copy-done.2, s32[128]{0:T(128)S(1)} %copy-done.3), custom_call_target="tpu_custom_call" | custom-call | flops 1000000 | bytes 4194304 | tf_op jit(solution)/shard_map/route/pallas_call | solution.py:189
  8.8 0.5 collective-permute-done.theirs
  9.3 2.7 %pack.1 = bf16[64,208,128]{2,1,0:T(8,128)(2,1)} custom-call(s32[432]{0:T(512)S(1)} %route.1.table, bf16[528,128]{1,0:T(8,128)(2,1)S(1)} %get-tuple-element.11.mine, bf16[528,128]{1,0:T(8,128)(2,1)S(1)} %collective-permute-done.theirs), custom_call_target="tpu_custom_call" | custom-call | tf_op jit(solution)/shard_map/pack/pallas_call | solution.py:259
  12.0 10.0 %all-to-all-start = ((bf16[64,208,128]{2,1,0:T(8,128)(2,1)}), bf16[64,208,128]{2,1,0:T(8,128)(2,1)S(1)}, u32[]{:S(2)}, u32[]{:S(2)}) async-start(bf16[64,208,128]{2,1,0:T(8,128)(2,1)} %pack.1), calls=%async_computation | async-start | bytes 6815744 | tf_op jit(solution)/shard_map/all_to_all | solution.py:692
  22.0 0.0 copy-start.1
  22.0 4.1 %turn.1.flipped = bf16[3,4,1024,256]{3,2,1,0:T(8,128)(2,1)} custom-call(s32[432]{0:T(512)S(1)} %route.1.table, bf16[3,4,256,1024]{3,2,1,0:T(8,128)(2,1)} %basis.1), custom_call_target="tpu_custom_call" | custom-call | flops 1000000 | bytes 25165824 | tf_op jit(solution)/shard_map/turn/pallas_call | solution.py:308
  26.2 37.8 %all-to-all-done.window = bf16[64,208,128]{2,1,0:T(8,128)(2,1)S(1)} async-done(((bf16[64,208,128]{2,1,0:T(8,128)(2,1)}), bf16[64,208,128]{2,1,0:T(8,128)(2,1)S(1)}, u32[]{:S(2)}, u32[]{:S(2)}) %all-to-all-start) | async-done | bytes 3407904 | tf_op jit(solution)/shard_map/all_to_all | solution.py:692
  64.0 0.0 copy-done.1
  64.0 4.4 %batches.1 = bf16[64,208,128]{2,1,0:T(8,128)(2,1)S(1)} custom-call(s32[432]{0:T(512)S(1)} %route.1.table, f32[3,256]{1,0:T(4,128)S(1)} %copy-done.1, bf16[3,4,1024,256]{3,2,1,0:T(8,128)(2,1)} %turn.1.flipped, bf16[64,208,128]{2,1,0:T(8,128)(2,1)S(1)} %all-to-all-done.window), custom_call_target="tpu_custom_call" | custom-call | tf_op jit(solution)/shard_map/batches/pallas_call | solution.py:453
  68.4 56.0 %all_to_all.10.arrived = bf16[64,208,128]{2,1,0:T(8,128)(2,1)S(1)} all-to-all(bf16[64,208,128]{2,1,0:T(8,128)(2,1)S(1)} %batches.1), channel_id=1, replica_groups=mesh['h'=2,'xl'=2,'y'=4,'z'=4,'c'=2] {'xl','y','z','c'}, dimensions={0} | all-to-all | bytes 6815744 | tf_op jit(solution)/shard_map/all_to_all | solution.py:695
  124.4 1.4 collect_other.1.sent
  125.8 2.2 %collective-permute-start.1 = (s16[528,128]{1,0:T(8,128)(2,1)S(1)}, s16[528,128]{1,0:T(8,128)(2,1)S(1)}, u32[]{:S(2)}, u32[]{:S(2)}) collective-permute-start(s16[528,128]{1,0:T(8,128)(2,1)S(1)} %collect_other.1.sent), channel_id=1, source_target_pairs={{0,64},{64,0},{1,65},{65,1},{2,66},{66,2},{3,67},{67,3},{4,68},{68... | collective-permute-start | bytes 405512 | tf_op jit(solution)/shard_map/ppermute | solution.py:698
  128.1 1.9 %collect_own.1 = (f32[520,128]{1,0:T(8,128)S(1)}, f32[4,8,128,128]{3,2,1,0:T(8,128)}) custom-call(s32[432]{0:T(512)S(1)} %route.1.table, bf16[64,208,128]{2,1,0:T(8,128)(2,1)S(1)} %all_to_all.10.arrived), custom_call_target="tpu_custom_call" | custom-call | flops 1000000 | bytes 4194304 | tf_op jit(solution)/shard_map/collect_own/pallas_call | solution.py:552
  130.0 3.2 %collective-permute-done.1.theirs = s16[528,128]{1,0:T(8,128)(2,1)S(1)} collective-permute-done((s16[528,128]{1,0:T(8,128)(2,1)S(1)}, s16[528,128]{1,0:T(8,128)(2,1)S(1)}, u32[]{:S(2)}, u32[]{:S(2)}) %collective-permute-start.1) | collective-permute-done | bytes 135200 | tf_op jit(solution)/shard_map/ppermute | solution.py:698
  133.2 0.2 merge.1
  133.4 3.9 %collective-permute-start.2 = (s16[272,128]{1,0:T(8,128)(2,1)S(1)}, s16[272,128]{1,0:T(8,128)(2,1)S(1)}, u32[]{:S(2)}, u32[]{:S(2)}) collective-permute-start(s16[272,128]{1,0:T(8,128)(2,1)S(1)} %get-tuple-element.17), channel_id=1, source_target_pairs={{0,0},{1,8},{2,16},{3,24},{4,32},{5,40},{6,48},{7,56},{8,1},{9,9},... | collective-permute-start | bytes 208904 | tf_op jit(solution)/shard_map/ppermute | solution.py:701
  137.3 5.3 %collective-permute-start.3 = (s16[272,128]{1,0:T(8,128)(2,1)S(1)}, s16[272,128]{1,0:T(8,128)(2,1)S(1)}, u32[]{:S(2)}, u32[]{:S(2)}) collective-permute-start(s16[272,128]{1,0:T(8,128)(2,1)S(1)} %get-tuple-element.18), channel_id=1, source_target_pairs={{0,64},{1,72},{2,80},{3,88},{4,96},{5,104},{6,112},{7,120},{8,65},... | collective-permute-start | bytes 208904 | tf_op jit(solution)/shard_map/ppermute | solution.py:702
  142.6 0.5 slice.3
  143.8 0.7 collective-permute-done.2.near
  144.5 1.8 %collective-permute-done.3.far = s16[272,128]{1,0:T(8,128)(2,1)S(1)} collective-permute-done((s16[272,128]{1,0:T(8,128)(2,1)S(1)}, s16[272,128]{1,0:T(8,128)(2,1)S(1)}, u32[]{:S(2)}, u32[]{:S(2)}) %collective-permute-start.3) | collective-permute-done | bytes 69664 | tf_op jit(solution)/shard_map/ppermute | solution.py:702
  146.3 1.3 place.1
Async XLA Ops:
  0.6 1.2 copy-start
  2.4 6.9 %collective-permute-start = (bf16[528,128]{1,0:T(8,128)(2,1)S(1)}, bf16[528,128]{1,0:T(8,128)(2,1)S(1)}, u32[]{:S(2)}, u32[]{:S(2)}) collective-permute-start(bf16[528,128]{1,0:T(8,128)(2,1)S(1)} %get-tuple-element.12), channel_id=1, source_target_pairs={{0,64},{64,0},{1,65},{65,1},{2,66},{66,2},{3,67},{67,3},{4,68},{68... | collective-permute-start | bytes 405512 | tf_op jit(solution)/shard_map/ppermute | solution.py:689
  4.6 0.7 copy-start.2
  5.3 0.7 copy-start.3
  12.0 52.0 %all-to-all-start = ((bf16[64,208,128]{2,1,0:T(8,128)(2,1)}), bf16[64,208,128]{2,1,0:T(8,128)(2,1)S(1)}, u32[]{:S(2)}, u32[]{:S(2)}) async-start(bf16[64,208,128]{2,1,0:T(8,128)(2,1)} %pack.1), calls=%async_computation | async-start | bytes 6815744 | tf_op jit(solution)/shard_map/all_to_all | solution.py:692
  22.0 42.0 %copy-start.1 = (f32[3,256]{1,0:T(4,128)S(1)}, f32[3,256]{1,0:T(4,128)}, u32[]{:S(2)}) copy-start(f32[3,256]{1,0:T(4,128)} %weights.1) | copy-start | bytes 9220
  125.8 7.3 %collective-permute-start.1 = (s16[528,128]{1,0:T(8,128)(2,1)S(1)}, s16[528,128]{1,0:T(8,128)(2,1)S(1)}, u32[]{:S(2)}, u32[]{:S(2)}) collective-permute-start(s16[528,128]{1,0:T(8,128)(2,1)S(1)} %collect_other.1.sent), channel_id=1, source_target_pairs={{0,64},{64,0},{1,65},{65,1},{2,66},{66,2},{3,67},{67,3},{4,68},{68... | collective-permute-start | bytes 405512 | tf_op jit(solution)/shard_map/ppermute | solution.py:698
  133.4 11.1 %collective-permute-start.2 = (s16[272,128]{1,0:T(8,128)(2,1)S(1)}, s16[272,128]{1,0:T(8,128)(2,1)S(1)}, u32[]{:S(2)}, u32[]{:S(2)}) collective-permute-start(s16[272,128]{1,0:T(8,128)(2,1)S(1)} %get-tuple-element.17), channel_id=1, source_target_pairs={{0,0},{1,8},{2,16},{3,24},{4,32},{5,40},{6,48},{7,56},{8,1},{9,9},... | collective-permute-start | bytes 208904 | tf_op jit(solution)/shard_map/ppermute | solution.py:701
  137.3 8.9 %collective-permute-start.3 = (s16[272,128]{1,0:T(8,128)(2,1)S(1)}, s16[272,128]{1,0:T(8,128)(2,1)S(1)}, u32[]{:S(2)}, u32[]{:S(2)}) collective-permute-start(s16[272,128]{1,0:T(8,128)(2,1)S(1)} %get-tuple-element.18), channel_id=1, source_target_pairs={{0,64},{1,72},{2,80},{3,88},{4,96},{5,104},{6,112},{7,120},{8,65},... | collective-permute-start | bytes 208904 | tf_op jit(solution)/shard_map/ppermute | solution.py:702

commit v9 on v8

--- a/solution.py
+++ b/solution.py
@@ -30,7 +30,14 @@
 ROW = ("h", "xl", "y")
 COL = ("z", "c")
 ALL = ROW + COL
-GROUP = ("xl", "y", "z", "c")
+ORDER = [
+    53, 42, 62, 31, 35, 37, 59, 57, 45, 33, 49, 50, 54, 38, 5, 0,
+    13, 14, 30, 21, 52, 41, 28, 58, 1, 3, 61, 48, 12, 17, 29, 16,
+    11, 15, 24, 7, 23, 39, 36, 20, 51, 34, 10, 27, 32, 63, 43, 26,
+    8, 40, 60, 9, 47, 55, 22, 19, 56, 6, 46, 18, 44, 2, 4, 25,
+]
+PLACE = [ORDER.index(x) for x in range(PEERS)]
+GROUPS = [[h * PEERS + x for x in ORDER] for h in range(2)]
 VMEM = pl.BlockSpec(memory_space=pltpu.VMEM)
 HBM = pl.BlockSpec(memory_space=pltpu.HBM)
 F32 = jnp.float32
@@ -71,7 +78,7 @@
 
 def entry(starts, peer, slot, where):
     row_id, col_id, h = where
-    start = starts[(h * PEERS + peer) * SLOTS + slot]
+    start = starts[(h * PEERS + ORDER[peer]) * SLOTS + slot]
     i = start + ((row_id - start) & (KB - 1))
     j = start + ((col_id - start) & (KB - 1))
     other = ((i >> 3) & 1) ^ h
@@ -153,6 +160,7 @@
 BOUNDS = 2 * ALL_SLOTS
 STRIDE = 16
 OWN = BOUNDS + 2 * STRIDE
+PLACES = OWN + STRIDE
 
 
 def route_kernel(starts, counts, table):
@@ -162,24 +170,21 @@
         table[OWN + slot] = starts[me * SLOTS + slot]
     table[OWN + SLOTS] = counts[me]
 
-    def one_chunk(chunk, ends):
-        for which in range(2):
-            table[BOUNDS + which * STRIDE + chunk] = ends[which]
-
-        for k in range(CHUNK):
-            peer = chunk * CHUNK + k
-
-            def one(slot, ends):
-                other, _, at = entry(starts, peer, slot, where)
-                index = jnp.where(other == 1, ends[1], ALL_SLOTS + ends[0])
-                table[index] = peer + slot * PEERS + at * (4 * PEERS)
-                return ends[0] + 1 - other, ends[1] + other
-
-            ends = one(0, ends)
-            ends = lax.fori_loop(1, counts[where[2] * PEERS + peer], one, ends)
-        return ends
-
-    ends = lax.fori_loop(0, PEERS // CHUNK, one_chunk, (jnp.int32(0), jnp.int32(0)))
+    ends = (jnp.int32(0), jnp.int32(0))
+    for peer in range(PEERS):
+        table[PLACES + peer] = PLACE[peer]
+        if peer % CHUNK == 0:
+            for which in range(2):
+                table[BOUNDS + which * STRIDE + peer // CHUNK] = ends[which]
+
+        def one(slot, ends):
+            other, _, at = entry(starts, peer, slot, where)
+            index = jnp.where(other == 1, ends[1], ALL_SLOTS + ends[0])
+            table[index] = peer + slot * PEERS + at * (4 * PEERS)
+            return ends[0] + 1 - other, ends[1] + other
+
+        ends = one(0, ends)
+        ends = lax.fori_loop(1, counts[where[2] * PEERS + ORDER[peer]], one, ends)
     for which in range(2):
         table[BOUNDS + which * STRIDE + PEERS // CHUNK] = ends[which]
 
@@ -188,7 +193,7 @@
     scalar = pl.BlockSpec(memory_space=pltpu.SMEM)
     return pl.pallas_call(
         route_kernel,
-        out_shape=jax.ShapeDtypeStruct((OWN + STRIDE,), jnp.int32),
+        out_shape=jax.ShapeDtypeStruct((PLACES + PEERS,), jnp.int32),
         in_specs=[scalar, scalar],
         out_specs=scalar,
         compiler_params=limit(4),
@@ -350,6 +355,9 @@
         start = table[OWN + slot]
         return start, [(start + o) & (KB - 1) for o in range(KB)]
 
+    def place_of(a, b):
+        return table[PLACES + a * KB + b]
+
     def rows_of(slot):
         return pl.ds(pl.multiple_of(slot * HB, HB), HB)
 
@@ -360,12 +368,12 @@
             r1 = slice(o1 * BF, (o1 + 1) * BF)
             for o2 in range(o1 + 1, KB):
                 r2 = slice(o2 * BF, (o2 + 1) * BF)
-                top = window[cls[o1] * KB + cls[o2], span, :]
-                bottom = window[cls[o2] * KB + cls[o1], span, :]
+                top = window[place_of(cls[o1], cls[o2]), span, :]
+                bottom = window[place_of(cls[o2], cls[o1]), span, :]
                 block = jnp.concatenate([top, bottom], axis=0)
                 mat[r1, r2] = block
                 mat[r2, r1] = block.T
-            diagonal = cls[o1] * (KB + 1)
+            diagonal = place_of(cls[o1], cls[o1])
             line = pick_row(window[diagonal, EXT:, :].astype(F32), (start + o1) >> 3)
             block = unpack_symmetric(window[diagonal, span, :].astype(F32), line)
             mat[r1, r1] = block.astype(BF16)
@@ -428,11 +436,11 @@
                     block = rows[k * BF : (k + 1) * BF, c0 : c0 + BF]
                     if o2 == o1:
                         packed, line = pack_symmetric(block)
-                        out[cls[o1] * (KB + 1), span, :] = packed.astype(BF16)
+                        out[place_of(cls[o1], cls[o1]), span, :] = packed.astype(BF16)
                         lines[cls[o1]] = jnp.where(row == slot, line, lines[cls[o1]])
                     else:
-                        out[cls[o1] * KB + cls[o2], span, :] = block[:HB].astype(BF16)
-                        out[cls[o2] * KB + cls[o1], span, :] = block[HB:].astype(BF16)
+                        out[place_of(cls[o1], cls[o2]), span, :] = block[:HB].astype(BF16)
+                        out[place_of(cls[o2], cls[o1]), span, :] = block[HB:].astype(BF16)
         assemble(jnp.minimum(slot + 1, SLOTS - 1))
         return total
 
@@ -444,9 +452,9 @@
     energy = jnp.where((row == 0) & (lane < 3), spread, 0.0)
     for peer in range(PEERS):
         if peer % (KB + 1) == 0:
-            out[peer, EXT:, :] = (lines[peer // (KB + 1)] + energy).astype(BF16)
+            out[PLACE[peer], EXT:, :] = (lines[peer // (KB + 1)] + energy).astype(BF16)
         else:
-            out[peer, EXT:, :] = energy.astype(BF16)
+            out[PLACE[peer], EXT:, :] = energy.astype(BF16)
 
 
 def batches(table, weights, flipped, window):
@@ -683,16 +691,20 @@
     return pairs
 
 
+def exchange(parts):
+    return lax.all_to_all(parts, ALL, 0, 0, axis_index_groups=GROUPS, tiled=True)
+
+
 def shards(density, basis, weights, batch_start, batch_count):
     swap = [(0, 1), (1, 0)]
     held, sent = share(density)
     theirs = lax.ppermute(sent, "h", swap)
     table = route(batch_start, batch_count)
     packed = pack(table, held, theirs)
-    window = lax.all_to_all(packed, GROUP, split_axis=0, concat_axis=0, tiled=True)
+    window = exchange(packed)
 
     outgoing = batches(table, weights, turn(table, basis), window)
-    arrived = lax.all_to_all(outgoing, GROUP, split_axis=0, concat_axis=0, tiled=True)
+    arrived = exchange(outgoing)
 
     sent = collect(1, table, arrived)
     theirs = lax.ppermute(sent, "h", swap)

time: 150 us -> 146 us (0.973)
  waiting for transfers between devices: 44 us -> 48.6 us
  starting transfers between devices: 23.6 us -> 19.3 us
  blocking collectives: 56 us -> 52.9 us
    ppermute x1, starting transfers between devices: 5.29 us -> 1.6 us  [shards(): far = lax.ppermute(far, ALL, mirror_pairs(1))]
    all_to_all x1, blocking collectives: 56 us -> 52.9 us  [exchange(): lax.all_to_all(parts, ALL, 0, 0, axis_index_groups=GROUPS, tiled=True)]
    ppermute x1, waiting for transfers between devices: 1.77 us -> 4.42 us  [shards(): far = lax.ppermute(far, ALL, mirror_pairs(1))]
    ppermute x1, starting transfers between devices: 3.92 us -> 6.47 us  [shards(): near = lax.ppermute(near, ALL, mirror_pairs(0))]
    all_to_all x1, starting transfers between devices: 9.98 us -> 7.92 us  [exchange(): lax.all_to_all(parts, ALL, 0, 0, axis_index_groups=GROUPS, tiled=True)]
where the time goes in v9:
time: 146 us; the launch traced here: 145 us
  blocking collectives  52.9 us (36%)
  waiting for transfers between devices  48.6 us (33%)
  starting transfers between devices  19.3 us (13%)
  Pallas kernels  19 us (13%)
  local copies, waits for them, and re-layouts  3.07 us (2%)
  between operations  2.51 us (2%)
    all_to_all x1, blocking collectives, exchange(): lax.all_to_all(parts, ALL, 0, 0, axis_index_groups=GROUPS, tiled=True)  52.9 us
    all_to_all x1, waiting for transfers between devices, exchange(): lax.all_to_all(parts, ALL, 0, 0, axis_index_groups=GROUPS, tiled=True)  37.5 us
    all_to_all x1, starting transfers between devices, exchange(): lax.all_to_all(parts, ALL, 0, 0, axis_index_groups=GROUPS, tiled=True)  7.92 us
    ppermute x1, starting transfers between devices, shards(): near = lax.ppermute(near, ALL, mirror_pairs(0))  6.47 us
    ppermute x2, waiting for transfers between devices, shards(): theirs = lax.ppermute(sent, 'h', swap)  4.81 us
    ppermute x1, waiting for transfers between devices, shards(): far = lax.ppermute(far, ALL, mirror_pairs(1))  4.42 us
    pallas_call x1, Pallas kernels, batches(): pl.pallas_call(batch_kernel, out_shape=jax.ShapeDtypeStruct((PEERS, ROWS,...  4.36 us
    pallas_call x1, Pallas kernels, turn(): pl.pallas_call(turn_kernel, out_shape=jax.ShapeDtypeStruct((SLOTS, 4, KF,...  4.14 us
  transfers between devices with their start and end apart: 5, of which 5 were waited for; matrix products, arithmetic and copies ran while one was open for 0% of the time, Pallas kernels for 6%

profile of v9, /device:TPU:18, one launch (start us, length us, event | category | flops | bytes accessed | tf_op | source)
XLA Modules:
  0.0 145.3 jit_solution(6045430931535334670)
XLA Ops:
  0.6 0.0 copy-start
  0.6 1.2 copy-done
  1.9 0.5 share.1
  2.4 2.2 %collective-permute-start = (bf16[528,128]{1,0:T(8,128)(2,1)S(1)}, bf16[528,128]{1,0:T(8,128)(2,1)S(1)}, u32[]{:S(2)}, u32[]{:S(2)}) collective-permute-start(bf16[528,128]{1,0:T(8,128)(2,1)S(1)} %get-tuple-element.12), channel_id=1, source_target_pairs={{0,64},{64,0},{1,65},{65,1},{2,66},{66,2},{3,67},{67,3},{4,68},{68... | collective-permute-start | bytes 405512 | tf_op jit(solution)/shard_map/ppermute | solution.py:701
  4.6 0.0 copy-start.2
  4.6 0.7 copy-done.2
  5.3 0.0 copy-start.3
  5.3 0.7 copy-done.3
  5.9 2.5 %route.1.table = s32[496]{0:T(512)S(1)} custom-call(s32[384]{0:T(512)S(1)} %copy-done.2, s32[128]{0:T(128)S(1)} %copy-done.3), custom_call_target="tpu_custom_call" | custom-call | flops 1000000 | bytes 4194304 | tf_op jit(solution)/shard_map/route/pallas_call | solution.py:194
  8.5 0.8 collective-permute-done.theirs
  9.3 2.7 %pack.1 = bf16[64,208,128]{2,1,0:T(8,128)(2,1)} custom-call(s32[496]{0:T(512)S(1)} %route.1.table, bf16[528,128]{1,0:T(8,128)(2,1)S(1)} %get-tuple-element.11.mine, bf16[528,128]{1,0:T(8,128)(2,1)S(1)} %collective-permute-done.theirs), custom_call_target="tpu_custom_call" | custom-call | tf_op jit(solution)/shard_map/pack/pallas_call | solution.py:264
  11.9 7.9 %all-to-all-start = ((bf16[64,208,128]{2,1,0:T(8,128)(2,1)}), bf16[64,208,128]{2,1,0:T(8,128)(2,1)S(1)}, u32[]{:S(2)}, u32[]{:S(2)}) async-start(bf16[64,208,128]{2,1,0:T(8,128)(2,1)} %pack.1), calls=%async_computation | async-start | bytes 6815744 | tf_op jit(solution)/shard_map/all_to_all | solution.py:695
  19.9 0.0 copy-start.1
  19.9 4.1 %turn.1.flipped = bf16[3,4,1024,256]{3,2,1,0:T(8,128)(2,1)} custom-call(s32[496]{0:T(512)S(1)} %route.1.table, bf16[3,4,256,1024]{3,2,1,0:T(8,128)(2,1)} %basis.1), custom_call_target="tpu_custom_call" | custom-call | flops 1000000 | bytes 25165824 | tf_op jit(solution)/shard_map/turn/pallas_call | solution.py:313
  24.0 37.5 %all-to-all-done.window = bf16[64,208,128]{2,1,0:T(8,128)(2,1)S(1)} async-done(((bf16[64,208,128]{2,1,0:T(8,128)(2,1)}), bf16[64,208,128]{2,1,0:T(8,128)(2,1)S(1)}, u32[]{:S(2)}, u32[]{:S(2)}) %all-to-all-start) | async-done | bytes 3407904 | tf_op jit(solution)/shard_map/all_to_all | solution.py:695
  61.6 0.0 copy-done.1
  61.6 4.4 %batches.1 = bf16[64,208,128]{2,1,0:T(8,128)(2,1)S(1)} custom-call(s32[496]{0:T(512)S(1)} %route.1.table, f32[3,256]{1,0:T(4,128)S(1)} %copy-done.1, bf16[3,4,1024,256]{3,2,1,0:T(8,128)(2,1)} %turn.1.flipped, bf16[64,208,128]{2,1,0:T(8,128)(2,1)S(1)} %all-to-all-done.window), custom_call_target="tpu_custom_call" | custom-call | tf_op jit(solution)/shard_map/batches/pallas_call | solution.py:461
  65.9 52.9 %all_to_all.10.arrived = bf16[64,208,128]{2,1,0:T(8,128)(2,1)S(1)} all-to-all(bf16[64,208,128]{2,1,0:T(8,128)(2,1)S(1)} %batches.1), channel_id=1, replica_groups={{53,42,62,31,35,37,59,57,45,33,49,50,54,38,5,0,13,14,30,21,52,41,28,58,..., dimensions={0} | all-to-all | bytes 6815744 | tf_op jit(solution)/shard_map/all_to_all | solution.py:695
  118.8 1.3 collect_other.1.sent
  120.1 1.1 collective-permute-start.1
  121.2 1.9 %collect_own.1 = (f32[520,128]{1,0:T(8,128)S(1)}, f32[4,8,128,128]{3,2,1,0:T(8,128)}) custom-call(s32[496]{0:T(512)S(1)} %route.1.table, bf16[64,208,128]{2,1,0:T(8,128)(2,1)S(1)} %all_to_all.10.arrived), custom_call_target="tpu_custom_call" | custom-call | flops 1000000 | bytes 4194304 | tf_op jit(solution)/shard_map/collect_own/pallas_call | solution.py:560
  123.1 4.0 %collective-permute-done.1.theirs = s16[528,128]{1,0:T(8,128)(2,1)S(1)} collective-permute-done((s16[528,128]{1,0:T(8,128)(2,1)S(1)}, s16[528,128]{1,0:T(8,128)(2,1)S(1)}, u32[]{:S(2)}, u32[]{:S(2)}) %collective-permute-start.1) | collective-permute-done | bytes 135200 | tf_op jit(solution)/shard_map/ppermute | solution.py:710
  127.1 0.2 merge.1
  127.4 6.5 %collective-permute-start.2 = (s16[272,128]{1,0:T(8,128)(2,1)S(1)}, s16[272,128]{1,0:T(8,128)(2,1)S(1)}, u32[]{:S(2)}, u32[]{:S(2)}) collective-permute-start(s16[272,128]{1,0:T(8,128)(2,1)S(1)} %get-tuple-element.17), channel_id=1, source_target_pairs={{0,0},{1,8},{2,16},{3,24},{4,32},{5,40},{6,48},{7,56},{8,1},{9,9},... | collective-permute-start | bytes 208904 | tf_op jit(solution)/shard_map/ppermute | solution.py:713
  133.8 1.6 %collective-permute-start.3 = (s16[272,128]{1,0:T(8,128)(2,1)S(1)}, s16[272,128]{1,0:T(8,128)(2,1)S(1)}, u32[]{:S(2)}, u32[]{:S(2)}) collective-permute-start(s16[272,128]{1,0:T(8,128)(2,1)S(1)} %get-tuple-element.18), channel_id=1, source_target_pairs={{0,64},{1,72},{2,80},{3,88},{4,96},{5,104},{6,112},{7,120},{8,65},... | collective-permute-start | bytes 208904 | tf_op jit(solution)/shard_map/ppermute | solution.py:714
  135.4 0.5 slice.3
  136.6 1.8 %collective-permute-done.2.near = s16[272,128]{1,0:T(8,128)(2,1)S(1)} collective-permute-done((s16[272,128]{1,0:T(8,128)(2,1)S(1)}, s16[272,128]{1,0:T(8,128)(2,1)S(1)}, u32[]{:S(2)}, u32[]{:S(2)}) %collective-permute-start.2) | collective-permute-done | bytes 69664 | tf_op jit(solution)/shard_map/ppermute | solution.py:713
  138.5 4.4 %collective-permute-done.3.far = s16[272,128]{1,0:T(8,128)(2,1)S(1)} collective-permute-done((s16[272,128]{1,0:T(8,128)(2,1)S(1)}, s16[272,128]{1,0:T(8,128)(2,1)S(1)}, u32[]{:S(2)}, u32[]{:S(2)}) %collective-permute-start.3) | collective-permute-done | bytes 69664 | tf_op jit(solution)/shard_map/ppermute | solution.py:714
  142.9 1.3 place.1
Async XLA Ops:
  0.6 1.2 copy-start
  2.4 6.9 %collective-permute-start = (bf16[528,128]{1,0:T(8,128)(2,1)S(1)}, bf16[528,128]{1,0:T(8,128)(2,1)S(1)}, u32[]{:S(2)}, u32[]{:S(2)}) collective-permute-start(bf16[528,128]{1,0:T(8,128)(2,1)S(1)} %get-tuple-element.12), channel_id=1, source_target_pairs={{0,64},{64,0},{1,65},{65,1},{2,66},{66,2},{3,67},{67,3},{4,68},{68... | collective-permute-start | bytes 405512 | tf_op jit(solution)/shard_map/ppermute | solution.py:701
  4.6 0.7 copy-start.2
  5.3 0.7 copy-start.3
  11.9 49.6 %all-to-all-start = ((bf16[64,208,128]{2,1,0:T(8,128)(2,1)}), bf16[64,208,128]{2,1,0:T(8,128)(2,1)S(1)}, u32[]{:S(2)}, u32[]{:S(2)}) async-start(bf16[64,208,128]{2,1,0:T(8,128)(2,1)} %pack.1), calls=%async_computation | async-start | bytes 6815744 | tf_op jit(solution)/shard_map/all_to_all | solution.py:695
  19.9 41.7 %copy-start.1 = (f32[3,256]{1,0:T(4,128)S(1)}, f32[3,256]{1,0:T(4,128)}, u32[]{:S(2)}) copy-start(f32[3,256]{1,0:T(4,128)} %weights.1) | copy-start | bytes 9220
  120.1 7.0 %collective-permute-start.1 = (s16[528,128]{1,0:T(8,128)(2,1)S(1)}, s16[528,128]{1,0:T(8,128)(2,1)S(1)}, u32[]{:S(2)}, u32[]{:S(2)}) collective-permute-start(s16[528,128]{1,0:T(8,128)(2,1)S(1)} %collect_other.1.sent), channel_id=1, source_target_pairs={{0,64},{64,0},{1,65},{65,1},{2,66},{66,2},{3,67},{67,3},{4,68},{68... | collective-permute-start | bytes 405512 | tf_op jit(solution)/shard_map/ppermute | solution.py:710
  127.4 11.1 %collective-permute-start.2 = (s16[272,128]{1,0:T(8,128)(2,1)S(1)}, s16[272,128]{1,0:T(8,128)(2,1)S(1)}, u32[]{:S(2)}, u32[]{:S(2)}) collective-permute-start(s16[272,128]{1,0:T(8,128)(2,1)S(1)} %get-tuple-element.17), channel_id=1, source_target_pairs={{0,0},{1,8},{2,16},{3,24},{4,32},{5,40},{6,48},{7,56},{8,1},{9,9},... | collective-permute-start | bytes 208904 | tf_op jit(solution)/shard_map/ppermute | solution.py:713
  133.8 9.0 %collective-permute-start.3 = (s16[272,128]{1,0:T(8,128)(2,1)S(1)}, s16[272,128]{1,0:T(8,128)(2,1)S(1)}, u32[]{:S(2)}, u32[]{:S(2)}) collective-permute-start(s16[272,128]{1,0:T(8,128)(2,1)S(1)} %get-tuple-element.18), channel_id=1, source_target_pairs={{0,64},{1,72},{2,80},{3,88},{4,96},{5,104},{6,112},{7,120},{8,65},... | collective-permute-start | bytes 208904 | tf_op jit(solution)/shard_map/ppermute | solution.py:714

commit v10 on v9

--- a/solution.py
+++ b/solution.py
@@ -31,10 +31,10 @@
 COL = ("z", "c")
 ALL = ROW + COL
 ORDER = [
-    53, 42, 62, 31, 35, 37, 59, 57, 45, 33, 49, 50, 54, 38, 5, 0,
-    13, 14, 30, 21, 52, 41, 28, 58, 1, 3, 61, 48, 12, 17, 29, 16,
-    11, 15, 24, 7, 23, 39, 36, 20, 51, 34, 10, 27, 32, 63, 43, 26,
-    8, 40, 60, 9, 47, 55, 22, 19, 56, 6, 46, 18, 44, 2, 4, 25,
+    47, 14, 49, 25, 4, 51, 17, 37, 3, 26, 56, 35, 52, 29, 33, 10,
+    36, 42, 20, 32, 43, 41, 48, 62, 12, 27, 39, 44, 16, 55, 57, 46,
+    19, 0, 15, 8, 28, 24, 30, 58, 34, 13, 23, 9, 61, 1, 11, 38,
+    18, 60, 59, 7, 2, 5, 21, 6, 45, 53, 54, 22, 63, 50, 40, 31,
 ]
 PLACE = [ORDER.index(x) for x in range(PEERS)]
 GROUPS = [[h * PEERS + x for x in ORDER] for h in range(2)]
@@ -361,10 +361,10 @@
     def rows_of(slot):
         return pl.ds(pl.multiple_of(slot * HB, HB), HB)
 
-    def assemble(slot):
+    def assemble(slot, quarter):
         start, cls = classes(slot)
         span = rows_of(slot)
-        for o1 in range(KB):
+        for o1 in ((0, 7), (1, 6), (2, 5), (3, 4))[quarter]:
             r1 = slice(o1 * BF, (o1 + 1) * BF)
             for o2 in range(o1 + 1, KB):
                 r2 = slice(o2 * BF, (o2 + 1) * BF)
@@ -378,7 +378,8 @@
             block = unpack_symmetric(window[diagonal, span, :].astype(F32), line)
             mat[r1, r1] = block.astype(BF16)
 
-    assemble(0)
+    for quarter in range(4):
+        assemble(0, quarter)
 
     def work(slot, total):
         _, cls = classes(slot)
@@ -428,6 +429,7 @@
             right[lo:hi, G:] = phi
         for t in range(4):
             lo, hi = 256 * t, 256 * (t + 1)
+            assemble(jnp.minimum(slot + 1, SLOTS - 1), t)
             rows = dot_nt(left[lo:hi, :], right[lo:, :])
             for k in range(2):
                 o1 = 2 * t + k
@@ -441,7 +443,6 @@
                     else:
                         out[place_of(cls[o1], cls[o2]), span, :] = block[:HB].astype(BF16)
                         out[place_of(cls[o2], cls[o1]), span, :] = block[HB:].astype(BF16)
-        assemble(jnp.minimum(slot + 1, SLOTS - 1))
         return total
 
     total = jnp.full((16, BF), lax.fori_loop(0, count, work, jnp.float32(0.0)), F32)

time: 146 us -> 147 us (level)
  waiting for transfers between devices: 48.6 us -> 46 us
  starting transfers between devices: 19.3 us -> 21.1 us
where the time goes in v10:
time: 147 us; the launch traced here: 146 us
  blocking collectives  53.9 us (37%)
  waiting for transfers between devices  46 us (31%)
  starting transfers between devices  21.1 us (14%)
  Pallas kernels  19 us (13%)
  local copies, waits for them, and re-layouts  3.07 us (2%)
  between operations  2.51 us (2%)
    all_to_all x1, blocking collectives, exchange(): lax.all_to_all(parts, ALL, 0, 0, axis_index_groups=GROUPS, tiled=True)  53.9 us
    all_to_all x1, waiting for transfers between devices, exchange(): lax.all_to_all(parts, ALL, 0, 0, axis_index_groups=GROUPS, tiled=True)  36.3 us
    all_to_all x1, starting transfers between devices, exchange(): lax.all_to_all(parts, ALL, 0, 0, axis_index_groups=GROUPS, tiled=True)  7.9 us
    ppermute x1, starting transfers between devices, shards(): near = lax.ppermute(near, ALL, mirror_pairs(0))  6.27 us
    pallas_call x1, Pallas kernels, batches(): pl.pallas_call(batch_kernel, out_shape=jax.ShapeDtypeStruct((PEERS, ROWS,...  4.37 us
    ppermute x2, waiting for transfers between devices, shards(): theirs = lax.ppermute(sent, 'h', swap)  4.34 us
    ppermute x2, starting transfers between devices, shards(): theirs = lax.ppermute(sent, 'h', swap)  4.23 us
    pallas_call x1, Pallas kernels, turn(): pl.pallas_call(turn_kernel, out_shape=jax.ShapeDtypeStruct((SLOTS, 4, KF,...  4.14 us
  transfers between devices with their start and end apart: 5, of which 5 were waited for; matrix products, arithmetic and copies ran while one was open for 0% of the time, Pallas kernels for 6%

profile of v10, /device:TPU:18, one launch (start us, length us, event | category | flops | bytes accessed | tf_op | source)
XLA Modules:
  0.0 145.6 jit_solution(15546003516091967118)
XLA Ops:
  0.6 0.0 copy-start
  0.6 1.2 copy-done
  1.9 0.5 share.1
  2.4 2.2 %collective-permute-start = (bf16[528,128]{1,0:T(8,128)(2,1)S(1)}, bf16[528,128]{1,0:T(8,128)(2,1)S(1)}, u32[]{:S(2)}, u32[]{:S(2)}) collective-permute-start(bf16[528,128]{1,0:T(8,128)(2,1)S(1)} %get-tuple-element.12), channel_id=1, source_target_pairs={{0,64},{64,0},{1,65},{65,1},{2,66},{66,2},{3,67},{67,3},{4,68},{68... | collective-permute-start | bytes 405512 | tf_op jit(solution)/shard_map/ppermute | solution.py:702
  4.6 0.0 copy-start.2
  4.6 0.7 copy-done.2
  5.3 0.0 copy-start.3
  5.3 0.7 copy-done.3
  5.9 2.5 %route.1.table = s32[496]{0:T(512)S(1)} custom-call(s32[384]{0:T(512)S(1)} %copy-done.2, s32[128]{0:T(128)S(1)} %copy-done.3), custom_call_target="tpu_custom_call" | custom-call | flops 1000000 | bytes 4194304 | tf_op jit(solution)/shard_map/route/pallas_call | solution.py:194
  8.5 0.8 collective-permute-done.theirs
  9.3 2.6 %pack.1 = bf16[64,208,128]{2,1,0:T(8,128)(2,1)} custom-call(s32[496]{0:T(512)S(1)} %route.1.table, bf16[528,128]{1,0:T(8,128)(2,1)S(1)} %get-tuple-element.11.mine, bf16[528,128]{1,0:T(8,128)(2,1)S(1)} %collective-permute-done.theirs), custom_call_target="tpu_custom_call" | custom-call | tf_op jit(solution)/shard_map/pack/pallas_call | solution.py:264
  11.9 7.9 %all-to-all-start = ((bf16[64,208,128]{2,1,0:T(8,128)(2,1)}), bf16[64,208,128]{2,1,0:T(8,128)(2,1)S(1)}, u32[]{:S(2)}, u32[]{:S(2)}) async-start(bf16[64,208,128]{2,1,0:T(8,128)(2,1)} %pack.1), calls=%async_computation | async-start | bytes 6815744 | tf_op jit(solution)/shard_map/all_to_all | solution.py:696
  19.8 0.0 copy-start.1
  19.8 4.1 %turn.1.flipped = bf16[3,4,1024,256]{3,2,1,0:T(8,128)(2,1)} custom-call(s32[496]{0:T(512)S(1)} %route.1.table, bf16[3,4,256,1024]{3,2,1,0:T(8,128)(2,1)} %basis.1), custom_call_target="tpu_custom_call" | custom-call | flops 1000000 | bytes 25165824 | tf_op jit(solution)/shard_map/turn/pallas_call | solution.py:313
  24.0 36.3 %all-to-all-done.window = bf16[64,208,128]{2,1,0:T(8,128)(2,1)S(1)} async-done(((bf16[64,208,128]{2,1,0:T(8,128)(2,1)}), bf16[64,208,128]{2,1,0:T(8,128)(2,1)S(1)}, u32[]{:S(2)}, u32[]{:S(2)}) %all-to-all-start) | async-done | bytes 3407904 | tf_op jit(solution)/shard_map/all_to_all | solution.py:696
  60.3 0.0 copy-done.1
  60.3 4.4 %batches.1 = bf16[64,208,128]{2,1,0:T(8,128)(2,1)S(1)} custom-call(s32[496]{0:T(512)S(1)} %route.1.table, f32[3,256]{1,0:T(4,128)S(1)} %copy-done.1, bf16[3,4,1024,256]{3,2,1,0:T(8,128)(2,1)} %turn.1.flipped, bf16[64,208,128]{2,1,0:T(8,128)(2,1)S(1)} %all-to-all-done.window), custom_call_target="tpu_custom_call" | custom-call | tf_op jit(solution)/shard_map/batches/pallas_call | solution.py:462
  64.7 53.9 %all_to_all.10.arrived = bf16[64,208,128]{2,1,0:T(8,128)(2,1)S(1)} all-to-all(bf16[64,208,128]{2,1,0:T(8,128)(2,1)S(1)} %batches.1), channel_id=1, replica_groups={{47,14,49,25,4,51,17,37,3,26,56,35,52,29,33,10,36,42,20,32,43,41,48,62,..., dimensions={0} | all-to-all | bytes 6815744 | tf_op jit(solution)/shard_map/all_to_all | solution.py:696
  118.5 1.4 collect_other.1.sent
  119.9 2.0 %collective-permute-start.1 = (s16[528,128]{1,0:T(8,128)(2,1)S(1)}, s16[528,128]{1,0:T(8,128)(2,1)S(1)}, u32[]{:S(2)}, u32[]{:S(2)}) collective-permute-start(s16[528,128]{1,0:T(8,128)(2,1)S(1)} %collect_other.1.sent), channel_id=1, source_target_pairs={{0,64},{64,0},{1,65},{65,1},{2,66},{66,2},{3,67},{67,3},{4,68},{68... | collective-permute-start | bytes 405512 | tf_op jit(solution)/shard_map/ppermute | solution.py:711
  121.9 1.9 %collect_own.1 = (f32[520,128]{1,0:T(8,128)S(1)}, f32[4,8,128,128]{3,2,1,0:T(8,128)}) custom-call(s32[496]{0:T(512)S(1)} %route.1.table, bf16[64,208,128]{2,1,0:T(8,128)(2,1)S(1)} %all_to_all.10.arrived), custom_call_target="tpu_custom_call" | custom-call | flops 1000000 | bytes 4194304 | tf_op jit(solution)/shard_map/collect_own/pallas_call | solution.py:561
  123.9 3.5 %collective-permute-done.1.theirs = s16[528,128]{1,0:T(8,128)(2,1)S(1)} collective-permute-done((s16[528,128]{1,0:T(8,128)(2,1)S(1)}, s16[528,128]{1,0:T(8,128)(2,1)S(1)}, u32[]{:S(2)}, u32[]{:S(2)}) %collective-permute-start.1) | collective-permute-done | bytes 135200 | tf_op jit(solution)/shard_map/ppermute | solution.py:711
  127.4 0.2 merge.1
  127.6 6.3 %collective-permute-start.2 = (s16[272,128]{1,0:T(8,128)(2,1)S(1)}, s16[272,128]{1,0:T(8,128)(2,1)S(1)}, u32[]{:S(2)}, u32[]{:S(2)}) collective-permute-start(s16[272,128]{1,0:T(8,128)(2,1)S(1)} %get-tuple-element.17), channel_id=1, source_target_pairs={{0,0},{1,8},{2,16},{3,24},{4,32},{5,40},{6,48},{7,56},{8,1},{9,9},... | collective-permute-start | bytes 208904 | tf_op jit(solution)/shard_map/ppermute | solution.py:714
  133.9 2.7 %collective-permute-start.3 = (s16[272,128]{1,0:T(8,128)(2,1)S(1)}, s16[272,128]{1,0:T(8,128)(2,1)S(1)}, u32[]{:S(2)}, u32[]{:S(2)}) collective-permute-start(s16[272,128]{1,0:T(8,128)(2,1)S(1)} %get-tuple-element.18), channel_id=1, source_target_pairs={{0,64},{1,72},{2,80},{3,88},{4,96},{5,104},{6,112},{7,120},{8,65},... | collective-permute-start | bytes 208904 | tf_op jit(solution)/shard_map/ppermute | solution.py:715
  136.7 0.5 slice.3
  137.8 1.4 collective-permute-done.2.near
  139.2 4.0 %collective-permute-done.3.far = s16[272,128]{1,0:T(8,128)(2,1)S(1)} collective-permute-done((s16[272,128]{1,0:T(8,128)(2,1)S(1)}, s16[272,128]{1,0:T(8,128)(2,1)S(1)}, u32[]{:S(2)}, u32[]{:S(2)}) %collective-permute-start.3) | collective-permute-done | bytes 69664 | tf_op jit(solution)/shard_map/ppermute | solution.py:715
  143.2 1.3 place.1
Async XLA Ops:
  0.6 1.2 copy-start
  2.4 6.9 %collective-permute-start = (bf16[528,128]{1,0:T(8,128)(2,1)S(1)}, bf16[528,128]{1,0:T(8,128)(2,1)S(1)}, u32[]{:S(2)}, u32[]{:S(2)}) collective-permute-start(bf16[528,128]{1,0:T(8,128)(2,1)S(1)} %get-tuple-element.12), channel_id=1, source_target_pairs={{0,64},{64,0},{1,65},{65,1},{2,66},{66,2},{3,67},{67,3},{4,68},{68... | collective-permute-start | bytes 405512 | tf_op jit(solution)/shard_map/ppermute | solution.py:702
  4.6 0.7 copy-start.2
  5.3 0.7 copy-start.3
  11.9 48.4 %all-to-all-start = ((bf16[64,208,128]{2,1,0:T(8,128)(2,1)}), bf16[64,208,128]{2,1,0:T(8,128)(2,1)S(1)}, u32[]{:S(2)}, u32[]{:S(2)}) async-start(bf16[64,208,128]{2,1,0:T(8,128)(2,1)} %pack.1), calls=%async_computation | async-start | bytes 6815744 | tf_op jit(solution)/shard_map/all_to_all | solution.py:696
  19.8 40.5 %copy-start.1 = (f32[3,256]{1,0:T(4,128)S(1)}, f32[3,256]{1,0:T(4,128)}, u32[]{:S(2)}) copy-start(f32[3,256]{1,0:T(4,128)} %weights.1) | copy-start | bytes 9220
  119.9 7.5 %collective-permute-start.1 = (s16[528,128]{1,0:T(8,128)(2,1)S(1)}, s16[528,128]{1,0:T(8,128)(2,1)S(1)}, u32[]{:S(2)}, u32[]{:S(2)}) collective-permute-start(s16[528,128]{1,0:T(8,128)(2,1)S(1)} %collect_other.1.sent), channel_id=1, source_target_pairs={{0,64},{64,0},{1,65},{65,1},{2,66},{66,2},{3,67},{67,3},{4,68},{68... | collective-permute-start | bytes 405512 | tf_op jit(solution)/shard_map/ppermute | solution.py:711
  127.6 11.6 %collective-permute-start.2 = (s16[272,128]{1,0:T(8,128)(2,1)S(1)}, s16[272,128]{1,0:T(8,128)(2,1)S(1)}, u32[]{:S(2)}, u32[]{:S(2)}) collective-permute-start(s16[272,128]{1,0:T(8,128)(2,1)S(1)} %get-tuple-element.17), channel_id=1, source_target_pairs={{0,0},{1,8},{2,16},{3,24},{4,32},{5,40},{6,48},{7,56},{8,1},{9,9},... | collective-permute-start | bytes 208904 | tf_op jit(solution)/shard_map/ppermute | solution.py:714
  133.9 9.3 %collective-permute-start.3 = (s16[272,128]{1,0:T(8,128)(2,1)S(1)}, s16[272,128]{1,0:T(8,128)(2,1)S(1)}, u32[]{:S(2)}, u32[]{:S(2)}) collective-permute-start(s16[272,128]{1,0:T(8,128)(2,1)S(1)} %get-tuple-element.18), channel_id=1, source_target_pairs={{0,64},{1,72},{2,80},{3,88},{4,96},{5,104},{6,112},{7,120},{8,65},... | collective-permute-start | bytes 208904 | tf_op jit(solution)/shard_map/ppermute | solution.py:715

commit v11 on v10

--- a/solution.py
+++ b/solution.py
@@ -155,7 +155,7 @@
     )(density)
 
 
-CHUNK = 8
+CHUNK = 16
 ALL_SLOTS = PEERS * SLOTS
 BOUNDS = 2 * ALL_SLOTS
 STRIDE = 16

time: 147 us -> 146 us (level)
  no operation moved by 1% of the time
where the time goes in v11:
time: 146 us; the launch traced here: 145 us
  blocking collectives  53.4 us (37%)
  waiting for transfers between devices  45.5 us (31%)
  starting transfers between devices  21.6 us (15%)
  Pallas kernels  19.2 us (13%)
  local copies, waits for them, and re-layouts  3.07 us (2%)
  between operations  2.51 us (2%)
    all_to_all x1, blocking collectives, exchange(): lax.all_to_all(parts, ALL, 0, 0, axis_index_groups=GROUPS, tiled=True)  53.4 us
    all_to_all x1, waiting for transfers between devices, exchange(): lax.all_to_all(parts, ALL, 0, 0, axis_index_groups=GROUPS, tiled=True)  36.3 us
    all_to_all x1, starting transfers between devices, exchange(): lax.all_to_all(parts, ALL, 0, 0, axis_index_groups=GROUPS, tiled=True)  7.9 us
    ppermute x1, starting transfers between devices, shards(): near = lax.ppermute(near, ALL, mirror_pairs(0))  6.17 us
    ppermute x2, starting transfers between devices, shards(): theirs = lax.ppermute(sent, 'h', swap)  4.47 us
    pallas_call x1, Pallas kernels, batches(): pl.pallas_call(batch_kernel, out_shape=jax.ShapeDtypeStruct((PEERS, ROWS,...  4.36 us
    pallas_call x1, Pallas kernels, turn(): pl.pallas_call(turn_kernel, out_shape=jax.ShapeDtypeStruct((SLOTS, 4, KF,...  4.14 us
    ppermute x2, waiting for transfers between devices, shards(): theirs = lax.ppermute(sent, 'h', swap)  4.1 us
  transfers between devices with their start and end apart: 5, of which 5 were waited for; matrix products, arithmetic and copies ran while one was open for 0% of the time, Pallas kernels for 6%

profile of v11, /device:TPU:18, one launch (start us, length us, event | category | flops | bytes accessed | tf_op | source)
XLA Modules:
  0.0 145.3 jit_solution(12244727826263672582)
XLA Ops:
  0.6 0.0 copy-start
  0.6 1.2 copy-done
  1.9 0.5 share.1
  2.4 2.2 %collective-permute-start = (bf16[528,128]{1,0:T(8,128)(2,1)S(1)}, bf16[528,128]{1,0:T(8,128)(2,1)S(1)}, u32[]{:S(2)}, u32[]{:S(2)}) collective-permute-start(bf16[528,128]{1,0:T(8,128)(2,1)S(1)} %get-tuple-element.12), channel_id=1, source_target_pairs={{0,64},{64,0},{1,65},{65,1},{2,66},{66,2},{3,67},{67,3},{4,68},{68... | collective-permute-start | bytes 405512 | tf_op jit(solution)/shard_map/ppermute | solution.py:702
  4.6 0.0 copy-start.2
  4.6 0.7 copy-done.2
  5.3 0.0 copy-start.3
  5.3 0.7 copy-done.3
  5.9 2.5 %route.1.table = s32[496]{0:T(512)S(1)} custom-call(s32[384]{0:T(512)S(1)} %copy-done.2, s32[128]{0:T(128)S(1)} %copy-done.3), custom_call_target="tpu_custom_call" | custom-call | flops 1000000 | bytes 4194304 | tf_op jit(solution)/shard_map/route/pallas_call | solution.py:194
  8.5 0.8 collective-permute-done.theirs
  9.3 2.7 %pack.1 = bf16[64,208,128]{2,1,0:T(8,128)(2,1)} custom-call(s32[496]{0:T(512)S(1)} %route.1.table, bf16[528,128]{1,0:T(8,128)(2,1)S(1)} %get-tuple-element.11.mine, bf16[528,128]{1,0:T(8,128)(2,1)S(1)} %collective-permute-done.theirs), custom_call_target="tpu_custom_call" | custom-call | tf_op jit(solution)/shard_map/pack/pallas_call | solution.py:264
  12.0 7.9 %all-to-all-start = ((bf16[64,208,128]{2,1,0:T(8,128)(2,1)}), bf16[64,208,128]{2,1,0:T(8,128)(2,1)S(1)}, u32[]{:S(2)}, u32[]{:S(2)}) async-start(bf16[64,208,128]{2,1,0:T(8,128)(2,1)} %pack.1), calls=%async_computation | async-start | bytes 6815744 | tf_op jit(solution)/shard_map/all_to_all | solution.py:696
  19.9 0.0 copy-start.1
  19.9 4.1 %turn.1.flipped = bf16[3,4,1024,256]{3,2,1,0:T(8,128)(2,1)} custom-call(s32[496]{0:T(512)S(1)} %route.1.table, bf16[3,4,256,1024]{3,2,1,0:T(8,128)(2,1)} %basis.1), custom_call_target="tpu_custom_call" | custom-call | flops 1000000 | bytes 25165824 | tf_op jit(solution)/shard_map/turn/pallas_call | solution.py:313
  24.1 36.3 %all-to-all-done.window = bf16[64,208,128]{2,1,0:T(8,128)(2,1)S(1)} async-done(((bf16[64,208,128]{2,1,0:T(8,128)(2,1)}), bf16[64,208,128]{2,1,0:T(8,128)(2,1)S(1)}, u32[]{:S(2)}, u32[]{:S(2)}) %all-to-all-start) | async-done | bytes 3407904 | tf_op jit(solution)/shard_map/all_to_all | solution.py:696
  60.4 0.0 copy-done.1
  60.4 4.4 %batches.1 = bf16[64,208,128]{2,1,0:T(8,128)(2,1)S(1)} custom-call(s32[496]{0:T(512)S(1)} %route.1.table, f32[3,256]{1,0:T(4,128)S(1)} %copy-done.1, bf16[3,4,1024,256]{3,2,1,0:T(8,128)(2,1)} %turn.1.flipped, bf16[64,208,128]{2,1,0:T(8,128)(2,1)S(1)} %all-to-all-done.window), custom_call_target="tpu_custom_call" | custom-call | tf_op jit(solution)/shard_map/batches/pallas_call | solution.py:462
  64.8 53.4 %all_to_all.10.arrived = bf16[64,208,128]{2,1,0:T(8,128)(2,1)S(1)} all-to-all(bf16[64,208,128]{2,1,0:T(8,128)(2,1)S(1)} %batches.1), channel_id=1, replica_groups={{47,14,49,25,4,51,17,37,3,26,56,35,52,29,33,10,36,42,20,32,43,41,48,62,..., dimensions={0} | all-to-all | bytes 6815744 | tf_op jit(solution)/shard_map/all_to_all | solution.py:696
  118.2 1.4 collect_other.1.sent
  119.6 2.3 %collective-permute-start.1 = (s16[528,128]{1,0:T(8,128)(2,1)S(1)}, s16[528,128]{1,0:T(8,128)(2,1)S(1)}, u32[]{:S(2)}, u32[]{:S(2)}) collective-permute-start(s16[528,128]{1,0:T(8,128)(2,1)S(1)} %collect_other.1.sent), channel_id=1, source_target_pairs={{0,64},{64,0},{1,65},{65,1},{2,66},{66,2},{3,67},{67,3},{4,68},{68... | collective-permute-start | bytes 405512 | tf_op jit(solution)/shard_map/ppermute | solution.py:711
  121.9 1.9 %collect_own.1 = (f32[520,128]{1,0:T(8,128)S(1)}, f32[4,8,128,128]{3,2,1,0:T(8,128)}) custom-call(s32[496]{0:T(512)S(1)} %route.1.table, bf16[64,208,128]{2,1,0:T(8,128)(2,1)S(1)} %all_to_all.10.arrived), custom_call_target="tpu_custom_call" | custom-call | flops 1000000 | bytes 4194304 | tf_op jit(solution)/shard_map/collect_own/pallas_call | solution.py:561
  123.8 3.3 %collective-permute-done.1.theirs = s16[528,128]{1,0:T(8,128)(2,1)S(1)} collective-permute-done((s16[528,128]{1,0:T(8,128)(2,1)S(1)}, s16[528,128]{1,0:T(8,128)(2,1)S(1)}, u32[]{:S(2)}, u32[]{:S(2)}) %collective-permute-start.1) | collective-permute-done | bytes 135200 | tf_op jit(solution)/shard_map/ppermute | solution.py:711
  127.1 0.2 merge.1
  127.4 6.2 %collective-permute-start.2 = (s16[272,128]{1,0:T(8,128)(2,1)S(1)}, s16[272,128]{1,0:T(8,128)(2,1)S(1)}, u32[]{:S(2)}, u32[]{:S(2)}) collective-permute-start(s16[272,128]{1,0:T(8,128)(2,1)S(1)} %get-tuple-element.17), channel_id=1, source_target_pairs={{0,0},{1,8},{2,16},{3,24},{4,32},{5,40},{6,48},{7,56},{8,1},{9,9},... | collective-permute-start | bytes 208904 | tf_op jit(solution)/shard_map/ppermute | solution.py:714
  133.5 3.1 %collective-permute-start.3 = (s16[272,128]{1,0:T(8,128)(2,1)S(1)}, s16[272,128]{1,0:T(8,128)(2,1)S(1)}, u32[]{:S(2)}, u32[]{:S(2)}) collective-permute-start(s16[272,128]{1,0:T(8,128)(2,1)S(1)} %get-tuple-element.18), channel_id=1, source_target_pairs={{0,64},{1,72},{2,80},{3,88},{4,96},{5,104},{6,112},{7,120},{8,65},... | collective-permute-start | bytes 208904 | tf_op jit(solution)/shard_map/ppermute | solution.py:715
  136.6 0.5 slice.3
  137.8 1.1 collective-permute-done.2.near
  138.9 3.9 %collective-permute-done.3.far = s16[272,128]{1,0:T(8,128)(2,1)S(1)} collective-permute-done((s16[272,128]{1,0:T(8,128)(2,1)S(1)}, s16[272,128]{1,0:T(8,128)(2,1)S(1)}, u32[]{:S(2)}, u32[]{:S(2)}) %collective-permute-start.3) | collective-permute-done | bytes 69664 | tf_op jit(solution)/shard_map/ppermute | solution.py:715
  142.8 1.3 place.1
Async XLA Ops:
  0.6 1.2 copy-start
  2.4 6.9 %collective-permute-start = (bf16[528,128]{1,0:T(8,128)(2,1)S(1)}, bf16[528,128]{1,0:T(8,128)(2,1)S(1)}, u32[]{:S(2)}, u32[]{:S(2)}) collective-permute-start(bf16[528,128]{1,0:T(8,128)(2,1)S(1)} %get-tuple-element.12), channel_id=1, source_target_pairs={{0,64},{64,0},{1,65},{65,1},{2,66},{66,2},{3,67},{67,3},{4,68},{68... | collective-permute-start | bytes 405512 | tf_op jit(solution)/shard_map/ppermute | solution.py:702
  4.6 0.7 copy-start.2
  5.3 0.7 copy-start.3
  12.0 48.4 %all-to-all-start = ((bf16[64,208,128]{2,1,0:T(8,128)(2,1)}), bf16[64,208,128]{2,1,0:T(8,128)(2,1)S(1)}, u32[]{:S(2)}, u32[]{:S(2)}) async-start(bf16[64,208,128]{2,1,0:T(8,128)(2,1)} %pack.1), calls=%async_computation | async-start | bytes 6815744 | tf_op jit(solution)/shard_map/all_to_all | solution.py:696
  19.9 40.5 %copy-start.1 = (f32[3,256]{1,0:T(4,128)S(1)}, f32[3,256]{1,0:T(4,128)}, u32[]{:S(2)}) copy-start(f32[3,256]{1,0:T(4,128)} %weights.1) | copy-start | bytes 9220
  119.6 7.5 %collective-permute-start.1 = (s16[528,128]{1,0:T(8,128)(2,1)S(1)}, s16[528,128]{1,0:T(8,128)(2,1)S(1)}, u32[]{:S(2)}, u32[]{:S(2)}) collective-permute-start(s16[528,128]{1,0:T(8,128)(2,1)S(1)} %collect_other.1.sent), channel_id=1, source_target_pairs={{0,64},{64,0},{1,65},{65,1},{2,66},{66,2},{3,67},{67,3},{4,68},{68... | collective-permute-start | bytes 405512 | tf_op jit(solution)/shard_map/ppermute | solution.py:711
  127.4 11.6 %collective-permute-start.2 = (s16[272,128]{1,0:T(8,128)(2,1)S(1)}, s16[272,128]{1,0:T(8,128)(2,1)S(1)}, u32[]{:S(2)}, u32[]{:S(2)}) collective-permute-start(s16[272,128]{1,0:T(8,128)(2,1)S(1)} %get-tuple-element.17), channel_id=1, source_target_pairs={{0,0},{1,8},{2,16},{3,24},{4,32},{5,40},{6,48},{7,56},{8,1},{9,9},... | collective-permute-start | bytes 208904 | tf_op jit(solution)/shard_map/ppermute | solution.py:714
  133.5 9.3 %collective-permute-start.3 = (s16[272,128]{1,0:T(8,128)(2,1)S(1)}, s16[272,128]{1,0:T(8,128)(2,1)S(1)}, u32[]{:S(2)}, u32[]{:S(2)}) collective-permute-start(s16[272,128]{1,0:T(8,128)(2,1)S(1)} %get-tuple-element.18), channel_id=1, source_target_pairs={{0,64},{1,72},{2,80},{3,88},{4,96},{5,104},{6,112},{7,120},{8,65},... | collective-permute-start | bytes 208904 | tf_op jit(solution)/shard_map/ppermute | solution.py:715
